TPU v7x, 32 devices: a whole 2x2x4 slice. The times are simulated.
32 devices in a mesh: section: 2 (over x), dp: 16 (over z, y, core).
Axes of the slice: x: 2, y: 2, z: 4, core: 2. Of those that a mesh axis runs over, the one named last changes fastest.
Arguments:
- atom_features: bfloat16 [2, 16, 2048, 128], P(None, 'dp'), may hold values from -6 to 6
- atom_single: bfloat16 [2048, 128], replicated, may hold values from -6 to 6
- atom_pairs: bfloat16 [64, 16, 32, 128], P('dp'), may hold values from -6 to 6
- atom_token: int32 [2048], replicated, may hold values from 0 to 511, never falling along the last dimension, each value on 1 to 12 neighbouring positions
- window_start: int32 [64], replicated, may hold values from 0 to 1920, as said below
- pair_repr: bfloat16 [512, 512, 128], P('dp'), may hold values from -6 to 6
- single_repr: bfloat16 [512, 384], replicated, may hold values from -6 to 6
- noise_table: float32 [200, 384], replicated, may hold values from -6 to 6
- noise_index: int32 [2, 16], P(None, 'dp'), may hold values from 0 to 199
- cotangent: bfloat16 [2, 16, 512, 768], P(None, 'dp'), may hold values from -6 to 6
- atomcond_gain: bfloat16 [128], replicated, may hold values from 0.5 to 1.5
- atomcond_weight: bfloat16 [128, 768], replicated, may hold values from -0.5 to 0.5
- atomcond_bias: bfloat16 [768], replicated, may hold values from -3 to 3
- atomproj_weight: bfloat16 [128, 512], replicated, may hold values from -0.5 to 0.5
- atomquery_bias: bfloat16 [128], replicated, may hold values from -4 to 4
- atomout_weight: bfloat16 [128, 128], replicated, may hold values from -2 to 2
- atomgu_weight: bfloat16 [128, 512], replicated, may hold values from -0.5 to 0.5
- atomdown_weight: bfloat16 [256, 128], replicated, may hold values from -0.375 to 0.375
- atompair_gain: bfloat16 [16], replicated, may hold values from 0.099609375 to 1.8984375
- atompair_weight: bfloat16 [16, 4], replicated, may hold values from -1.5 to 1.5
- gather_weight: bfloat16 [128, 768], replicated, may hold values from -0.5 to 0.5
- tokcond_gain: bfloat16 [384], replicated, may hold values from 0.5 to 1.5
- tokcond_weight: bfloat16 [384, 4608], replicated, may hold values from -0.3125 to 0.3125
- tokcond_bias: bfloat16 [4608], replicated, may hold values from -3 to 3
- tokproj_weight: bfloat16 [768, 3072], replicated, may hold values from -0.21875 to 0.21875
- tokquery_bias: bfloat16 [768], replicated, may hold values from -4 to 4
- tokout_weight: bfloat16 [768, 768], replicated, may hold values from -0.875 to 0.875
- tokgu_weight: bfloat16 [768, 3072], replicated, may hold values from -0.21875 to 0.21875
- tokdown_weight: bfloat16 [1536, 768], replicated, may hold values from -0.15625 to 0.15625
- tokpair_gain: bfloat16 [128], replicated, may hold values from 0.099609375 to 1.8984375
- tokpair_weight: bfloat16 [128, 16], replicated, may hold values from -0.5 to 0.5
Outputs:
- output: bfloat16 [2, 16, 512, 768], P(None, 'dp', 'section')
- features_grad: float32 [2, 16, 2048, 128], P(None, 'dp', 'section')
- atomcondgain_grad: float32 [128], P('section')
- atomcondweight_grad: float32 [128, 768], P('section')
- atomcondbias_grad: float32 [768], P('section')
- atomproj_grad: float32 [128, 512], P('section')
- atomquery_grad: float32 [128], P('section')
- atomout_grad: float32 [128, 128], P('section')
- atomgu_grad: float32 [128, 512], P('section')
- atomdown_grad: float32 [256, 128], P('section')
- atompairgain_grad: float32 [16], P('section')
- atompairweight_grad: float32 [16, 4], P('section')
- gather_grad: float32 [128, 768], P('section')
- tokcondgain_grad: float32 [384], P('section')
- tokcondweight_grad: float32 [384, 4608], P('section')
- tokcondbias_grad: float32 [4608], P('section')
- tokproj_grad: float32 [768, 3072], P('section')
- tokquery_grad: float32 [768], P('section')
- tokout_grad: float32 [768, 768], P('section')
- tokgu_grad: float32 [768, 3072], P('section')
- tokdown_grad: float32 [1536, 768], P('section')
- tokpairgain_grad: float32 [128], P('section')
- tokpairweight_grad: float32 [128, 16], P('section')
Inputs may be any that keep to these rules, and one draw needn't show every extreme that they name: `atom_token`: non-decreasing; each of the 512 tokens has 1 to 12 atoms. `window_start`: window w holds its 32 query atoms w * 32 to w * 32 + 31 among its 128 keys. `noise_index`: rows of noise_table.
All inputs are finite; a program needn't handle non-finite values.
Results may differ from a plain program's by a relative error of at most 0.03.
Values may be sent and summed in bfloat16 or wider, within the bound.
No kernel may reach another device: no remote copies, remote signals or barrier semaphores. Data moves between devices by JAX's collectives and lax.ppermute only.
A program may use at most 576 MiB of HBM per device.

v0:
```python
from functools import partial

import jax
import jax.numpy as jnp
from jax import lax
from jax.sharding import PartitionSpec as P

EPS = 1e-05
HIGH = lax.Precision.HIGHEST
LOWTYPE = jnp.bfloat16
WIDE = jnp.float32


def from_behind(block, axis, distance):
    devices = range(lax.axis_size(axis))
    route = [(i - distance, i) for i in devices if i - distance in devices]
    return lax.ppermute(block, axis, route)


def layer_norm(values, axis=-1):
    centre = values - jnp.mean(values, axis=axis, keepdims=True)
    spread = jnp.mean(centre * centre, axis=axis, keepdims=True)
    return centre * lax.rsqrt(spread + EPS)


def cond_norm(condition, cond_gain):
    return layer_norm(condition) * cond_gain


def modulate(features, scale_in, shift_in):
    return layer_norm(features) * jax.nn.sigmoid(scale_in) + shift_in


def rounded(values):
    return lax.optimization_barrier(values.astype(LOWTYPE)).astype(WIDE)


def product(left, right):
    return jnp.dot(left, right, preferred_element_type=WIDE)


def product_left(left, right):
    return lax.dot_general(left, right, (((0,), (0,)), ((), ())), preferred_element_type=WIDE)


def product_right(left, right):
    return lax.dot_general(left, right, (((1,), (1,)), ((), ())), preferred_element_type=WIDE)


def silu_slope(values):
    logistic = jax.nn.sigmoid(values)
    return logistic * (1.0 + values * (1.0 - logistic))


def sigmoid_slope(values):
    logistic = jax.nn.sigmoid(values)
    return logistic * (1.0 - logistic)


def token_slab(pair_rows, pair_gain, pair_weight):
    normed = layer_norm(pair_rows) * pair_gain
    return jnp.einsum("ijc,ch->hij", normed, pair_weight, precision=HIGH)


def atom_slab(pair_rows, pair_gain, pair_weight):
    normed = layer_norm(pair_rows, 1) * pair_gain[None, :, None, None]
    return jnp.einsum("wcqk,ch->whqk", normed, pair_weight, precision=HIGH)


def softmax_rows(scores):
    maximum = jnp.max(scores, axis=-1, keepdims=True)
    exponent = jnp.exp(scores - maximum)
    return exponent / jnp.sum(exponent, axis=-1, keepdims=True)


def window_scores(query_win, key_win, bias_rows, factor):
    raw_scores = jnp.einsum("wqhe,wkhe->whqk", query_win, key_win, preferred_element_type=WIDE)
    return raw_scores * factor + bias_rows.astype(WIDE)


def attend_forward(query_win, key_win, value_win, bias_rows, factor):
    probability = softmax_rows(window_scores(query_win, key_win, bias_rows, factor)).astype(LOWTYPE)
    return jnp.einsum("whqk,wkhe->wqhe", probability, value_win, preferred_element_type=WIDE)


def attend_backward(query_win, key_win, value_win, bias_rows, factor, d_attended):
    probability = softmax_rows(window_scores(query_win, key_win, bias_rows, factor))
    d_probability = jnp.einsum(
        "wqhe,wkhe->whqk", d_attended, value_win, preferred_element_type=WIDE
    )
    d_scores = (
        probability * (d_probability - jnp.sum(probability * d_probability, axis=-1, keepdims=True))
    ).astype(LOWTYPE)
    d_queries = (
        jnp.einsum("whqk,wkhe->wqhe", d_scores, key_win, preferred_element_type=WIDE) * factor
    )
    d_keys = (
        jnp.einsum("whqk,wqhe->wkhe", d_scores, query_win, preferred_element_type=WIDE) * factor
    )
    d_values = jnp.einsum(
        "whqk,wqhe->wkhe", probability.astype(LOWTYPE), d_attended, preferred_element_type=WIDE
    )
    return (d_queries, d_keys, d_values, d_scores)


def atom_windows(queries, key_rows, value_rows, atom_bias, positions):
    windows, head_count, span_query, span_key = atom_bias.shape
    col_count = queries.shape[1]
    head_size = col_count // head_count
    query_win = queries.reshape(windows, span_query, head_count, head_size)
    key_win = key_rows[positions].reshape(windows, span_key, head_count, head_size)
    value_win = value_rows[positions].reshape(windows, span_key, head_count, head_size)
    return (query_win, key_win, value_win, head_size)


def atom_forward_attend(queries, key_rows, value_rows, atom_bias, positions):
    query_win, key_win, value_win, head_size = atom_windows(
        queries, key_rows, value_rows, atom_bias, positions
    )
    attended = attend_forward(query_win, key_win, value_win, atom_bias, head_size ** (-0.5))
    return attended.reshape(queries.shape)


def atom_backward_attend(queries, key_rows, value_rows, d_attended, atom_bias, positions):
    query_win, key_win, value_win, head_size = atom_windows(
        queries, key_rows, value_rows, atom_bias, positions
    )
    atom_count, col_count = queries.shape
    d_window = d_attended.reshape(query_win.shape)
    d_query_win, d_key_win, d_value_win, d_scores = attend_backward(
        query_win, key_win, value_win, atom_bias, head_size ** (-0.5), d_window
    )
    flat_positions = positions.reshape(-1)
    d_keys = (
        jnp.zeros((atom_count, col_count), WIDE)
        .at[flat_positions]
        .add(d_key_win.reshape(-1, col_count))
    )
    d_values = (
        jnp.zeros((atom_count, col_count), WIDE)
        .at[flat_positions]
        .add(d_value_win.reshape(-1, col_count))
    )
    return (d_query_win.reshape(atom_count, col_count), d_keys, d_values, d_scores)


def token_shapes(queries, key_rows, value_rows, token_bias):
    head_count = token_bias.shape[0]
    row_count, col_count = queries.shape
    head_size = col_count // head_count
    shaped = [
        member.reshape(1, row_count, head_count, head_size)
        for member in (queries, key_rows, value_rows)
    ]
    return (shaped, head_size)


def token_forward_attend(queries, key_rows, value_rows, token_bias):
    shaped, head_size = token_shapes(queries, key_rows, value_rows, token_bias)
    attended = attend_forward(
        shaped[0], shaped[1], shaped[2], token_bias[None], head_size ** (-0.5)
    )
    return attended.reshape(queries.shape)


def token_backward_attend(queries, key_rows, value_rows, d_attended, token_bias):
    shaped, head_size = token_shapes(queries, key_rows, value_rows, token_bias)
    d_window = d_attended.reshape(shaped[0].shape)
    d_query_win, d_key_win, d_value_win, d_scores = attend_backward(
        shaped[0], shaped[1], shaped[2], token_bias[None], head_size ** (-0.5), d_window
    )
    return (
        d_query_win.reshape(queries.shape),
        d_key_win.reshape(queries.shape),
        d_value_win.reshape(queries.shape),
        d_scores[0],
    )


def block_forward(features, condition, weights, attend):
    (
        cond_gain,
        cond_weight,
        cond_bias,
        proj_weight,
        query_bias,
        out_weight,
        gu_weight,
        down_weight,
    ) = weights
    col_count = features.shape[1]
    normed_low = cond_norm(condition, cond_gain.astype(WIDE)).astype(LOWTYPE)
    projected = product(normed_low, cond_weight) + cond_bias.astype(WIDE)
    pieces = jnp.split(projected, 6, axis=1)
    normed_one_low = modulate(features, pieces[0], pieces[1]).astype(LOWTYPE)
    raw_proj = product(normed_one_low, proj_weight)
    projections = jnp.concatenate(
        [raw_proj[:, :col_count] + query_bias.astype(WIDE), raw_proj[:, col_count:]], axis=1
    ).astype(LOWTYPE)
    queries, key_rows, value_rows, gate_low = jnp.split(projections, 4, axis=1)
    gate_cols = gate_low.astype(WIDE)
    attended = attend(queries, key_rows, value_rows)
    gated_low = (attended * jax.nn.sigmoid(gate_cols)).astype(LOWTYPE)
    attn_out = product(gated_low, out_weight)
    middle = features + jax.nn.sigmoid(pieces[2]) * attn_out
    normed_two_low = modulate(middle, pieces[3], pieces[4]).astype(LOWTYPE)
    gate_up = product(normed_two_low, gu_weight)
    gate_half, up_half = jnp.split(gate_up, 2, axis=1)
    hidden_low = (jax.nn.silu(gate_half) * up_half).astype(LOWTYPE)
    down_out = product(hidden_low, down_weight)
    result = middle + jax.nn.sigmoid(pieces[5]) * down_out
    stored = (
        normed_low,
        pieces,
        normed_one_low,
        queries,
        key_rows,
        value_rows,
        gate_cols,
        attended,
        gated_low,
        attn_out,
        middle,
        normed_two_low,
        gate_up,
        hidden_low,
        down_out,
    )
    return (result, stored)


def block_backward(features, condition, weights, stored, attend_back, d_result):
    (
        cond_gain,
        cond_weight,
        cond_bias,
        proj_weight,
        query_bias,
        out_weight,
        gu_weight,
        down_weight,
    ) = weights
    (
        normed_low,
        pieces,
        normed_one_low,
        queries,
        key_rows,
        value_rows,
        gate_cols,
        attended,
        gated_low,
        attn_out,
        middle,
        normed_two_low,
        gate_up,
        hidden_low,
        down_out,
    ) = stored
    col_count = features.shape[1]
    d_down = (d_result * jax.nn.sigmoid(pieces[5])).astype(LOWTYPE)
    d_last = d_result * down_out * sigmoid_slope(pieces[5])
    grad_down = product_left(hidden_low, d_down)
    d_hidden = rounded(product_right(d_down, down_weight))
    gate_half, up_half = jnp.split(gate_up, 2, axis=1)
    d_gate_up = jnp.concatenate(
        [d_hidden * up_half * silu_slope(gate_half), d_hidden * jax.nn.silu(gate_half)], axis=1
    ).astype(LOWTYPE)
    grad_updown = product_left(normed_two_low, d_gate_up)
    d_normed_two = product_right(d_gate_up, gu_weight)
    _, modulate_back = jax.vjp(modulate, middle, pieces[3], pieces[4])
    d_middle_part, d_scale_two, d_shift_two = modulate_back(d_normed_two)
    d_middle = d_result + d_middle_part
    d_attn_out = (d_middle * jax.nn.sigmoid(pieces[2])).astype(LOWTYPE)
    d_first = d_middle * attn_out * sigmoid_slope(pieces[2])
    grad_output = product_left(gated_low, d_attn_out)
    d_gated = rounded(product_right(d_attn_out, out_weight))
    d_attended = (d_gated * jax.nn.sigmoid(gate_cols)).astype(LOWTYPE)
    d_gate_cols = d_gated * attended * sigmoid_slope(gate_cols)
    d_queries, d_keys, d_values, d_scores = attend_back(queries, key_rows, value_rows, d_attended)
    d_projections = jnp.concatenate([d_queries, d_keys, d_values, d_gate_cols], axis=1).astype(
        LOWTYPE
    )
    grad_inproj = product_left(normed_one_low, d_projections)
    grad_query = jnp.sum(d_projections[:, :col_count].astype(WIDE), axis=0)
    d_normed_one = product_right(d_projections, proj_weight)
    _, modulate_back = jax.vjp(modulate, features, pieces[0], pieces[1])
    d_features_part, d_scale_one, d_shift_one = modulate_back(d_normed_one)
    d_features = d_middle + d_features_part
    d_projected = jnp.concatenate(
        [d_scale_one, d_shift_one, d_first, d_scale_two, d_shift_two, d_last], axis=1
    ).astype(LOWTYPE)
    grad_condition = product_left(normed_low, d_projected)
    grad_offset = jnp.sum(d_projected.astype(WIDE), axis=0)
    d_normed = product_right(d_projected, cond_weight)
    _, norm_back = jax.vjp(cond_norm, condition, cond_gain.astype(WIDE))
    _, grad_gain = norm_back(d_normed)
    gradients = (
        grad_gain,
        grad_condition,
        grad_offset,
        grad_inproj,
        grad_query,
        grad_output,
        grad_updown,
        grad_down,
    )
    return (d_features, gradients, d_scores.astype(WIDE))


def local(
    atom_features,
    atom_single,
    atom_pairs,
    atom_token,
    window_start,
    pair_repr,
    single_repr,
    noise_table,
    noise_index,
    cotangent,
    atomcond_gain,
    atomcond_weight,
    atomcond_bias,
    atomproj_weight,
    atomquery_bias,
    atomout_weight,
    atomgu_weight,
    atomdown_weight,
    atompair_gain,
    atompair_weight,
    gather_weight,
    tokcond_gain,
    tokcond_weight,
    tokcond_bias,
    tokproj_weight,
    tokquery_bias,
    tokout_weight,
    tokgu_weight,
    tokdown_weight,
    tokpair_gain,
    tokpair_weight,
):
    atom_block = (
        atomcond_gain,
        atomcond_weight,
        atomcond_bias,
        atomproj_weight,
        atomquery_bias,
        atomout_weight,
        atomgu_weight,
        atomdown_weight,
    )
    token_block = (
        tokcond_gain,
        tokcond_weight,
        tokcond_bias,
        tokproj_weight,
        tokquery_bias,
        tokout_weight,
        tokgu_weight,
        tokdown_weight,
    )
    micro_count = atom_features.shape[0]
    atom_count = atom_features.shape[2]
    atom_width = atom_features.shape[3]
    length = cotangent.shape[2]
    model_width = cotangent.shape[3]
    section_index = lax.axis_index("section")
    is_first = section_index == 0
    repr_wide = pair_repr.astype(WIDE)
    pairs_wide = atom_pairs.astype(WIDE)
    token_part = token_slab(
        repr_wide, tokpair_gain.astype(WIDE), tokpair_weight.astype(WIDE)
    ).astype(LOWTYPE)
    atom_part = atom_slab(
        pairs_wide, atompair_gain.astype(WIDE), atompair_weight.astype(WIDE)
    ).astype(LOWTYPE)
    token_bias, atom_bias = (
        lax.all_gather(token_part, "dp", axis=1, tiled=True),
        lax.all_gather(atom_part, "dp", axis=0, tiled=True),
    )
    positions = window_start[:, None] + jnp.arange(atom_bias.shape[3], dtype=jnp.int32)[None, :]
    onehot_wide = (atom_token[None, :] == jnp.arange(length, dtype=jnp.int32)[:, None]).astype(WIDE)
    counts = jnp.sum(onehot_wide, axis=1, keepdims=True)
    onehot_low = onehot_wide.astype(LOWTYPE)
    atom_cond = atom_single.astype(WIDE)
    single_wide = single_repr.astype(WIDE)
    atom_fwd = partial(atom_forward_attend, atom_bias=atom_bias, positions=positions)
    atom_bwd = partial(atom_backward_attend, atom_bias=atom_bias, positions=positions)
    token_fwd = partial(token_forward_attend, token_bias=token_bias)
    token_bwd = partial(token_backward_attend, token_bias=token_bias)
    empty_send = jnp.zeros((length, model_width), LOWTYPE)
    zero_tokens = jnp.zeros((length, model_width), WIDE)
    zero_atoms = jnp.zeros((atom_count, atom_width), WIDE)
    atom_zero = tuple((jnp.zeros(member.shape, WIDE) for member in atom_block + (gather_weight,)))
    token_zero = tuple((jnp.zeros(member.shape, WIDE) for member in token_block))
    zero_token_bias = jnp.zeros(token_bias.shape, WIDE)
    zero_atom_bias = jnp.zeros(atom_bias.shape, WIDE)

    def token_condition(sample):
        return single_wide + noise_table[noise_index[sample, 0]]

    def pooled_tokens(features_low):
        result, stored = block_forward(features_low.astype(WIDE), atom_cond, atom_block, atom_fwd)
        result_low = result.astype(LOWTYPE)
        pre_act = product(result_low, gather_weight)
        pooled = product(onehot_low, jax.nn.silu(pre_act).astype(LOWTYPE)) / counts
        return (result_low, pre_act, pooled, stored)

    def atom_back(features_low, d_pooled):
        features = features_low.astype(WIDE)
        result_low, pre_act, pooled, stored = pooled_tokens(features_low)
        d_rows = (d_pooled.astype(WIDE) / counts)[atom_token]
        d_pre = (d_rows * silu_slope(pre_act)).astype(LOWTYPE)
        grad_gather = product_left(result_low, d_pre)
        d_result = product_right(d_pre, gather_weight)
        d_features, gradients, d_bias = block_backward(
            features, atom_cond, atom_block, stored, atom_bwd, d_result
        )
        return (d_features, gradients + (grad_gather,), d_bias)

    def token_back(inbound, sample, d_output):
        condition = token_condition(sample)
        features = inbound.astype(WIDE)
        result, stored = block_forward(features, condition, token_block, token_fwd)
        return block_backward(
            features, condition, token_block, stored, token_bwd, d_output.astype(WIDE)
        )

    bias_state = (
        jnp.zeros(token_part.shape, WIDE),
        jnp.zeros(atom_part.shape, WIDE),
        zero_token_bias,
        zero_atom_bias,
    )
    atom_sums = atom_zero
    token_sums = token_zero
    received = empty_send
    kept_inputs = []
    token_outputs = []
    for tick_index in range(micro_count + 1):

        def section_one(tick_index=tick_index):
            if tick_index < micro_count:
                pooled = pooled_tokens(atom_features[tick_index, 0])[2]
                return (pooled.astype(LOWTYPE), zero_tokens)
            return (empty_send, zero_tokens)

        def section_two(inbound=received, tick_index=tick_index):
            if tick_index >= 1:
                result, stored = block_forward(
                    inbound.astype(WIDE), token_condition(tick_index - 1), token_block, token_fwd
                )
                return (empty_send, result)
            return (empty_send, zero_tokens)

        sending, produced = lax.cond(is_first, section_one, section_two)
        if tick_index >= 1:
            kept_inputs.append(received)
            token_outputs.append(produced)
        if tick_index < micro_count:
            received = from_behind(sending, "section", 1)
    back_in = empty_send
    atom_grad_rows = [zero_atoms] * micro_count
    for tick_index in range(micro_count + 1):
        token_sample = micro_count - 1 - tick_index
        atom_sample = micro_count - tick_index

        def section_one(inbound=back_in, atom_sample=atom_sample):
            if atom_sample < micro_count:
                d_features, gradients, d_bias = atom_back(atom_features[atom_sample, 0], inbound)
                return (empty_send, d_features, gradients, token_zero, zero_token_bias, d_bias)
            return (empty_send, zero_atoms, atom_zero, token_zero, zero_token_bias, zero_atom_bias)

        def section_two(token_sample=token_sample):
            if token_sample >= 0:
                d_inbound, gradients, d_bias = token_back(
                    kept_inputs[token_sample], token_sample, cotangent[token_sample, 0]
                )
                return (
                    d_inbound.astype(LOWTYPE),
                    zero_atoms,
                    atom_zero,
                    gradients,
                    d_bias,
                    zero_atom_bias,
                )
            return (empty_send, zero_atoms, atom_zero, token_zero, zero_token_bias, zero_atom_bias)

        sending, d_features, grads_atom, grads_token, d_token_bias, d_atom_bias = lax.cond(
            is_first, section_one, section_two
        )
        if atom_sample < micro_count:
            atom_grad_rows[atom_sample] = d_features
        atom_sums = tuple((left + right for left, right in zip(atom_sums, grads_atom)))
        token_sums = tuple((left + right for left, right in zip(token_sums, grads_token)))
        add_slab_token, add_slab_atom, add_total_token_bias, add_total_atom_bias = bias_state
        bias_state = (
            add_slab_token,
            add_slab_atom,
            add_total_token_bias + d_token_bias,
            add_total_atom_bias + d_atom_bias,
        )
        if token_sample >= 0:
            back_in = from_behind(sending, "section", -1)
    slab_token, slab_atom, total_token_bias, total_atom_bias = bias_state
    slab_token, slab_atom = (
        lax.psum_scatter(total_token_bias, "dp", scatter_dimension=1, tiled=True),
        lax.psum_scatter(total_atom_bias, "dp", scatter_dimension=0, tiled=True),
    )
    _, token_slab_back = jax.vjp(
        partial(token_slab, repr_wide), tokpair_gain.astype(WIDE), tokpair_weight.astype(WIDE)
    )
    grad_tok_gain, grad_tok_weight = token_slab_back(slab_token)
    _, atom_slab_back = jax.vjp(
        partial(atom_slab, pairs_wide), atompair_gain.astype(WIDE), atompair_weight.astype(WIDE)
    )
    grad_atom_gain, grad_atom_weight = atom_slab_back(slab_atom)
    grads_all = (
        atom_sums[0:8]
        + (grad_atom_gain, grad_atom_weight, atom_sums[8])
        + token_sums
        + (grad_tok_gain, grad_tok_weight)
    )
    output_full = jnp.stack(token_outputs)[:, None]
    atom_full = jnp.stack(atom_grad_rows)[:, None]
    totals = lax.psum(
        (
            grads_all[0],
            grads_all[1],
            grads_all[2],
            grads_all[3],
            grads_all[4],
            grads_all[5],
            grads_all[6],
            grads_all[7],
            grads_all[8],
            grads_all[9],
            grads_all[10],
            grads_all[11],
            grads_all[12],
            grads_all[13],
            grads_all[14],
            grads_all[15],
            grads_all[16],
            grads_all[17],
            grads_all[18],
            grads_all[19],
            grads_all[20],
        ),
        "dp",
    )
    finished = tuple(
        (
            lax.psum_scatter(
                output_full.astype(jnp.bfloat16), "section", scatter_dimension=2, tiled=True
            ).astype(jnp.float32),
            lax.psum_scatter(
                atom_full.astype(jnp.bfloat16), "section", scatter_dimension=2, tiled=True
            ).astype(jnp.float32),
            lax.psum_scatter(
                totals[0].astype(jnp.bfloat16), "section", scatter_dimension=0, tiled=True
            ).astype(jnp.float32),
            lax.psum_scatter(
                totals[1].astype(jnp.bfloat16), "section", scatter_dimension=0, tiled=True
            ).astype(jnp.float32),
            lax.psum_scatter(
                totals[2].astype(jnp.bfloat16), "section", scatter_dimension=0, tiled=True
            ).astype(jnp.float32),
            lax.psum_scatter(
                totals[3].astype(jnp.bfloat16), "section", scatter_dimension=0, tiled=True
            ).astype(jnp.float32),
            lax.psum_scatter(
                totals[4].astype(jnp.bfloat16), "section", scatter_dimension=0, tiled=True
            ).astype(jnp.float32),
            lax.psum_scatter(
                totals[5].astype(jnp.bfloat16), "section", scatter_dimension=0, tiled=True
            ).astype(jnp.float32),
            lax.psum_scatter(
                totals[6].astype(jnp.bfloat16), "section", scatter_dimension=0, tiled=True
            ).astype(jnp.float32),
            lax.psum_scatter(
                totals[7].astype(jnp.bfloat16), "section", scatter_dimension=0, tiled=True
            ).astype(jnp.float32),
            lax.psum_scatter(
                totals[8].astype(jnp.bfloat16), "section", scatter_dimension=0, tiled=True
            ).astype(jnp.float32),
            lax.psum_scatter(
                totals[9].astype(jnp.bfloat16), "section", scatter_dimension=0, tiled=True
            ).astype(jnp.float32),
            lax.psum_scatter(
                totals[10].astype(jnp.bfloat16), "section", scatter_dimension=0, tiled=True
            ).astype(jnp.float32),
            lax.psum_scatter(
                totals[11].astype(jnp.bfloat16), "section", scatter_dimension=0, tiled=True
            ).astype(jnp.float32),
            lax.psum_scatter(
                totals[12].astype(jnp.bfloat16), "section", scatter_dimension=0, tiled=True
            ).astype(jnp.float32),
            lax.psum_scatter(
                totals[13].astype(jnp.bfloat16), "section", scatter_dimension=0, tiled=True
            ).astype(jnp.float32),
            lax.psum_scatter(
                totals[14].astype(jnp.bfloat16), "section", scatter_dimension=0, tiled=True
            ).astype(jnp.float32),
            lax.psum_scatter(
                totals[15].astype(jnp.bfloat16), "section", scatter_dimension=0, tiled=True
            ).astype(jnp.float32),
            lax.psum_scatter(
                totals[16].astype(jnp.bfloat16), "section", scatter_dimension=0, tiled=True
            ).astype(jnp.float32),
            lax.psum_scatter(
                totals[17].astype(jnp.bfloat16), "section", scatter_dimension=0, tiled=True
            ).astype(jnp.float32),
            lax.psum_scatter(
                totals[18].astype(jnp.bfloat16), "section", scatter_dimension=0, tiled=True
            ).astype(jnp.float32),
            lax.psum_scatter(
                totals[19].astype(jnp.bfloat16), "section", scatter_dimension=0, tiled=True
            ).astype(jnp.float32),
            lax.psum_scatter(
                totals[20].astype(jnp.bfloat16), "section", scatter_dimension=0, tiled=True
            ).astype(jnp.float32),
        )
    )
    return (finished[0].astype(LOWTYPE),) + tuple(finished[1:])


def solution(mesh):
    return jax.shard_map(
        local,
        mesh=mesh,
        in_specs=(
            P(None, "dp", None, None),
            P(),
            P("dp", None, None, None),
            P(),
            P(),
            P("dp", None, None),
            P(),
            P(),
            P(None, "dp"),
            P(None, "dp", None, None),
            P(),
            P(),
            P(),
            P(),
            P(),
            P(),
            P(),
            P(),
            P(),
            P(),
            P(),
            P(),
            P(),
            P(),
            P(),
            P(),
            P(),
            P(),
            P(),
            P(),
            P(),
        ),
        out_specs=(
            P(None, "dp", "section", None),
            P(None, "dp", "section", None),
            P("section"),
            P("section", None),
            P("section"),
            P("section", None),
            P("section"),
            P("section", None),
            P("section", None),
            P("section", None),
            P("section"),
            P("section", None),
            P("section", None),
            P("section"),
            P("section", None),
            P("section"),
            P("section", None),
            P("section"),
            P("section", None),
            P("section", None),
            P("section", None),
            P("section"),
            P("section", None),
        ),
        check_vma=False,
    )
```

profile of v0, /device:TPU:0, one launch (start us, length us, event | category | flops | bytes accessed | tf_op | source)
XLA Modules:
  0.0 2684.2 jit_solution(3529834029223923130)
XLA Ops:
  34.8 22.7 all-gather.3.cloned.1.call-done
  57.6 134.2 %conditional.6 = (bf16[512,768]{0,1:T(8,128)(2,1)S(1)}) conditional(s32[]{:T(128)} %convert_element_type.731, () %tuple.60, (bf16[2,1,2048,128]{3,2,1,0:T(8,128)(2,1)S(1)}, f32[2048,128]{1,0:T(8,128)S(1)}, bf16[128]{0:T(256)(128)(2,1)S(1)}, bf16[128,768]{1,0:T(8,128)(2,1)S(1)}, bf16[768]{0:T(1024)(128)(2,1)S(1)}, ...), branch_computations={%region_3.0_spmd, %region_4.13_spmd} | conditional | flops 3323501568 | bytes 135663680 | solution.py:458
  80.8 29.5 %gather_fusion.7 = bf16[8192,128]{1,0:T(8,128)(2,1)} fusion(bf16[2048,128]{1,0:T(8,128)(2,1)S(1)} %copy.568, s32[8192]{0:T(1024)S(1)} %fusion.56), kind=kCustom, calls=%fused_computation.1 | custom fusion | bytes 4227072 | tf_op jit(solution)/shard_map/cond/branch_1_fun/gather | solution.py:111
  127.3 29.5 %gather_fusion.6 = bf16[8192,128]{1,0:T(8,128)(2,1)} fusion(bf16[2048,128]{1,0:T(8,128)(2,1)S(1)} %copy.565, s32[8192]{0:T(1024)S(1)} %fusion.56), kind=kCustom, calls=%fused_computation | custom fusion | bytes 4227072 | tf_op jit(solution)/shard_map/cond/branch_1_fun/gather | solution.py:112
  196.2 15.7 collective-permute-done
  212.0 134.3 %conditional.7 = (bf16[512,768]{0,1:T(8,128)(2,1)}, bf16[1,1,512,768]{3,2,1,0:T(8,128)(2,1)S(1)}) conditional(s32[]{:T(128)} %convert_element_type.731, (bf16[512,768]{1,0:T(8,128)(2,1)}, s32[2,1]{0,1:T(1,128)S(1)}, f32[200,384]{1,0:T(8,128)}, f32[512,384]{1,0:T(8,128)S(1)}, bf16[384]{0:T(512)(128)(2,1)S(1)}, ...), branch_computations={%region_15.24_spmd, %region_24.33_spmd} | conditional | flops 9739124736 | bytes 223270992 | solution.py:458
  237.9 29.5 %gather_fusion.9 = bf16[8192,128]{1,0:T(8,128)(2,1)} fusion(bf16[2048,128]{1,0:T(8,128)(2,1)S(1)} %copy.579, s32[8192]{0:T(1024)S(1)} %fusion.119), kind=kCustom, calls=%fused_computation.3 | custom fusion | bytes 4227072 | tf_op jit(solution)/shard_map/cond/branch_1_fun/gather | solution.py:111
  283.3 29.5 %gather_fusion.8 = bf16[8192,128]{1,0:T(8,128)(2,1)} fusion(bf16[2048,128]{1,0:T(8,128)(2,1)S(1)} %copy.576, s32[8192]{0:T(1024)S(1)} %fusion.119), kind=kCustom, calls=%fused_computation.2 | custom fusion | bytes 4227072 | tf_op jit(solution)/shard_map/cond/branch_1_fun/gather | solution.py:112
  350.9 16.0 collective-permute-done.1
  366.9 30.7 %conditional.9 = (bf16[512,768]{1,0:T(8,128)(2,1)}, f32[384]{0:T(512)}, f32[384,4608]{1,0:T(8,128)}, f32[4608]{0:T(1024)}, f32[768,3072]{1,0:T(8,128)}, /*index=...) conditional(s32[]{:T(128)} %convert_element_type.731, ...), branch_computations={%region_44.61_spmd, %region_61.62_spmd} | conditional | flops 28818231296 | bytes 787697472 | solution.py:491
  399.5 203.0 %collective-permute-done.2 = bf16[512,768]{1,0:T(8,128)(2,1)S(1)} collective-permute-done((bf16[512,768]{1,0:T(8,128)(2,1)}, bf16[512,768]{1,0:T(8,128)(2,1)S(1)}, u32[]{:S(2)}, u32[]{:S(2)}) %collective-permute-start.2) | collective-permute-done | bytes 786464 | tf_op jit(solution)/shard_map/ppermute | solution.py:17
  602.6 362.7 %conditional.10 = (bf16[512,768]{1,0:T(8,128)(2,1)}, f32[128]{0:T(128)}, f32[128,768]{1,0:T(8,128)}, f32[768]{0:T(1024)}, f32[128,512]{1,0:T(8,128)}, /*index=5*...) conditional(s32[]{:T(128)} %convert_element_type.731, ...), branch_computations={%region_62.79_spmd, %region_79.98_spmd} | conditional | flops 28818231296 | bytes 800186240 | solution.py:491
  632.7 29.5 %gather_fusion.2 = bf16[8192,128]{1,0:T(8,128)(2,1)} fusion(bf16[2048,128]{1,0:T(8,128)(2,1)S(1)} %copy.590, s32[8192]{0:T(1024)S(1)} %fusion.201), kind=kCustom, calls=%fused_computation.6 | custom fusion | bytes 4227072 | tf_op jit(solution)/shard_map/cond/branch_1_fun/gather | solution.py:112
  671.5 29.5 %gather_fusion = bf16[8192,128]{1,0:T(8,128)(2,1)} fusion(bf16[2048,128]{1,0:T(8,128)(2,1)S(1)} %copy.586, s32[8192]{0:T(1024)S(1)} %fusion.201), kind=kCustom, calls=%fused_computation.4 | custom fusion | bytes 4227072 | tf_op jit(solution)/shard_map/cond/branch_1_fun/gather | solution.py:111
  779.7 45.0 %scatter_custom_fusion.1 = f32[2048,128]{1,0:T(8,128)S(1)} fusion(s32[8192]{0:T(1024)} %bitcast.688, f32[8192,128]{1,0:T(8,128)} %copy.606, f32[]{:T(128)} %constant.287.clone), kind=kCustom, calls=%fused_computation.310 | custom fusion | flops 1048576 | bytes 1049088 | tf_op jit(solution)/shard_map/cond/branch_1_fun/scatter-add | solution.py:142
  856.3 45.5 %scatter_custom_fusion = f32[2048,128]{1,0:T(8,128)} fusion(s32[8192]{0:T(1024)} %bitcast.689, f32[8192,128]{1,0:T(8,128)} %copy.602, f32[]{:T(128)} %constant.287.clone), kind=kCustom, calls=%fused_computation.312 | custom fusion | flops 1048576 | bytes 1049088 | tf_op jit(solution)/shard_map/cond/branch_1_fun/scatter-add | solution.py:137
  966.6 18.7 collective-permute-done.3
  985.3 329.8 %conditional.11 = (f32[128]{0:T(128)S(1)}, f32[128,768]{1,0:T(8,128)}, f32[768]{0:T(1024)S(1)}, f32[128,512]{1,0:T(8,128)}, f32[128]{0:T(128)S(1)}, /*index=5*/f...) conditional(s32[]{:T(128)} %convert_element_type.731, () %tuple.65, ...), branch_computations={%region_98.99_spmd, %region_99.118_spmd} | conditional | flops 5158295552 | bytes 559648448 | solution.py:491
  1010.2 29.5 %gather_fusion.5 = bf16[8192,128]{1,0:T(8,128)(2,1)} fusion(bf16[2048,128]{1,0:T(8,128)(2,1)S(1)} %copy.612, s32[8192]{0:T(1024)S(1)} %fusion.286), kind=kCustom, calls=%fused_computation.9 | custom fusion | bytes 4227072 | tf_op jit(solution)/shard_map/cond/branch_1_fun/gather | solution.py:112
  1048.9 29.5 %gather_fusion.3 = bf16[8192,128]{1,0:T(8,128)(2,1)} fusion(bf16[2048,128]{1,0:T(8,128)(2,1)S(1)} %copy.608, s32[8192]{0:T(1024)S(1)} %fusion.286), kind=kCustom, calls=%fused_computation.7 | custom fusion | bytes 4227072 | tf_op jit(solution)/shard_map/cond/branch_1_fun/gather | solution.py:111
  1156.3 44.7 %scatter_custom_fusion.3 = f32[2048,128]{1,0:T(8,128)S(1)} fusion(s32[8192]{0:T(1024)S(1)} %bitcast.686, f32[8192,128]{1,0:T(8,128)} %copy.628, f32[]{:T(128)} %constant.298.clone), kind=kCustom, calls=%fused_computation.461 | custom fusion | flops 1048576 | bytes 1049088 | tf_op jit(solution)/shard_map/cond/branch_1_fun/scatter-add | solution.py:142
  1232.8 45.8 %scatter_custom_fusion.2 = f32[2048,128]{1,0:T(8,128)} fusion(s32[8192]{0:T(1024)S(1)} %bitcast.687, f32[8192,128]{1,0:T(8,128)} %copy.624, f32[]{:T(128)} %constant.298.clone), kind=kCustom, calls=%fused_computation.463 | custom fusion | flops 1048576 | bytes 1049088 | tf_op jit(solution)/shard_map/cond/branch_1_fun/scatter-add | solution.py:137
  1322.2 19.5 add.1020
  1407.0 167.9 %reduce-scatter.48.cloned.1.call-done = f32[16,32,512]{2,1,0:T(8,128)} async-done(((f32[16,512,512]{2,1,0:T(8,128)}), f32[16,32,512]{2,1,0:T(8,128)}) %reduce-scatter.48.cloned.1.call-update) | async-done | bytes 1048592 | tf_op jit(solution)/shard_map/reduce_scatter | solution.py:509
  1574.9 13.8 fusion.567
  1599.6 713.1 %all-reduce.12 = (bf16[128]{0:T(256)(128)(2,1)}, bf16[128,768]{1,0:T(8,128)(2,1)}, bf16[768]{0:T(1024)(128)(2,1)}, bf16[128,512]{1,0:T(8,128)(2,1)}, bf16[128]{0...) all-reduce(f32[128]{0:T(128)} %add.1002, ...), channel_id=1, replica_groups=mesh['section'=2,'dp'=16] {'dp'}, use_global_device_ids=true, to_apply=%region_119.120 | all-reduce | flops 8643408 | bytes 51860448 | tf_op jit(solution)/shard_map/psum | solution.py:528
  2333.1 78.5 %all-reduce.10 = (bf16[128]{0:T(256)(128)(2,1)S(1)}, bf16[768]{0:T(1024)(128)(2,1)S(1)}, bf16[128]{0:T(256)(128)(2,1)S(1)}, bf16[16]{0:T(256)(128)(2,1)S(1)}, bf...) all-reduce(bf16[128]{0:T(256)(128)(2,1)S(1)} %copy-done.300, ...), channel_id=4, replica_groups=mesh['section'=2,'dp'=16] {'section'}, use_global_device_ids=true, to_apply=%region_120.121.clone | all-reduce | flops 6992 | bytes 27968
  2437.5 35.4 %reduce-scatter.46.cloned.1.call-done = bf16[768,768]{1,0:T(8,128)(2,1)} async-done(((bf16[1536,768]{1,0:T(8,128)(2,1)}), bf16[768,768]{1,0:T(8,128)(2,1)}) %reduce-scatter.46.cloned.1.call-update) | async-done | bytes 1179664 | tf_op jit(solution)/shard_map/reduce_scatter | solution.py:616
  2475.7 47.5 %reduce-scatter.38.cloned.1.call-done = bf16[192,4608]{1,0:T(8,128)(2,1)} async-done(((bf16[384,4608]{1,0:T(8,128)(2,1)}), bf16[192,4608]{1,0:T(8,128)(2,1)}) %reduce-scatter.38.cloned.1.call-update) | async-done | bytes 1769488 | tf_op jit(solution)/shard_map/reduce_scatter | solution.py:598
  2526.9 59.2 %reduce-scatter.40.cloned.1.call-done = bf16[384,3072]{1,0:T(8,128)(2,1)} async-done(((bf16[768,3072]{1,0:T(8,128)(2,1)}), bf16[384,3072]{1,0:T(8,128)(2,1)}) %reduce-scatter.40.cloned.1.call-update) | async-done | bytes 2359312 | tf_op jit(solution)/shard_map/reduce_scatter | solution.py:604
  2590.5 57.8 %reduce-scatter.44.cloned.1.call-done = bf16[384,3072]{1,0:T(8,128)(2,1)} async-done(((bf16[768,3072]{1,0:T(8,128)(2,1)}), bf16[384,3072]{1,0:T(8,128)(2,1)}) %reduce-scatter.44.cloned.1.call-update) | async-done | bytes 2359312 | tf_op jit(solution)/shard_map/reduce_scatter | solution.py:613
  2652.7 24.5 reduce-scatter.20.cloned.1.call-done
  (848 shorter events, 735.1 us)
Async XLA Ops:
  7.2 50.3 %all-gather.3.cloned.1.call-start = ((), (), s32[]{:S(2)}) async-start(), calls=%async_computation.16 | async-start | bytes 2228224 | tf_op jit(solution)/shard_map/all_gather | solution.py:381
  13.3 198.7 %all-gather.5.cloned.1.call-start = ((), (), s32[]{:S(2)}) async-start(), calls=%async_computation.17 | async-start | bytes 8912896 | tf_op jit(solution)/shard_map/all_gather | solution.py:380
  31.0 26.5 copy-start.23
  31.0 26.5 copy-start.110
  31.2 1370.3 %reduce-scatter.34.cloned.1.call-start = ((), (), s32[]{:S(2)}) async-start(), calls=%async_computation.25 | async-start | bytes 4456448 | tf_op jit(solution)/shard_map/reduce_scatter | solution.py:510
  31.7 180.3 %copy-start.1 = (f32[2048,128]{1,0:T(8,128)}, f32[2048,128]{1,0:T(8,128)S(1)}, u32[]{:S(2)}) copy-start(f32[2048,128]{1,0:T(8,128)S(1)} %convert_element_type.732) | copy-start | bytes 3145732
  32.9 179.1 %copy-start.136 = (s32[64,128]{1,0:T(8,128)}, s32[64,128]{1,0:T(8,128)S(1)}, u32[]{:S(2)}) copy-start(s32[64,128]{1,0:T(8,128)S(1)} %iota_add_fusion) | copy-start | bytes 98308
  193.0 19.0 collective-permute-start
  196.2 406.3 %copy-start.5 = (f32[512,384]{1,0:T(8,128)}, f32[512,384]{1,0:T(8,128)S(1)}, u32[]{:S(2)}) copy-start(f32[512,384]{1,0:T(8,128)S(1)} %convert_element_type.739) | copy-start | bytes 2359300
  348.7 18.2 collective-permute-start.1
  366.9 235.6 %copy-start.2 = (f32[2048,128]{1,0:T(8,128)S(1)}, f32[2048,128]{1,0:T(8,128)}, u32[]{:S(2)}) copy-start(f32[2048,128]{1,0:T(8,128)} %copy-done.1) | copy-start | bytes 3145732
  366.9 235.6 %copy-start.118 = (bf16[128,512]{1,0:T(8,128)(2,1)S(1)}, bf16[128,512]{1,0:T(8,128)(2,1)}, u32[]{:S(2)}) copy-start(bf16[128,512]{1,0:T(8,128)(2,1)} %param.59) | copy-start | bytes 393220
  398.2 204.3 %collective-permute-start.2 = (bf16[512,768]{1,0:T(8,128)(2,1)}, bf16[512,768]{1,0:T(8,128)(2,1)S(1)}, u32[]{:S(2)}, u32[]{:S(2)}) collective-permute-start(bf16[512,768]{1,0:T(8,128)(2,1)} %get-tuple-element.427), channel_id=1, source_target_pairs={{16,0},{17,1},{18,2},{19,3},{20,4},{21,5},{22,6},{23,7},{24,8},{25... | collective-permute-start | bytes 2359304 | tf_op jit(solution)/shard_map/ppermute | solution.py:17
  779.7 46.0 %copy-start.203 = (f32[64,4,32]{2,1,0:T(4,128)S(1)}, f32[64,4,32]{2,1,0:T(4,128)}, u32[]{:S(2)}) copy-start(f32[64,4,32]{2,1,0:T(4,128)} %get-tuple-element.1250) | copy-start | bytes 98308 | tf_op jit(solution)/shard_map/cond
  965.3 20.0 collective-permute-start.3
  1322.1 252.8 %reduce-scatter.48.cloned.1.call-start = ((), (), s32[]{:S(2)}) async-start(), calls=%async_computation.32 | async-start | bytes 17825792 | tf_op jit(solution)/shard_map/reduce_scatter | solution.py:509
  1341.7 989.3 %reduce-scatter.22.cloned.1.call-start = ((), (), s32[]{:S(2)}) async-start(), calls=%async_computation.19 | async-start | bytes 1572864 | tf_op jit(solution)/shard_map/reduce_scatter | solution.py:559
  1344.0 1071.9 %reduce-scatter.50.cloned.1.call-start = ((), (), s32[]{:S(2)}) async-start(), calls=%async_computation.33 | async-start | bytes 49152
  1400.2 174.7 %copy-start.192 = (f32[32,512]{1,0:T(8,128)S(1)}, f32[32,512]{1,0:T(8,128)}, u32[]{:S(2)}) copy-start(f32[32,512]{1,0:T(8,128)} %copy-done.191) | copy-start | bytes 196612
  1400.2 174.7 %copy-start.240 = (f32[32,512]{1,0:T(8,128)S(1)}, f32[32,512]{1,0:T(8,128)}, u32[]{:S(2)}) copy-start(f32[32,512]{1,0:T(8,128)} %copy-done.239) | copy-start | bytes 196612
  2314.1 103.2 %reduce-scatter.28.cloned.1.call-start = ((), (), s32[]{:S(2)}) async-start(), calls=%async_computation.22 | async-start | bytes 49152 | tf_op jit(solution)/shard_map/reduce_scatter | solution.py:577
  2314.9 103.8 %reduce-scatter.32.cloned.1.call-start = ((), (), s32[]{:S(2)}) async-start(), calls=%async_computation.24 | async-start | bytes 98304 | tf_op jit(solution)/shard_map/reduce_scatter | solution.py:583
  2315.6 104.4 %reduce-scatter.26.cloned.1.call-start = ((), (), s32[]{:S(2)}) async-start(), calls=%async_computation.21 | async-start | bytes 196608 | tf_op jit(solution)/shard_map/reduce_scatter | solution.py:571
  2316.4 105.2 %reduce-scatter.30.cloned.1.call-start = ((), (), s32[]{:S(2)}) async-start(), calls=%async_computation.23 | async-start | bytes 196608 | tf_op jit(solution)/shard_map/reduce_scatter | solution.py:580
  2317.0 106.1 %reduce-scatter.24.cloned.1.call-start = ((), (), s32[]{:S(2)}) async-start(), calls=%async_computation.20 | async-start | bytes 294912 | tf_op jit(solution)/shard_map/reduce_scatter | solution.py:565
  2317.7 107.0 %reduce-scatter.36.cloned.1.call-start = ((), (), s32[]{:S(2)}) async-start(), calls=%async_computation.26 | async-start | bytes 294912 | tf_op jit(solution)/shard_map/reduce_scatter | solution.py:592
  2318.3 117.1 %reduce-scatter.42.cloned.1.call-start = ((), (), s32[]{:S(2)}) async-start(), calls=%async_computation.29 | async-start | bytes 1769472 | tf_op jit(solution)/shard_map/reduce_scatter | solution.py:610
  2319.0 153.8 %reduce-scatter.46.cloned.1.call-start = ((), (), s32[]{:S(2)}) async-start(), calls=%async_computation.31 | async-start | bytes 3538944 | tf_op jit(solution)/shard_map/reduce_scatter | solution.py:616
  2319.6 203.6 %reduce-scatter.38.cloned.1.call-start = ((), (), s32[]{:S(2)}) async-start(), calls=%async_computation.27 | async-start | bytes 5308416 | tf_op jit(solution)/shard_map/reduce_scatter | solution.py:598
  2320.2 265.9 %reduce-scatter.40.cloned.1.call-start = ((), (), s32[]{:S(2)}) async-start(), calls=%async_computation.28 | async-start | bytes 7077888 | tf_op jit(solution)/shard_map/reduce_scatter | solution.py:604
  2320.8 327.5 %reduce-scatter.44.cloned.1.call-start = ((), (), s32[]{:S(2)}) async-start(), calls=%async_computation.30 | async-start | bytes 7077888 | tf_op jit(solution)/shard_map/reduce_scatter | solution.py:613
  2321.4 355.8 %reduce-scatter.20.cloned.1.call-start = ((), (), s32[]{:S(2)}) async-start(), calls=%async_computation.18 | async-start | bytes 2359296 | tf_op jit(solution)/shard_map/reduce_scatter | solution.py:556
  (215 other events, 1181.5 us)
Sparse Core Ops, SparseCore 0:
  13.4 44.0 all-gather.2
  59.7 73.6 all-gather.4
  1322.2 70.4 reduce-scatter.33
  1397.2 177.6 reduce-scatter.47
  1577.7 19.2 reduce-scatter.21
  2314.3 18.1 reduce-scatter.49
  2335.2 9.8 reduce-scatter.27
  2347.8 9.8 reduce-scatter.31
  2360.5 10.2 reduce-scatter.25
  2373.4 10.2 reduce-scatter.29
  2386.5 10.9 reduce-scatter.23
  2399.6 11.0 reduce-scatter.35
  2413.5 21.7 reduce-scatter.41
  2438.1 34.6 reduce-scatter.45
  2475.5 47.6 reduce-scatter.37
  2526.1 59.9 reduce-scatter.39
  2588.2 59.9 reduce-scatter.43
  2651.0 26.0 reduce-scatter.19
where the time goes:
time: 2690 us; the launch traced here: 2680 us
  blocking collectives  792 us (29%)
  waiting for transfers between devices  684 us (25%)
  local copies, waits for them, and re-layouts  536 us (20%)
  other arithmetic  379 us (14%)
  matrix products  245 us (9%)
    psum x1, blocking collectives, local(): lax.psum((grads_all[0], grads_all[1], grads_all[2], grads_all[3], grads_a...  713 us
    ppermute x4, waiting for transfers between devices, from_behind(): return lax.ppermute(block, axis, route)  254 us
    reduce_scatter x1, waiting for transfers between devices, local(): lax.psum_scatter(total_token_bias, 'dp', scatter_dimension=1, tiled=True)  168 us
    gather x8, local copies, waits for them, and re-layouts, atom_windows(): key_rows[positions].reshape(windows, span_key, head_count, head_size)  135 us
    gather x8, local copies, waits for them, and re-layouts, atom_windows(): value_rows[positions].reshape(windows, span_key, head_count, head_size)  132 us
    scatter-add x2, other arithmetic, atom_backward_attend(): d_keys = jnp.zeros((atom_count, col_count), WIDE).at[flat_positions].add(...  91.3 us
    scatter-add x2, other arithmetic, atom_backward_attend(): d_values = jnp.zeros((atom_count, col_count), WIDE).at[flat_positions].ad...  89.7 us
    unnamed x1, blocking collectives  78.5 us
  transfers between devices with their start and end apart: 22, of which 12 were waited for; matrix products, arithmetic and copies ran while one was open for 11% of the time, Pallas kernels for 0%

commit v1 on v0

--- a/solution.py
+++ b/solution.py
@@ -361,154 +361,64 @@
         tokgu_weight,
         tokdown_weight,
     )
-    micro_count = atom_features.shape[0]
-    atom_count = atom_features.shape[2]
-    atom_width = atom_features.shape[3]
+    section = lax.axis_index("section")
+    sections = lax.axis_size("section")
     length = cotangent.shape[2]
-    model_width = cotangent.shape[3]
-    section_index = lax.axis_index("section")
-    is_first = section_index == 0
-    repr_wide = pair_repr.astype(WIDE)
-    pairs_wide = atom_pairs.astype(WIDE)
+
+    def mine(member):
+        return lax.dynamic_index_in_dim(member, section, 0, keepdims=False)[0]
+
+    rows = pair_repr.shape[0] // sections
+    repr_wide = lax.dynamic_slice_in_dim(pair_repr, section * rows, rows, 0).astype(WIDE)
+    span = atom_pairs.shape[2] // sections
+    pairs_wide = lax.dynamic_slice_in_dim(atom_pairs, section * span, span, 2).astype(WIDE)
+    both = ("dp", "section")
     token_part = token_slab(
         repr_wide, tokpair_gain.astype(WIDE), tokpair_weight.astype(WIDE)
     ).astype(LOWTYPE)
     atom_part = atom_slab(
         pairs_wide, atompair_gain.astype(WIDE), atompair_weight.astype(WIDE)
     ).astype(LOWTYPE)
-    token_bias, atom_bias = (
-        lax.all_gather(token_part, "dp", axis=1, tiled=True),
-        lax.all_gather(atom_part, "dp", axis=0, tiled=True),
-    )
+    token_bias = lax.all_gather(token_part, both, axis=1, tiled=True)
+    windows = atom_pairs.shape[0] * lax.axis_size("dp")
+    atom_bias = lax.all_gather(atom_part[:, :, None], both, axis=0, tiled=True)
+    atom_bias = atom_bias.reshape(windows // atom_pairs.shape[0], sections, atom_pairs.shape[0], -1, span, atom_pairs.shape[3])
+    atom_bias = atom_bias.transpose(0, 2, 3, 1, 4, 5).reshape(windows, -1, atom_pairs.shape[2], atom_pairs.shape[3])
     positions = window_start[:, None] + jnp.arange(atom_bias.shape[3], dtype=jnp.int32)[None, :]
     onehot_wide = (atom_token[None, :] == jnp.arange(length, dtype=jnp.int32)[:, None]).astype(WIDE)
     counts = jnp.sum(onehot_wide, axis=1, keepdims=True)
     onehot_low = onehot_wide.astype(LOWTYPE)
     atom_cond = atom_single.astype(WIDE)
-    single_wide = single_repr.astype(WIDE)
     atom_fwd = partial(atom_forward_attend, atom_bias=atom_bias, positions=positions)
     atom_bwd = partial(atom_backward_attend, atom_bias=atom_bias, positions=positions)
     token_fwd = partial(token_forward_attend, token_bias=token_bias)
     token_bwd = partial(token_backward_attend, token_bias=token_bias)
-    empty_send = jnp.zeros((length, model_width), LOWTYPE)
-    zero_tokens = jnp.zeros((length, model_width), WIDE)
-    zero_atoms = jnp.zeros((atom_count, atom_width), WIDE)
-    atom_zero = tuple((jnp.zeros(member.shape, WIDE) for member in atom_block + (gather_weight,)))
-    token_zero = tuple((jnp.zeros(member.shape, WIDE) for member in token_block))
-    zero_token_bias = jnp.zeros(token_bias.shape, WIDE)
-    zero_atom_bias = jnp.zeros(atom_bias.shape, WIDE)
-
-    def token_condition(sample):
-        return single_wide + noise_table[noise_index[sample, 0]]
-
-    def pooled_tokens(features_low):
-        result, stored = block_forward(features_low.astype(WIDE), atom_cond, atom_block, atom_fwd)
-        result_low = result.astype(LOWTYPE)
-        pre_act = product(result_low, gather_weight)
-        pooled = product(onehot_low, jax.nn.silu(pre_act).astype(LOWTYPE)) / counts
-        return (result_low, pre_act, pooled, stored)
-
-    def atom_back(features_low, d_pooled):
-        features = features_low.astype(WIDE)
-        result_low, pre_act, pooled, stored = pooled_tokens(features_low)
-        d_rows = (d_pooled.astype(WIDE) / counts)[atom_token]
-        d_pre = (d_rows * silu_slope(pre_act)).astype(LOWTYPE)
-        grad_gather = product_left(result_low, d_pre)
-        d_result = product_right(d_pre, gather_weight)
-        d_features, gradients, d_bias = block_backward(
-            features, atom_cond, atom_block, stored, atom_bwd, d_result
-        )
-        return (d_features, gradients + (grad_gather,), d_bias)
-
-    def token_back(inbound, sample, d_output):
-        condition = token_condition(sample)
-        features = inbound.astype(WIDE)
-        result, stored = block_forward(features, condition, token_block, token_fwd)
-        return block_backward(
-            features, condition, token_block, stored, token_bwd, d_output.astype(WIDE)
-        )
-
-    bias_state = (
-        jnp.zeros(token_part.shape, WIDE),
-        jnp.zeros(atom_part.shape, WIDE),
-        zero_token_bias,
-        zero_atom_bias,
-    )
-    atom_sums = atom_zero
-    token_sums = token_zero
-    received = empty_send
-    kept_inputs = []
-    token_outputs = []
-    for tick_index in range(micro_count + 1):
-
-        def section_one(tick_index=tick_index):
-            if tick_index < micro_count:
-                pooled = pooled_tokens(atom_features[tick_index, 0])[2]
-                return (pooled.astype(LOWTYPE), zero_tokens)
-            return (empty_send, zero_tokens)
-
-        def section_two(inbound=received, tick_index=tick_index):
-            if tick_index >= 1:
-                result, stored = block_forward(
-                    inbound.astype(WIDE), token_condition(tick_index - 1), token_block, token_fwd
-                )
-                return (empty_send, result)
-            return (empty_send, zero_tokens)
-
-        sending, produced = lax.cond(is_first, section_one, section_two)
-        if tick_index >= 1:
-            kept_inputs.append(received)
-            token_outputs.append(produced)
-        if tick_index < micro_count:
-            received = from_behind(sending, "section", 1)
-    back_in = empty_send
-    atom_grad_rows = [zero_atoms] * micro_count
-    for tick_index in range(micro_count + 1):
-        token_sample = micro_count - 1 - tick_index
-        atom_sample = micro_count - tick_index
-
-        def section_one(inbound=back_in, atom_sample=atom_sample):
-            if atom_sample < micro_count:
-                d_features, gradients, d_bias = atom_back(atom_features[atom_sample, 0], inbound)
-                return (empty_send, d_features, gradients, token_zero, zero_token_bias, d_bias)
-            return (empty_send, zero_atoms, atom_zero, token_zero, zero_token_bias, zero_atom_bias)
-
-        def section_two(token_sample=token_sample):
-            if token_sample >= 0:
-                d_inbound, gradients, d_bias = token_back(
-                    kept_inputs[token_sample], token_sample, cotangent[token_sample, 0]
-                )
-                return (
-                    d_inbound.astype(LOWTYPE),
-                    zero_atoms,
-                    atom_zero,
-                    gradients,
-                    d_bias,
-                    zero_atom_bias,
-                )
-            return (empty_send, zero_atoms, atom_zero, token_zero, zero_token_bias, zero_atom_bias)
-
-        sending, d_features, grads_atom, grads_token, d_token_bias, d_atom_bias = lax.cond(
-            is_first, section_one, section_two
-        )
-        if atom_sample < micro_count:
-            atom_grad_rows[atom_sample] = d_features
-        atom_sums = tuple((left + right for left, right in zip(atom_sums, grads_atom)))
-        token_sums = tuple((left + right for left, right in zip(token_sums, grads_token)))
-        add_slab_token, add_slab_atom, add_total_token_bias, add_total_atom_bias = bias_state
-        bias_state = (
-            add_slab_token,
-            add_slab_atom,
-            add_total_token_bias + d_token_bias,
-            add_total_atom_bias + d_atom_bias,
-        )
-        if token_sample >= 0:
-            back_in = from_behind(sending, "section", -1)
-    slab_token, slab_atom, total_token_bias, total_atom_bias = bias_state
-    slab_token, slab_atom = (
-        lax.psum_scatter(total_token_bias, "dp", scatter_dimension=1, tiled=True),
-        lax.psum_scatter(total_atom_bias, "dp", scatter_dimension=0, tiled=True),
-    )
+
+    features = mine(atom_features).astype(WIDE)
+    condition = single_repr.astype(WIDE) + noise_table[mine(noise_index)]
+    result, atom_stored = block_forward(features, atom_cond, atom_block, atom_fwd)
+    result_low = result.astype(LOWTYPE)
+    pre_act = product(result_low, gather_weight)
+    pooled = product(onehot_low, jax.nn.silu(pre_act).astype(LOWTYPE)) / counts
+    token_in = pooled.astype(LOWTYPE).astype(WIDE)
+    output, token_stored = block_forward(token_in, condition, token_block, token_fwd)
+
+    d_token_in, token_grads, d_token_bias = block_backward(
+        token_in, condition, token_block, token_stored, token_bwd, mine(cotangent).astype(WIDE)
+    )
+    d_scaled = (d_token_in.astype(LOWTYPE).astype(WIDE) / counts).astype(LOWTYPE)
+    d_rows = product_left(onehot_low, d_scaled)
+    d_pre = (d_rows * silu_slope(pre_act)).astype(LOWTYPE)
+    grad_gather = product_left(result_low, d_pre)
+    d_result = product_right(d_pre, gather_weight)
+    d_features, atom_grads, d_atom_bias = block_backward(
+        features, atom_cond, atom_block, atom_stored, atom_bwd, d_result
+    )
+    slab_token = lax.psum_scatter(d_token_bias.astype(LOWTYPE), both, scatter_dimension=1, tiled=True).astype(WIDE)
+    shape = d_atom_bias.shape
+    d_atom_bias = d_atom_bias.reshape(-1, atom_pairs.shape[0], shape[1], sections, span, shape[3]).transpose(0, 3, 1, 2, 4, 5)
+    d_atom_bias = d_atom_bias.reshape(-1, shape[1], span, shape[3])
+    slab_atom = lax.psum_scatter(d_atom_bias.astype(LOWTYPE), both, scatter_dimension=0, tiled=True).astype(WIDE)
     _, token_slab_back = jax.vjp(
         partial(token_slab, repr_wide), tokpair_gain.astype(WIDE), tokpair_weight.astype(WIDE)
     )
@@ -517,114 +427,32 @@
         partial(atom_slab, pairs_wide), atompair_gain.astype(WIDE), atompair_weight.astype(WIDE)
     )
     grad_atom_gain, grad_atom_weight = atom_slab_back(slab_atom)
-    grads_all = (
-        atom_sums[0:8]
-        + (grad_atom_gain, grad_atom_weight, atom_sums[8])
-        + token_sums
+    grads = (
+        tuple(atom_grads)
+        + (grad_atom_gain, grad_atom_weight, grad_gather)
+        + tuple(token_grads)
         + (grad_tok_gain, grad_tok_weight)
     )
-    output_full = jnp.stack(token_outputs)[:, None]
-    atom_full = jnp.stack(atom_grad_rows)[:, None]
-    totals = lax.psum(
-        (
-            grads_all[0],
-            grads_all[1],
-            grads_all[2],
-            grads_all[3],
-            grads_all[4],
-            grads_all[5],
-            grads_all[6],
-            grads_all[7],
-            grads_all[8],
-            grads_all[9],
-            grads_all[10],
-            grads_all[11],
-            grads_all[12],
-            grads_all[13],
-            grads_all[14],
-            grads_all[15],
-            grads_all[16],
-            grads_all[17],
-            grads_all[18],
-            grads_all[19],
-            grads_all[20],
-        ),
-        "dp",
-    )
-    finished = tuple(
-        (
-            lax.psum_scatter(
-                output_full.astype(jnp.bfloat16), "section", scatter_dimension=2, tiled=True
-            ).astype(jnp.float32),
-            lax.psum_scatter(
-                atom_full.astype(jnp.bfloat16), "section", scatter_dimension=2, tiled=True
-            ).astype(jnp.float32),
-            lax.psum_scatter(
-                totals[0].astype(jnp.bfloat16), "section", scatter_dimension=0, tiled=True
-            ).astype(jnp.float32),
-            lax.psum_scatter(
-                totals[1].astype(jnp.bfloat16), "section", scatter_dimension=0, tiled=True
-            ).astype(jnp.float32),
-            lax.psum_scatter(
-                totals[2].astype(jnp.bfloat16), "section", scatter_dimension=0, tiled=True
-            ).astype(jnp.float32),
-            lax.psum_scatter(
-                totals[3].astype(jnp.bfloat16), "section", scatter_dimension=0, tiled=True
-            ).astype(jnp.float32),
-            lax.psum_scatter(
-                totals[4].astype(jnp.bfloat16), "section", scatter_dimension=0, tiled=True
-            ).astype(jnp.float32),
-            lax.psum_scatter(
-                totals[5].astype(jnp.bfloat16), "section", scatter_dimension=0, tiled=True
-            ).astype(jnp.float32),
-            lax.psum_scatter(
-                totals[6].astype(jnp.bfloat16), "section", scatter_dimension=0, tiled=True
-            ).astype(jnp.float32),
-            lax.psum_scatter(
-                totals[7].astype(jnp.bfloat16), "section", scatter_dimension=0, tiled=True
-            ).astype(jnp.float32),
-            lax.psum_scatter(
-                totals[8].astype(jnp.bfloat16), "section", scatter_dimension=0, tiled=True
-            ).astype(jnp.float32),
-            lax.psum_scatter(
-                totals[9].astype(jnp.bfloat16), "section", scatter_dimension=0, tiled=True
-            ).astype(jnp.float32),
-            lax.psum_scatter(
-                totals[10].astype(jnp.bfloat16), "section", scatter_dimension=0, tiled=True
-            ).astype(jnp.float32),
-            lax.psum_scatter(
-                totals[11].astype(jnp.bfloat16), "section", scatter_dimension=0, tiled=True
-            ).astype(jnp.float32),
-            lax.psum_scatter(
-                totals[12].astype(jnp.bfloat16), "section", scatter_dimension=0, tiled=True
-            ).astype(jnp.float32),
-            lax.psum_scatter(
-                totals[13].astype(jnp.bfloat16), "section", scatter_dimension=0, tiled=True
-            ).astype(jnp.float32),
-            lax.psum_scatter(
-                totals[14].astype(jnp.bfloat16), "section", scatter_dimension=0, tiled=True
-            ).astype(jnp.float32),
-            lax.psum_scatter(
-                totals[15].astype(jnp.bfloat16), "section", scatter_dimension=0, tiled=True
-            ).astype(jnp.float32),
-            lax.psum_scatter(
-                totals[16].astype(jnp.bfloat16), "section", scatter_dimension=0, tiled=True
-            ).astype(jnp.float32),
-            lax.psum_scatter(
-                totals[17].astype(jnp.bfloat16), "section", scatter_dimension=0, tiled=True
-            ).astype(jnp.float32),
-            lax.psum_scatter(
-                totals[18].astype(jnp.bfloat16), "section", scatter_dimension=0, tiled=True
-            ).astype(jnp.float32),
-            lax.psum_scatter(
-                totals[19].astype(jnp.bfloat16), "section", scatter_dimension=0, tiled=True
-            ).astype(jnp.float32),
-            lax.psum_scatter(
-                totals[20].astype(jnp.bfloat16), "section", scatter_dimension=0, tiled=True
-            ).astype(jnp.float32),
-        )
-    )
-    return (finished[0].astype(LOWTYPE),) + tuple(finished[1:])
+    large = [i for i, member in enumerate(grads) if member.size > 500000]
+    small = [i for i in range(len(grads)) if i not in large]
+    finished = [None] * len(grads)
+    flat = jnp.concatenate([grads[i].astype(LOWTYPE).reshape(sections, -1) for i in small], axis=1)
+    flat = lax.psum_scatter(flat, "section", scatter_dimension=0, tiled=True)
+    flat = lax.psum(flat, "dp")[0].astype(WIDE)
+    start = 0
+    for i in small:
+        size = grads[i].size // sections
+        finished[i] = flat[start : start + size].reshape((-1,) + grads[i].shape[1:])
+        start += size
+    for i in large:
+        half = lax.psum_scatter(grads[i].astype(LOWTYPE), "section", scatter_dimension=0, tiled=True)
+        finished[i] = lax.psum(half, "dp").astype(WIDE)
+
+    def to_halves(member):
+        halves = member.reshape(sections, -1, member.shape[1])
+        return lax.all_to_all(halves, "section", 0, 0, tiled=False)[:, None]
+
+    return (to_halves(output.astype(LOWTYPE)), to_halves(d_features.astype(LOWTYPE)).astype(WIDE)) + tuple(finished)
 
 
 def solution(mesh):

time: 2690 us -> 1260 us (0.47)
  blocking collectives: 792 us -> 11.4 us
  waiting for transfers between devices: 684 us -> 431 us
  local copies, waits for them, and re-layouts: 536 us -> 305 us
  other arithmetic: 379 us -> 219 us
    psum x1 -> x0, blocking collectives: 713 us -> none  [local(): lax.psum((grads_all[0], grads_all[1], grads_all[2], grads_all[3], grads_a...]
    ppermute x4 -> x0, waiting for transfers between devices: 254 us -> none  [from_behind(): return lax.ppermute(block, axis, route)]
    psum x0 -> x1, waiting for transfers between devices: none -> 157 us  [local(): flat = lax.psum(flat, 'dp')[0].astype(WIDE)]
    reduce_scatter x15 -> x7, waiting for transfers between devices: 401 us -> 261 us  [the longest x5 235 us: local(): lax.psum_scatter(grads[i].astype(LOWTYPE), 'section', scatter_dimension=0...]
    gather x8 -> x2, local copies, waits for them, and re-layouts: 135 us -> 36.1 us  [atom_windows(): key_rows[positions].reshape(windows, span_key, head_count, head_size)]
    gather x8 -> x2, local copies, waits for them, and re-layouts: 132 us -> 36.1 us  [atom_windows(): value_rows[positions].reshape(windows, span_key, head_count, head_size)]
    add x19 -> x0, other arithmetic: 83.6 us -> none  [the longest x17 57.2 us: local(): left + right]
    unnamed x1 -> x0, blocking collectives: 78.5 us -> none
  transfers between devices with their start and end apart: 22 -> 12, of which waited for: 12 -> 9; matrix products, arithmetic and copies ran while one was open for 11% -> 43% of each run, Pallas kernels for 0% -> 0%
where the time goes in v1:
time: 1260 us; the launch traced here: 1250 us
  waiting for transfers between devices  431 us (34%)
  local copies, waits for them, and re-layouts  305 us (24%)
  matrix products  258 us (20%)
  other arithmetic  219 us (17%)
  between operations  18 us (1%)
    reduce_scatter x5, waiting for transfers between devices, local(): lax.psum_scatter(grads[i].astype(LOWTYPE), 'section', scatter_dimension=0...  235 us
    psum x1, waiting for transfers between devices, local(): flat = lax.psum(flat, 'dp')[0].astype(WIDE)  157 us
    unnamed x320, local copies, waits for them, and re-layouts  77.3 us
    dot_general x12, matrix products, product_left(): lax.dot_general(left, right, (((0,), (0,)), ((), ())), preferred_element_...  52.8 us
    scatter-add x1, other arithmetic, atom_backward_attend(): d_keys = jnp.zeros((atom_count, col_count), WIDE).at[flat_positions].add(...  45.3 us
    scatter-add x1, other arithmetic, atom_backward_attend(): d_values = jnp.zeros((atom_count, col_count), WIDE).at[flat_positions].ad...  45.3 us
    dot_general x12, matrix products, product(): return jnp.dot(left, right, preferred_element_type=WIDE)  36.6 us
    gather x2, local copies, waits for them, and re-layouts, atom_windows(): value_rows[positions].reshape(windows, span_key, head_count, head_size)  36.1 us
  transfers between devices with their start and end apart: 12, of which 9 were waited for; matrix products, arithmetic and copies ran while one was open for 43% of the time, Pallas kernels for 0%

profile of v1, /device:TPU:0, one launch (start us, length us, event | category | flops | bytes accessed | tf_op | source)
XLA Modules:
  0.0 1247.9 jit_solution(12071066225219995413)
XLA Ops:
  57.8 32.0 %gather_fusion.1 = bf16[8192,128]{1,0:T(8,128)(2,1)} fusion(bf16[2048,128]{1,0:T(8,128)(2,1)} %get-tuple-element.155, s32[8192]{0:T(1024)} %fusion.190), kind=kCustom, calls=%fused_computation.1 | custom fusion | bytes 4227072 | tf_op jit(solution)/shard_map/gather | solution.py:111
  97.5 32.0 %gather_fusion = bf16[8192,128]{1,0:T(8,128)(2,1)} fusion(bf16[2048,128]{1,0:T(8,128)(2,1)} %get-tuple-element.156, s32[8192]{0:T(1024)} %fusion.190), kind=kCustom, calls=%fused_computation | custom fusion | bytes 4227072 | tf_op jit(solution)/shard_map/gather | solution.py:112
  142.8 6.4 convolution_add_fusion
  161.1 20.8 %convolution_bitcast_fusion.1 = f32[64,32,4,32]{1,3,2,0:T(8,128)} fusion(bf16[64,128,4,32]{1,0,3,2:T(8,128)(2,1)} %bitcast.282, f32[64,4,32]{2,1,0:T(4,128)} %get-tuple-element.160, f32[64,4,32,128]{3,2,1,0:T(8,128)} %copy-done.8), kind=kOutput, calls=%fused_computation.83 | convolution fusion | flops 70262912 | bytes 7372800 | tf_op jit(solution)/shard_map/whqk,wkhe->wqhe/dot_general | solution.py:83
  228.9 13.9 %copy.205 = bf16[16,512,512]{1,2,0:T(8,128)(2,1)} copy(bf16[16,512,512]{2,0,1:T(8,128)(2,1)} %all-gather.4.cloned.1.call-done) | data formatting | bytes 16777216 | tf_op jit(solution)/shard_map/all_gather | solution.py:382
  242.8 12.8 %fusion.225 = (f32[16,512]{1,0:T(8,128)}, f32[16,512,512]{1,2,0:T(8,128)}) fusion(bf16[16,512,512]{1,2,0:T(8,128)(2,1)} %copy.205, bf16[512,16,48]{0,2,1:T(8,128)(2,1)} %bitcast.275, bf16[512,16,48]{0,2,1:T(8,128)(2,1)} %bitcast.266), kind=kOutput, calls=%fused_computation.384 | convolution fusion | flops 423625216 | bytes 26771456 | tf_op jit(solution)/shard_map/sub | solution.py:72
  255.6 12.1 fusion.16
  303.9 12.2 fusion.84
  316.1 13.3 %multiply_reduce_fusion = (f32[16,512]{1,0:T(8,128)S(1)}, f32[16,512,512]{1,2,0:T(8,128)}) fusion(f32[16,512,512]{1,2,0:T(8,128)} %get-tuple-element.170, f32[16,512]{1,0:T(8,128)} %get-tuple-element.169, bf16[512,16,48]{0,2,1:T(8,128)(2,1)} %bitcast.290, bf16[512,16,48]{0,2,1:T(8,128)(2,1)} %bitcast.287), kind=kOutput, calls=%fused_computation.7 | convolution fusion | flops 415227904 | bytes 35192832 | tf_op jit(solution)/shard_map/wqhe,wkhe->whqk/dot_general | solution.py:88
  329.5 11.8 multiply_convert_fusion
  354.8 6.9 fusion.62
  364.7 6.7 multiply_convert_fusion.1
  391.8 8.3 multiply_reduce_fusion.1
  406.6 14.9 %copy.235 = bf16[16,512,512]{2,0,1:T(8,128)(2,1)} copy(bf16[16,512,512]{1,2,0:T(8,128)(2,1)} %copy-done.1) | data formatting | bytes 16777216 | tf_op jit(solution)/shard_map/convert_element_type | solution.py:93
  441.2 20.5 %convolution_bitcast_fusion = f32[64,128,4,32]{1,3,2,0:T(8,128)} fusion(bf16[64,32,4,32]{1,3,2,0:T(8,128)(2,1)} %copy.225, f32[64,4,32]{2,1,0:T(4,128)} %get-tuple-element.160, f32[64,4,32,128]{3,2,1,0:T(8,128)} %copy-done.8), kind=kOutput, calls=%fused_computation.82 | convolution fusion | flops 70262912 | bytes 8945664 | tf_op jit(solution)/shard_map/whqk,wqhe->wkhe/dot_general | solution.py:100
  471.8 5.6 copy.227
  477.4 45.3 %scatter_custom_fusion.1 = f32[2048,128]{1,0:T(8,128)} fusion(s32[8192]{0:T(1024)} %bitcast.294, f32[8192,128]{1,0:T(8,128)} %copy.227, f32[]{:T(128)} %constant.89.clone.1), kind=kCustom, calls=%fused_computation.289 | custom fusion | flops 1048576 | bytes 1049088 | tf_op jit(solution)/shard_map/scatter-add | solution.py:142
  524.8 6.0 fusion.226
  557.8 45.3 %scatter_custom_fusion = f32[2048,128]{1,0:T(8,128)} fusion(s32[8192]{0:T(1024)} %bitcast.295, f32[8192,128]{1,0:T(8,128)} %copy.224, f32[]{:T(128)} %constant.89.clone.1), kind=kCustom, calls=%fused_computation.291 | custom fusion | flops 1048576 | bytes 1049088 | tf_op jit(solution)/shard_map/scatter-add | solution.py:137
  656.5 5.7 fusion.99
  702.2 25.3 %reduce-scatter.10.cloned.1.call-done = bf16[16,16,512]{2,0,1:T(8,128)(2,1)} async-done(((bf16[16,512,512]{2,0,1:T(8,128)(2,1)}), bf16[16,16,512]{2,0,1:T(8,128)(2,1)}) %reduce-scatter.10.cloned.1.call-update) | async-done | bytes 262160 | tf_op jit(solution)/shard_map/reduce_scatter | solution.py:417
  752.3 6.4 convolution_convert_fusion
  758.8 7.0 convolution_convert_fusion.1
  767.0 7.0 convolution_convert_fusion.2
  782.7 21.5 %reduce-scatter.16.cloned.1.call-done = bf16[384,768]{1,0:T(8,128)(2,1)} async-done(((bf16[768,768]{1,0:T(8,128)(2,1)}), bf16[384,768]{1,0:T(8,128)(2,1)}) %reduce-scatter.16.cloned.1.call-update) | async-done | bytes 589840 | tf_op jit(solution)/shard_map/reduce_scatter | solution.py:448
  804.3 37.7 %reduce-scatter.20.cloned.1.call-done = bf16[768,768]{1,0:T(8,128)(2,1)} async-done(((bf16[1536,768]{1,0:T(8,128)(2,1)}), bf16[768,768]{1,0:T(8,128)(2,1)}) %reduce-scatter.20.cloned.1.call-update) | async-done | bytes 1179664 | tf_op jit(solution)/shard_map/reduce_scatter | solution.py:448
  841.9 50.5 %reduce-scatter.12.cloned.1.call-done = bf16[192,4608]{1,0:T(8,128)(2,1)} async-done(((bf16[384,4608]{1,0:T(8,128)(2,1)}), bf16[192,4608]{1,0:T(8,128)(2,1)}) %reduce-scatter.12.cloned.1.call-update) | async-done | bytes 1769488 | tf_op jit(solution)/shard_map/reduce_scatter | solution.py:448
  892.4 63.0 %reduce-scatter.18.cloned.1.call-done = bf16[384,3072]{1,0:T(8,128)(2,1)} async-done(((bf16[768,3072]{1,0:T(8,128)(2,1)}), bf16[384,3072]{1,0:T(8,128)(2,1)}) %reduce-scatter.18.cloned.1.call-update) | async-done | bytes 2359312 | tf_op jit(solution)/shard_map/reduce_scatter | solution.py:448
  955.5 62.8 %reduce-scatter.14.cloned.1.call-done = bf16[384,3072]{1,0:T(8,128)(2,1)} async-done(((bf16[768,3072]{1,0:T(8,128)(2,1)}), bf16[384,3072]{1,0:T(8,128)(2,1)}) %reduce-scatter.14.cloned.1.call-update) | async-done | bytes 2359312 | tf_op jit(solution)/shard_map/reduce_scatter | solution.py:448
  1022.1 11.4 all_to_all.10
  1039.9 8.2 all-to-all-done
  1048.1 156.7 %all-reduce.7.cloned.1.call-done = (bf16[1,192936]{1,0:T(2,128)(2,1)}, bf16[192,4608]{1,0:T(8,128)(2,1)}, bf16[384,3072]{1,0:T(8,128)(2,1)}, bf16[384,768]{1,0:T...) async-done(((bf16[1,192936]{1,0:T(2,128)(2,1)}, bf16[192,4608]{1,0:T(8,128)(2,1)}, bf16[384,3072]{1,0:T(8,128)(2,1)}, bf16[384,768]{1,0:T(8,128)(2,1)}, ...) | async-done | bytes 8643424 | tf_op jit(solution)/shard_map/psum | solution.py:441
  (548 shorter events, 439.8 us)
Async XLA Ops:
  7.2 135.7 %copy-start = (bf16[384,4608]{1,0:T(8,128)(2,1)S(1)}, bf16[384,4608]{1,0:T(8,128)(2,1)}, u32[]{:S(2)}) copy-start(bf16[384,4608]{1,0:T(8,128)(2,1)} %param.53) | copy-start | bytes 10616836
  7.2 142.0 %all-gather.6.cloned.1.call-start = ((), (), s32[]{:S(2)}) async-start(), calls=%async_computation.17 | async-start | bytes 2162688 | tf_op jit(solution)/shard_map/all_gather | solution.py:384
  11.7 217.2 %all-gather.4.cloned.1.call-start = ((), (), s32[]{:S(2)}) async-start(), calls=%async_computation.9 | async-start | bytes 8650752 | tf_op jit(solution)/shard_map/all_gather | solution.py:382
  18.6 10.1 copy-start.127
  18.6 10.0 copy-start.125
  18.7 10.1 copy-start.126
  24.0 658.3 %reduce-scatter.8.cloned.1.call-start = ((), (), s32[]{:S(2)}) async-start(), calls=%async_computation.10 | async-start | bytes 2162688 | tf_op jit(solution)/shard_map/reduce_scatter | solution.py:421
  26.8 9.3 copy-start.28
  26.8 9.3 copy-start.79
  27.5 9.8 copy-start.124
  28.7 113.5 %copy-start.109 = (f32[384]{0:T(512)}, f32[384]{0:T(512)S(1)}, u32[]{:S(2)}) copy-start(f32[384]{0:T(512)S(1)} %convert_element_type.367) | copy-start | bytes 4612
  142.2 66.2 %copy-start.135 = (f32[512]{0:T(512)}, f32[512]{0:T(512)S(1)}, u32[]{:S(2)}) copy-start(f32[512]{0:T(512)S(1)} %convert_reduce_fusion) | copy-start | bytes 6148
  211.0 150.7 %copy-start.107 = (f32[512]{0:T(512)}, f32[512]{0:T(512)S(1)}, u32[]{:S(2)}) copy-start(f32[512]{0:T(512)S(1)} %broadcast_multiply_fusion.6) | copy-start | bytes 6148
  211.4 150.3 %copy-start.111 = (f32[512]{0:T(512)}, f32[512]{0:T(512)S(1)}, u32[]{:S(2)}) copy-start(f32[512]{0:T(512)S(1)} %fusion.195) | copy-start | bytes 6148
  276.7 13.7 %copy-start.17 = (f32[512,768]{1,0:T(8,128)}, f32[512,768]{1,0:T(8,128)S(1)}, u32[]{:S(2)}) copy-start(f32[512,768]{1,0:T(8,128)S(1)} %get-tuple-element.138) | copy-start | bytes 4718596
  276.7 13.7 %copy-start.115 = (f32[512]{0:T(512)}, f32[512]{0:T(512)S(1)}, u32[]{:S(2)}) copy-start(f32[512]{0:T(512)S(1)} %broadcast_multiply_fusion.5) | copy-start | bytes 6148
  277.0 13.4 %copy-start.119 = (f32[512]{0:T(512)}, f32[512]{0:T(512)S(1)}, u32[]{:S(2)}) copy-start(f32[512]{0:T(512)S(1)} %fusion.196) | copy-start | bytes 6148
  295.8 68.8 %copy-start.117 = (f32[512]{0:T(512)}, f32[512]{0:T(512)S(1)}, u32[]{:S(2)}) copy-start(f32[512]{0:T(512)S(1)} %negate_multiply_fusion.3) | copy-start | bytes 6148
  316.1 13.3 %copy-start.108 = (f32[16,512]{1,0:T(8,128)S(1)}, f32[16,512]{1,0:T(8,128)}, u32[]{:S(2)}) copy-start(f32[16,512]{1,0:T(8,128)} %get-tuple-element.169) | copy-start | bytes 98308
  329.4 11.9 copy-start.49
  354.8 9.8 copy-start.36
  354.8 9.8 copy-start.39
  361.8 9.6 slice-start
  405.9 321.7 %reduce-scatter.10.cloned.1.call-start = ((), (), s32[]{:S(2)}) async-start(), calls=%async_computation.11 | async-start | bytes 8650752 | tf_op jit(solution)/shard_map/reduce_scatter | solution.py:417
  421.6 358.0 %all-reduce.5.cloned.1.call-start = ((), (), s32[]{:S(2)}) async-start(), calls=%async_computation.18 | async-start | bytes 1544192
  744.5 59.8 %reduce-scatter.16.cloned.1.call-start = ((), (), s32[]{:S(2)}) async-start(), calls=%async_computation.14 | async-start | bytes 1769472 | tf_op jit(solution)/shard_map/reduce_scatter | solution.py:448
  747.8 94.2 %reduce-scatter.20.cloned.1.call-start = ((), (), s32[]{:S(2)}) async-start(), calls=%async_computation.16 | async-start | bytes 3538944 | tf_op jit(solution)/shard_map/reduce_scatter | solution.py:448
  752.3 140.2 %reduce-scatter.12.cloned.1.call-start = ((), (), s32[]{:S(2)}) async-start(), calls=%async_computation.12 | async-start | bytes 5308416 | tf_op jit(solution)/shard_map/reduce_scatter | solution.py:448
  758.8 196.7 %reduce-scatter.18.cloned.1.call-start = ((), (), s32[]{:S(2)}) async-start(), calls=%async_computation.15 | async-start | bytes 7077888 | tf_op jit(solution)/shard_map/reduce_scatter | solution.py:448
  765.8 252.4 %reduce-scatter.14.cloned.1.call-start = ((), (), s32[]{:S(2)}) async-start(), calls=%async_computation.13 | async-start | bytes 7077888 | tf_op jit(solution)/shard_map/reduce_scatter | solution.py:448
  774.1 430.7 %all-reduce.7.cloned.1.call-start = ((), (), s32[]{:S(2)}) async-start(), calls=%async_computation.19 | async-start | bytes 18059264 | tf_op jit(solution)/shard_map/psum | solution.py:441
  1033.4 14.6 %all-to-all-start = ((bf16[2,256,768]{2,1,0:T(8,128)(2,1)}), bf16[2,256,768]{2,1,0:T(8,128)(2,1)}, u32[]{:S(2)}, u32[]{:S(2)}) async-start(bf16[2,256,768]{2,1,0:T(8,128)(2,1)} %bitcast.285), calls=%async_computation | async-start | bytes 1572864 | tf_op jit(solution)/shard_map/all_to_all | solution.py:453
  (128 other events, 388.2 us)
Sparse Core Ops, SparseCore 0:
  11.9 59.2 all-gather.5
  74.1 76.2 all-gather.3
  406.0 140.1 reduce-scatter.7
  548.4 179.0 reduce-scatter.9
  744.6 34.8 all-reduce.4
  782.2 22.0 reduce-scatter.15
  807.2 34.7 reduce-scatter.19
  844.8 47.6 reduce-scatter.11
  895.4 59.9 reduce-scatter.17
  958.2 59.9 reduce-scatter.13
  1024.0 180.7 all-reduce.6

commit v2 on v1

v2 whole, which is shorter than its diff:
```python
import functools

import jax
import jax.numpy as jnp
from jax import lax
from jax.experimental import pallas as pl
from jax.experimental.pallas import tpu as pltpu
from jax.sharding import PartitionSpec as P

EPS = 1e-05
LOWTYPE = jnp.bfloat16
WIDE = jnp.float32
ATOM_ROWS = 256
MEBI = 1024 * 1024


def takes(microseconds):
    return pl.CostEstimate(flops=0, transcendentals=0, bytes_accessed=int(microseconds * 3690000))

FAR = 4


def product(left, right):
    return jnp.dot(left, right, preferred_element_type=WIDE)


def product_left(left, right):
    return lax.dot_general(left, right, (((0,), (0,)), ((), ())), preferred_element_type=WIDE)


def product_right(left, right):
    return lax.dot_general(left, right, (((1,), (1,)), ((), ())), preferred_element_type=WIDE)


def sigmoid(values):
    return jax.nn.sigmoid(values)


def normalise(values):
    centre = values - jnp.mean(values, axis=-1, keepdims=True)
    scale = lax.rsqrt(jnp.mean(centre * centre, axis=-1, keepdims=True) + EPS)
    return centre * scale, scale


def normalise_back(grad, unit, scale):
    return scale * (
        grad
        - jnp.mean(grad, axis=-1, keepdims=True)
        - unit * jnp.mean(grad * unit, axis=-1, keepdims=True)
    )


def column_sum(values):
    return jnp.sum(values, axis=0, keepdims=True)


def low(values):
    return values.astype(LOWTYPE)


def wide(values):
    return values.astype(WIDE)


def head_masks(head_count, head_size, width, kind):
    lanes = lax.broadcasted_iota(jnp.int32, (1, width), 1)
    return [
        jnp.where((lanes >= h * head_size) & (lanes < (h + 1) * head_size), 1.0, 0.0).astype(kind)
        for h in range(head_count)
    ]


def full_spec(member):
    rank = len(member.shape)
    return pl.BlockSpec(member.shape, lambda *_: (0,) * rank)


def atom_forward_kernel(
    starts,
    place,
    features,
    single,
    token_rows,
    bias_own,
    bias_other,
    cond_gain,
    cond_weight,
    cond_bias,
    proj_weight,
    query_bias,
    out_weight,
    gu_weight,
    down_weight,
    gather_weight,
    pooled,
    counts,
    projections,
    attended,
    probability,
    key_wide,
    value_wide,
    pool_sum,
    count_sum,
):
    step = pl.program_id(0)
    blocks = pl.num_programs(0) // 2
    width = features.shape[1]
    _, _, half_group, head_count, span, keys = bias_own.shape
    group = 2 * half_group
    head_size = width // head_count
    factor = head_size**-0.5
    half = gu_weight.shape[1] // 2

    def conditioned(rows, first, last):
        unit, _ = normalise(wide(single[rows, :]))
        normed = low(unit * wide(cond_gain[...]))
        return product(normed, cond_weight[:, first:last]) + wide(cond_bias[:, first:last])

    @pl.when(step < blocks)
    def _():
        rows = pl.ds(pl.multiple_of(step * ATOM_ROWS, ATOM_ROWS), ATOM_ROWS)
        pieces = conditioned(rows, 0, 2 * width)
        unit, _ = normalise(wide(features[rows, :]))
        normed_one = low(unit * sigmoid(pieces[:, :width]) + pieces[:, width:])
        raw = product(normed_one, proj_weight[...])
        queries = low(raw[:, :width] + wide(query_bias[...]))
        rest = low(raw[:, width:])
        projections[rows, :width] = queries
        projections[rows, width:] = rest
        key_wide[rows, :] = wide(rest[:, :width])
        value_wide[rows, :] = wide(rest[:, width : 2 * width])

    @pl.when(step >= blocks)
    def _():
        block = step - blocks
        rows = pl.ds(pl.multiple_of(block * ATOM_ROWS, ATOM_ROWS), ATOM_ROWS)
        masks = head_masks(head_count, head_size, width, LOWTYPE)
        wide_masks = head_masks(head_count, head_size, width, WIDE)
        query_rows = projections[rows, :width]
        parts = []
        for u in range(group):
            start = starts[block * group + u]
            key_win = low(key_wide[pl.ds(start, keys), :])
            value_win = low(value_wide[pl.ds(start, keys), :])
            query_win = query_rows[u * span : (u + 1) * span]
            stacked = jnp.concatenate([query_win * mask for mask in masks], axis=0)
            scores = product_right(stacked, key_win) * factor
            own, other = bias_own[0, 0, u % half_group], bias_other[0, 0, u % half_group]
            bias = jnp.where(place[3] == u // half_group, own, other)
            scores = scores + wide(bias.reshape(head_count * span, keys))
            exponent = jnp.exp(scores - jnp.max(scores, axis=-1, keepdims=True))
            chance = low(exponent / jnp.sum(exponent, axis=-1, keepdims=True))
            probability[u] = chance
            mixed = product(chance, value_win)
            parts.append(
                sum(mixed[h * span : (h + 1) * span] * wide_masks[h] for h in range(head_count))
            )
        mixed = jnp.concatenate(parts, axis=0)
        attended[rows, :] = mixed
        gated = low(mixed * sigmoid(wide(projections[rows, 3 * width :])))
        pieces = conditioned(rows, 2 * width, 6 * width)
        middle = wide(features[rows, :]) + sigmoid(pieces[:, :width]) * product(
            gated, out_weight[...]
        )
        unit, _ = normalise(middle)
        normed_two = low(
            unit * sigmoid(pieces[:, width : 2 * width]) + pieces[:, 2 * width : 3 * width]
        )
        gate_up = product(normed_two, gu_weight[...])
        gate_half = gate_up[:, :half]
        hidden = low(gate_half * sigmoid(gate_half) * gate_up[:, half:])
        result = low(middle + sigmoid(pieces[:, 3 * width :]) * product(hidden, down_weight[...]))
        pre_act = product(result, gather_weight[...])
        pooled_atoms = low(pre_act * sigmoid(pre_act))
        token_ids = token_rows[block]
        tokens = lax.broadcasted_iota(jnp.int32, (pooled.shape[0], ATOM_ROWS), 0)
        onehot = jnp.where(tokens == token_ids, 1.0, 0.0)
        part = product(low(onehot), pooled_atoms)
        part_count = jnp.sum(onehot, axis=1, keepdims=True)

        @pl.when(block == 0)
        def _():
            pool_sum[...] = part
            count_sum[...] = part_count

        @pl.when(block > 0)
        def _():
            pool_sum[...] += part
            count_sum[...] += part_count

        @pl.when(block == blocks - 1)
        def _():
            counts[...] = count_sum[...]
            pooled[...] = low(pool_sum[...] / count_sum[...])


def far_at(run, place):
    distance = run ^ place[1]
    return distance % 2 * 2 + distance // 2


def block_of(step, place):
    return step % 2 ^ place[2], far_at(step // 2, place)


def atom_forward(
    starts, place, features, single, atom_token, bias, weights, gather_weight, length
):
    atoms, width = features.shape
    blocks = atoms // ATOM_ROWS
    _, _, half_group, head_count, span, keys = bias[0].shape
    windows = 2 * half_group * blocks
    model_width = gather_weight.shape[1]
    token_rows = atom_token.reshape(blocks, 1, ATOM_ROWS)
    flat = [member[None] if member.ndim == 1 else member for member in weights]
    whole = [features, single, token_rows]

    def bias_block(i, starts, place):
        near, far = block_of(jnp.maximum(i - blocks, 0), place)
        return near, far, 0, 0, 0, 0

    later3 = lambda i, *_: (jnp.maximum(i - blocks, 0), 0, 0)
    outs = [
        jax.ShapeDtypeStruct((length, model_width), LOWTYPE),
        jax.ShapeDtypeStruct((length, 1), WIDE),
        jax.ShapeDtypeStruct((atoms, 4 * width), LOWTYPE),
        jax.ShapeDtypeStruct((atoms, width), WIDE),
        jax.ShapeDtypeStruct((windows, head_count * span, keys), LOWTYPE),
    ]
    return pl.pallas_call(
        atom_forward_kernel,
        grid_spec=pltpu.PrefetchScalarGridSpec(
            num_scalar_prefetch=2,
            grid=(2 * blocks,),
            in_specs=[full_spec(member) for member in whole]
            + [pl.BlockSpec((1, 1, half_group, head_count, span, keys), bias_block)] * 2
            + [full_spec(member) for member in flat + [gather_weight]],
            out_specs=[full_spec(member) for member in outs[:4]]
            + [pl.BlockSpec((2 * half_group, head_count * span, keys), later3)],
            scratch_shapes=[
                pltpu.VMEM((atoms, width), WIDE),
                pltpu.VMEM((atoms, width), WIDE),
                pltpu.VMEM((length, model_width), WIDE),
                pltpu.VMEM((length, 1), WIDE),
            ],
        ),
        out_shape=outs,
        cost_estimate=takes(40),
        compiler_params=pltpu.CompilerParams(
            dimension_semantics=("arbitrary",), vmem_limit_bytes=48 * MEBI
        ),
        name="atom_forward",
    )(starts, place, *whole, *bias, *flat, gather_weight)


def atom_tokens_back_kernel(
    features,
    single,
    token_cols,
    gates,
    attended,
    d_tokens,
    counts,
    cond_gain,
    cond_weight,
    cond_bias,
    out_weight,
    gu_weight,
    down_weight,
    gather_weight,
    d_attended,
    d_gates,
    d_middles,
    d_pieces,
    packed,
    grad_out,
    grad_gu,
    grad_down,
    grad_gather,
):
    step = pl.program_id(0)
    blocks = pl.num_programs(0)
    width = features.shape[1]
    half = gu_weight.shape[1] // 2

    @pl.when(step == 0)
    def _():
        for member in (grad_out, grad_gu, grad_down, grad_gather):
            member[...] = jnp.zeros_like(member)

    rows = slice(None)
    unit, _ = normalise(wide(single[rows, :]))
    normed = low(unit * wide(cond_gain[...]))
    pieces = product(normed, cond_weight[:, 2 * width :]) + wide(cond_bias[:, 2 * width :])
    mixed = attended[rows, :]
    gate = sigmoid(wide(gates[rows, :]))
    gated = low(mixed * gate)
    attn_out = product(gated, out_weight[...])
    gate_one = sigmoid(pieces[:, :width])
    middle = wide(features[rows, :]) + gate_one * attn_out
    unit_two, spread_two = normalise(middle)
    scale_two = sigmoid(pieces[:, width : 2 * width])
    normed_two = low(unit_two * scale_two + pieces[:, 2 * width : 3 * width])
    gate_up = product(normed_two, gu_weight[...])
    gate_half, up_half = gate_up[:, :half], gate_up[:, half:]
    logistic = sigmoid(gate_half)
    hidden = low(gate_half * logistic * up_half)
    down_out = product(hidden, down_weight[...])
    gate_two = sigmoid(pieces[:, 3 * width :])
    result = low(middle + gate_two * down_out)
    pre_act = product(result, gather_weight[...])

    d_scaled = low(wide(d_tokens[...]) / counts[...])
    tokens = lax.broadcasted_iota(jnp.int32, (ATOM_ROWS, d_tokens.shape[0]), 1)
    onehot = low(jnp.where(tokens == token_cols[...], 1.0, 0.0))
    d_rows = product(onehot, d_scaled)
    pre_logistic = sigmoid(pre_act)
    d_pre = low(d_rows * (pre_logistic * (1.0 + pre_act * (1.0 - pre_logistic))))
    grad_gather[...] += product_left(result, d_pre)
    d_result = product_right(d_pre, gather_weight[...])

    d_down = low(d_result * gate_two)
    d_pieces[rows, 3 * width :] = low(d_result * down_out * gate_two * (1.0 - gate_two))
    grad_down[...] += product_left(hidden, d_down)
    d_hidden = wide(low(product_right(d_down, down_weight[...])))
    d_gate_half = low(d_hidden * up_half * logistic * (1.0 + gate_half * (1.0 - logistic)))
    d_up_half = low(d_hidden * gate_half * logistic)
    d_gate_up = jnp.concatenate([d_gate_half, d_up_half], axis=1)
    grad_gu[...] += product_left(normed_two, d_gate_up)
    d_normed_two = product_right(d_gate_up, gu_weight[...])
    d_pieces[rows, 2 * width : 3 * width] = low(d_normed_two)
    d_pieces[rows, width : 2 * width] = low(
        d_normed_two * unit_two * scale_two * (1.0 - scale_two)
    )
    d_middle = d_result + normalise_back(d_normed_two * scale_two, unit_two, spread_two)
    d_middles[rows, :] = d_middle
    d_attn_out = low(d_middle * gate_one)
    d_pieces[rows, :width] = low(
        d_middle * attn_out * gate_one * (1.0 - gate_one)
    )
    grad_out[...] += product_left(gated, d_attn_out)
    d_gated = wide(low(product_right(d_attn_out, out_weight[...])))
    d_attended[rows, :] = low(d_gated * gate)
    d_gates[rows, :] = low(d_gated * mixed * gate * (1.0 - gate))

    @pl.when(step == blocks - 1)
    def _():
        model_width = gather_weight.shape[1]
        packed[:, :model_width] = low(grad_gather[...])
        last = model_width + 2 * half
        packed[:, model_width:last] = low(grad_gu[...])
        packed[:, last : last + width] = low(grad_out[...])
        last = last + width
        run = grad_down.shape[0] // 4
        for part in range(4):
            rows_at = slice(part // 2 * run, (part // 2 + 1) * run)
            columns = slice(last + part % 2 * width, last + (part % 2 + 1) * width)
            packed[rows_at, columns] = low(grad_down[part * run : (part + 1) * run, :])


def atom_attention_back_kernel(
    starts,
    place,
    projections,
    attended,
    probability,
    d_attended,
    d_projections,
    d_bias_own,
    d_bias_other,
    key_wide,
    value_wide,
    d_keys,
    d_values,
):
    step = pl.program_id(0)
    blocks = pl.num_programs(0)
    width = attended.shape[1]
    group, stack, keys = probability.shape
    half_group = group // 2
    span = ATOM_ROWS // group
    head_count = stack // span
    head_size = width // head_count
    factor = head_size**-0.5

    @pl.when(step == 0)
    def _():
        for member in (d_keys, d_values):
            member[...] = jnp.zeros_like(member)
        key_wide[...] = wide(projections[:, width : 2 * width])
        value_wide[...] = wide(projections[:, 2 * width : 3 * width])

    rows = pl.ds(pl.multiple_of(step * ATOM_ROWS, ATOM_ROWS), ATOM_ROWS)
    row_grad = d_attended[...]
    row_part = wide(row_grad) * attended[...]

    masks = head_masks(head_count, head_size, width, LOWTYPE)
    wide_masks = head_masks(head_count, head_size, width, WIDE)
    query_rows = projections[rows, :width]
    score_grads, query_grads = [], []
    for u in range(group):
        start = starts[step * group + u]
        cut = slice(u * span, (u + 1) * span)
        key_win = low(key_wide[pl.ds(start, keys), :])
        value_win = low(value_wide[pl.ds(start, keys), :])
        stacked_query = jnp.concatenate([query_rows[cut] * mask for mask in masks], axis=0)
        stacked_grad = jnp.concatenate([row_grad[cut] * mask for mask in masks], axis=0)
        stacked_part = jnp.concatenate([row_part[cut] * mask for mask in wide_masks], axis=0)
        row_sum = jnp.sum(stacked_part, axis=-1, keepdims=True)
        chance = probability[u]
        d_chance = product_right(stacked_grad, value_win)
        d_scores = low(wide(chance) * (d_chance - row_sum))
        score_grads.append(d_scores)
        d_stacked = product(d_scores, key_win) * factor
        query_grads.append(
            sum(d_stacked[h * span : (h + 1) * span] * wide_masks[h] for h in range(head_count))
        )
        d_keys[pl.ds(start, keys), :] += product_left(d_scores, stacked_query) * factor
        d_values[pl.ds(start, keys), :] += product_left(chance, stacked_grad)
    d_projections[rows, :width] = low(jnp.concatenate(query_grads, axis=0))
    for u in range(half_group):
        first = place[3] == 0
        d_bias_own[0, 0, u] = jnp.where(first, score_grads[u], score_grads[u + half_group])
        d_bias_other[0, 0, u] = jnp.where(first, score_grads[u + half_group], score_grads[u])

    @pl.when(step == blocks - 1)
    def _():
        d_projections[:, width : 2 * width] = low(d_keys[...])
        d_projections[:, 2 * width : 3 * width] = low(d_values[...])


def atom_features_back_kernel(
    features,
    single,
    d_projections,
    d_gates,
    d_middles,
    d_pieces,
    cond_gain,
    cond_weight,
    cond_bias,
    proj_weight,
    d_features,
    packed,
    grad_gain,
    grad_offset,
    grad_query,
    grad_cond,
    grad_proj,
):
    step = pl.program_id(0)
    blocks = pl.num_programs(0)
    width = features.shape[1]

    @pl.when(step == 0)
    def _():
        for member in (grad_gain, grad_offset, grad_query, grad_cond, grad_proj):
            member[...] = jnp.zeros_like(member)

    unit, _ = normalise(wide(single[...]))
    normed = low(unit * wide(cond_gain[...]))
    pieces = product(normed, cond_weight[:, : 2 * width]) + wide(cond_bias[:, : 2 * width])
    unit_one, spread_one = normalise(wide(features[...]))
    scale_one = sigmoid(pieces[:, :width])
    normed_one = low(unit_one * scale_one + pieces[:, width:])
    d_projection = jnp.concatenate([d_projections[...], d_gates[...]], axis=1)
    grad_proj[...] += product_left(normed_one, d_projection)
    grad_query[...] += column_sum(wide(d_projection[:, :width]))
    d_normed_one = product_right(d_projection, proj_weight[...])
    d_features[...] = d_middles[...] + normalise_back(
        d_normed_one * scale_one, unit_one, spread_one
    )
    d_projected = jnp.concatenate(
        [
            low(d_normed_one * unit_one * scale_one * (1.0 - scale_one)),
            low(d_normed_one),
            d_pieces[...],
        ],
        axis=1,
    )
    grad_cond[...] += product_left(normed, d_projected)
    grad_offset[...] += column_sum(wide(d_projected))
    d_normed = product_right(d_projected, cond_weight[...])
    grad_gain[...] += column_sum(d_normed * unit)

    @pl.when(step == blocks - 1)
    def _():
        packed[:, : 6 * width] = low(grad_cond[...])
        packed[:, 6 * width :] = low(grad_proj[...])


def atom_tokens_back(features, single, atom_token, d_tokens, counts, stored, weights, gather_weight):
    projections, attended, _ = stored
    atoms, width = features.shape
    gain, cond, offset, _, _, out, gu, down = weights
    flat = [gain[None], cond, offset[None], out, gu, down, gather_weight]
    token_cols = atom_token.reshape(atoms, 1)
    columns = gather_weight.shape[1] + gu.shape[1] + 3 * width
    outs = [
        jax.ShapeDtypeStruct((atoms, width), LOWTYPE),
        jax.ShapeDtypeStruct((atoms, width), LOWTYPE),
        jax.ShapeDtypeStruct((atoms, width), WIDE),
        jax.ShapeDtypeStruct((atoms, 4 * width), LOWTYPE),
        jax.ShapeDtypeStruct((width, columns), LOWTYPE),
    ]

    def rows_of(member):
        return pl.BlockSpec((ATOM_ROWS, member.shape[1]), lambda i: (i, 0))

    return pl.pallas_call(
        atom_tokens_back_kernel,
        grid=(atoms // ATOM_ROWS,),
        in_specs=[
            rows_of(features),
            rows_of(single),
            rows_of(token_cols),
            pl.BlockSpec((ATOM_ROWS, width), lambda i: (i, 3)),
            rows_of(attended),
            full_spec(d_tokens),
            full_spec(counts),
        ]
        + [full_spec(member) for member in flat],
        out_specs=[rows_of(member) for member in outs[:4]] + [full_spec(outs[4])],
        out_shape=outs,
        scratch_shapes=[
            pltpu.VMEM(member.shape, WIDE) for member in (out, gu, down, gather_weight)
        ],
        cost_estimate=takes(3),
        compiler_params=pltpu.CompilerParams(
            dimension_semantics=("arbitrary",), vmem_limit_bytes=48 * MEBI
        ),
        name="atom_tokens_back",
    )(features, single, token_cols, projections, attended, d_tokens, counts, *flat)


def atom_attention_back(starts, place, d_attended, stored):
    projections, attended, probability = stored
    atoms, width = attended.shape
    blocks = atoms // ATOM_ROWS
    windows, stack, keys = probability.shape
    group = windows // blocks
    score_shape = (2, blocks // 2, group // 2, stack, keys)
    outs = [
        jax.ShapeDtypeStruct((atoms, 3 * width), LOWTYPE),
        jax.ShapeDtypeStruct(score_shape, LOWTYPE),
        jax.ShapeDtypeStruct(score_shape, LOWTYPE),
    ]

    def bias_block(i, starts, place):
        near, far = block_of(i, place)
        return near, far, 0, 0, 0

    block = pl.BlockSpec((ATOM_ROWS, width), lambda i, *_: (i, 0))
    return pl.pallas_call(
        atom_attention_back_kernel,
        grid_spec=pltpu.PrefetchScalarGridSpec(
            num_scalar_prefetch=2,
            grid=(blocks,),
            in_specs=[
                full_spec(projections),
                block,
                pl.BlockSpec((group, stack, keys), lambda i, *_: (i, 0, 0)),
                block,
            ],
            out_specs=[full_spec(outs[0])]
            + [pl.BlockSpec((1, 1, group // 2, stack, keys), bias_block)] * 2,
            scratch_shapes=[pltpu.VMEM((atoms, width), WIDE)] * 4,
        ),
        out_shape=outs,
        cost_estimate=takes(2),
        compiler_params=pltpu.CompilerParams(
            dimension_semantics=("arbitrary",), vmem_limit_bytes=48 * MEBI
        ),
        name="atom_attention_back",
    )(starts, place, projections, attended, probability, d_attended)


def atom_features_back(features, single, d_projections, d_gates, d_middles, d_pieces, weights):
    atoms, width = features.shape
    gain, cond, offset, proj = weights[:4]
    flat = [gain[None], cond, offset[None], proj]
    rows = [features, single, d_projections, d_gates, d_middles, d_pieces]
    outs = [
        jax.ShapeDtypeStruct((atoms, width), WIDE),
        jax.ShapeDtypeStruct((width, 10 * width), LOWTYPE),
        jax.ShapeDtypeStruct((1, width), WIDE),
        jax.ShapeDtypeStruct((1, 6 * width), WIDE),
        jax.ShapeDtypeStruct((1, width), WIDE),
    ]
    return pl.pallas_call(
        atom_features_back_kernel,
        grid=(atoms // ATOM_ROWS,),
        in_specs=[
            pl.BlockSpec((ATOM_ROWS, member.shape[1]), lambda i: (i, 0)) for member in rows
        ]
        + [full_spec(member) for member in flat],
        out_specs=[pl.BlockSpec((ATOM_ROWS, width), lambda i: (i, 0))]
        + [full_spec(member) for member in outs[1:]],
        out_shape=outs,
        scratch_shapes=[pltpu.VMEM(cond.shape, WIDE), pltpu.VMEM(proj.shape, WIDE)],
        cost_estimate=takes(0.5),
        compiler_params=pltpu.CompilerParams(
            dimension_semantics=("arbitrary",), vmem_limit_bytes=32 * MEBI
        ),
        name="atom_features_back",
    )(*rows, *flat)


LANES = 128
GROUP_HEADS = 8


def head_window(head, head_size, total):
    first = min(head * head_size // LANES * LANES, total - 2 * LANES)
    return first, head * head_size - first


def head_lanes(offset, head_size, kind):
    lanes = lax.broadcasted_iota(jnp.int32, (1, 2 * LANES), 1)
    return jnp.where((lanes >= offset) & (lanes < offset + head_size), 1.0, 0.0).astype(kind)


def chosen_rows(place, own, other, head):
    parts = []
    for near in range(2):
        for core in range(2):
            for section in range(2):
                at = (near ^ place[2], section ^ place[0])
                parts.append(
                    jnp.where(place[3] == core, own[(*at, 0, head)], other[(*at, 0, head)])
                )
    return jnp.concatenate(parts, axis=0)


def token_forward_kernel(
    place, queries, keys, values, gates, own_a, other_a, own_b, other_b, probability, attended, gated
):
    heads = probability.shape[0]
    rows, total = queries.shape
    head_size = total // heads
    factor = head_size**-0.5

    def attend(own, other):
        tiles = [None] * (total // LANES)
        for h in range(heads):
            first, offset = head_window(h, head_size, total)
            cut = slice(first, first + 2 * LANES)
            mask = head_lanes(offset, head_size, LOWTYPE)
            scores = product_right(queries[:, cut] * mask, keys[:, cut]) * factor
            scores = scores + wide(chosen_rows(place, own, other, h))
            exponent = jnp.exp(scores - jnp.max(scores, axis=-1, keepdims=True))
            chance = low(exponent * (1.0 / jnp.sum(exponent, axis=-1, keepdims=True)))
            probability[h] = chance
            mixed = product(chance, values[:, cut]) * wide(mask)
            for t in range(2):
                at = first // LANES + t
                part = mixed[:, t * LANES : (t + 1) * LANES]
                tiles[at] = part if tiles[at] is None else tiles[at] + part
        whole = jnp.concatenate(tiles, axis=1)
        attended[...] = whole
        gated[...] = low(whole * sigmoid(wide(gates[...])))

    @pl.when(pl.program_id(0) == 0)
    def _():
        attend(own_a, other_a)

    @pl.when(pl.program_id(0) == 1)
    def _():
        attend(own_b, other_b)


def bias_spec(member, group):
    shape = member.shape
    resting = 0 if group else FAR - 1

    def index(g, i, place):
        run = jnp.where(g == group, i, resting)
        return 0, 0, far_at(run, place), 0, 0, 0

    return pl.BlockSpec((*shape[:2], 1, *shape[3:]), index)


def token_forward(place, projections, bias):
    length, columns = projections.shape
    width = columns // 4
    rows = length // FAR
    group_heads = bias[0].shape[3]
    groups = len(bias) // 2
    heads = group_heads * groups
    total = width // groups
    block = pl.BlockSpec((rows, total), lambda g, i, _: (i, g))
    return pl.pallas_call(
        token_forward_kernel,
        grid_spec=pltpu.PrefetchScalarGridSpec(
            num_scalar_prefetch=1,
            grid=(groups, FAR),
            in_specs=[
                block,
                pl.BlockSpec((length, total), lambda g, i, _: (0, groups + g)),
                pl.BlockSpec((length, total), lambda g, i, _: (0, 2 * groups + g)),
                pl.BlockSpec((rows, total), lambda g, i, _: (i, 3 * groups + g)),
            ]
            + [bias_spec(member, index // 2) for index, member in enumerate(bias)],
            out_specs=[
                pl.BlockSpec((group_heads, rows, length), lambda g, i, _: (g, i, 0)),
                block,
                block,
            ],
        ),
        out_shape=[
            jax.ShapeDtypeStruct((heads, length, length), LOWTYPE),
            jax.ShapeDtypeStruct((length, width), WIDE),
            jax.ShapeDtypeStruct((length, width), LOWTYPE),
        ],
        cost_estimate=takes(31),
        compiler_params=pltpu.CompilerParams(
            dimension_semantics=("arbitrary", "arbitrary"), vmem_limit_bytes=48 * MEBI
        ),
        name="token_forward",
    )(place, projections, projections, projections, projections, *bias)


def token_backward_kernel(
    place,
    queries,
    keys,
    values,
    gates,
    probability,
    attended,
    d_gated,
    own,
    other,
    d_projections,
    d_keys,
    d_values,
):
    group, step = pl.program_id(0), pl.program_id(1)
    heads = probability.shape[0]
    rows, total = queries.shape
    head_size = total // heads
    factor = head_size**-0.5
    width = d_projections.shape[1] // 4
    run = own.shape[4]

    @pl.when(step == 0)
    def _():
        d_keys[...] = jnp.zeros_like(d_keys)
        d_values[...] = jnp.zeros_like(d_values)

    gate = sigmoid(wide(gates[...]))
    grad = wide(d_gated[...])
    mixed = attended[...]
    d_attended = low(grad * gate)
    d_gates = low(grad * mixed * gate * (1.0 - gate))
    row_part = wide(d_attended) * mixed
    tiles = [None] * (total // LANES)
    for h in range(heads):
        first, offset = head_window(h, head_size, total)
        cut = slice(first, first + 2 * LANES)
        mask = head_lanes(offset, head_size, LOWTYPE)
        row_sum = jnp.sum(row_part[:, cut] * wide(mask), axis=-1, keepdims=True)
        head_grad = d_attended[:, cut] * mask
        chance = probability[h]
        d_scores = low(wide(chance) * (product_right(head_grad, values[:, cut]) - row_sum))
        for near in range(2):
            for section in range(2):
                at = (near ^ place[2], section ^ place[0], 0, h)
                pair = []
                for core in range(2):
                    start = (4 * near + 2 * core + section) * run
                    pair.append(d_scores[start : start + run])
                own[at] = jnp.where(place[3] == 0, pair[0], pair[1])
                other[at] = jnp.where(place[3] == 0, pair[1], pair[0])
        part = product(d_scores, keys[:, cut]) * (wide(mask) * factor)
        for t in range(2):
            at = first // LANES + t
            piece = part[:, t * LANES : (t + 1) * LANES]
            tiles[at] = piece if tiles[at] is None else tiles[at] + piece
        d_keys[:, cut] += product_left(d_scores, queries[:, cut] * mask)
        d_values[:, cut] += product_left(chance, head_grad)
    rows_at = pl.ds(pl.multiple_of(step * rows, rows), rows)
    first = group * total
    d_projections[rows_at, pl.ds(pl.multiple_of(first, LANES), total)] = low(
        jnp.concatenate(tiles, axis=1)
    )
    gates_at = pl.ds(pl.multiple_of(first + 3 * width, LANES), total)
    d_projections[rows_at, gates_at] = d_gates

    @pl.when(step == pl.num_programs(1) - 1)
    def _():
        first = group * total
        d_projections[:, pl.ds(pl.multiple_of(first + width, LANES), total)] = low(
            d_keys[...] * factor
        )
        d_projections[:, pl.ds(pl.multiple_of(first + 2 * width, LANES), total)] = low(
            d_values[...]
        )


def token_backward(place, projections, probability, attended, d_gated, run):
    length, columns = projections.shape
    width = columns // 4
    rows = length // FAR
    heads = probability.shape[0]
    groups = heads // GROUP_HEADS
    total = width // groups
    block = pl.BlockSpec((rows, total), lambda g, i, _: (i, g))
    grad = jax.ShapeDtypeStruct((2, 2, FAR, heads, run, length), LOWTYPE)
    grad_spec = pl.BlockSpec(
        (2, 2, 1, GROUP_HEADS, run, length), lambda g, i, place: (0, 0, far_at(i, place), g, 0, 0)
    )
    return pl.pallas_call(
        token_backward_kernel,
        grid_spec=pltpu.PrefetchScalarGridSpec(
            num_scalar_prefetch=1,
            grid=(groups, FAR),
            in_specs=[
                block,
                pl.BlockSpec((length, total), lambda g, i, _: (0, groups + g)),
                pl.BlockSpec((length, total), lambda g, i, _: (0, 2 * groups + g)),
                pl.BlockSpec((rows, total), lambda g, i, _: (i, 3 * groups + g)),
                pl.BlockSpec((GROUP_HEADS, rows, length), lambda g, i, _: (g, i, 0)),
                block,
                block,
            ],
            out_specs=[grad_spec] * 2
            + [pl.BlockSpec((length, columns), lambda g, i, _: (0, 0))],
            scratch_shapes=[pltpu.VMEM((length, total), WIDE)] * 2,
        ),
        out_shape=[grad] * 2 + [jax.ShapeDtypeStruct((length, columns), LOWTYPE)],
        cost_estimate=takes(8),
        compiler_params=pltpu.CompilerParams(
            dimension_semantics=("arbitrary", "arbitrary"), vmem_limit_bytes=48 * MEBI
        ),
        name="token_backward",
    )(place, projections, projections, projections, projections, probability, attended, d_gated)


PIECES = 8
COLUMNS = 384


def places():
    place = lax.axis_index("dp")
    return lax.axis_index("section"), place // 4, place // 2 % 2, place % 2


def swap_section(member):
    return lax.ppermute(member, "section", [(0, 1), (1, 0)])


def swap_bit(member, bit):
    return lax.ppermute(member, "dp", [(i, i ^ (1 << bit)) for i in range(lax.axis_size("dp"))])


def swap_core(member):
    return swap_bit(member, 0)


def swap_near(member):
    return swap_bit(member, 1)


def swap_far(member, bit):
    return swap_bit(member, 2 + bit)


def more_bits():
    return range(4, (lax.axis_size("dp") - 1).bit_length())


def piece_index():
    place = lax.axis_index("dp")
    return place // 2 % 2 * 4 + place // 4 % 2 * 2 + place // 8 % 2


def run_of(member, index, count):
    rows = member.shape[0] // count
    return lax.dynamic_slice_in_dim(member, index * rows, rows, 0)


def add_low(*members):
    return low(sum(wide(member) for member in members))


def scatter_plane(member):
    for bit, half in ((2, 2), (3, 1)):
        member = add_low(member[:half], swap_bit(member[half:], bit))
    for bit in more_bits():
        member = add_low(member, swap_bit(member, bit))
    return member


def rest_sum(*members):
    total = add_low(*members)
    for bit in more_bits():
        total = add_low(total, swap_bit(total, bit))
    return total


def from_here(member):
    half = member.shape[1] // 2
    first, second = member[:, :half], member[:, half:]
    turned = jnp.concatenate([second, first], axis=1)
    return jnp.where(lax.axis_index("section") == 0, member, turned)


def gather_pieces(member):
    for bit in (3, 2, 1):
        member = jnp.concatenate([member, swap_bit(member, bit)], axis=0)
    return member


class Weight:
    def __init__(self, rows, columns):
        self.rows, self.columns = rows // 2, columns
        self.blocks = columns // 2 // COLUMNS
        self.run = self.blocks * self.rows // PIECES

    def segments(self, piece):
        at, last, found = piece * self.run, (piece + 1) * self.run, []
        while at < last:
            block, row = divmod(at, self.rows)
            size = min(self.rows - row, last - at)
            found.append((block, row, size, at - piece * self.run))
            at += size
        return found


def aligned(start, size, step):
    return pl.ds(pl.multiple_of(start, step), size)


def product_blocks(place, weights, members, core, half):
    found, at = [], 0
    for weight in weights:
        if weight.direct:
            held = members[at]
            at += 1
        else:
            left, right = members[at], members[at + 1]
            at += 2
            if weight.rows % LANES:
                side = left[:, half * weight.rows : (half + 1) * weight.rows]
            else:
                side = left[:, aligned((half ^ place[0]) * weight.rows, weight.rows, LANES)]
        blocks = []
        for block in range(weight.blocks):
            columns = aligned(
                core * (weight.columns // 2) + block * COLUMNS, COLUMNS, LANES
            )
            if weight.direct:
                rows = aligned((half ^ place[0]) * weight.rows, weight.rows, 16)
                blocks.append(wide(held[rows, columns]))
            else:
                blocks.append(product_left(side, right[:, columns]))
        found.append(blocks)
    return found


def store_pieces(place, weights, found, store):
    for piece in range(PIECES):
        at = 0
        for weight, blocks in zip(weights, found):
            for block, row, size, offset in weight.segments(piece):
                store(piece ^ place[4], slice(at + offset, at + offset + size), blocks[block][row : row + size])
            at += weight.run


def given_kernel(weights, place, *refs):
    *members, out = refs
    for half in range(2):

        @pl.when(pl.program_id(0) == half)
        def _(half=half):
            def store(piece, rows, values):
                out[0, piece, rows, :] = low(values)

            store_pieces(
                place, weights, product_blocks(place, weights, members, 1 - place[3], half), store
            )


def kept_kernel(weights, place, *refs):
    *members, received, given, kept = refs
    for step, (half, target) in enumerate(((1, given), (0, kept))):

        @pl.when(pl.program_id(0) == step)
        def _(half=half, target=target):
            def store(piece, rows, values):
                target[piece, rows, :] = low(values + wide(received[0, piece, rows, :]))

            store_pieces(
                place, weights, product_blocks(place, weights, members, place[3], half), store
            )


def chunk_rows(weights):
    return sum(weight.run for weight in weights)


def chunk_given(place, weights, members):
    block = (1, PIECES, chunk_rows(weights), COLUMNS)
    return pl.pallas_call(
        functools.partial(given_kernel, weights),
        grid_spec=pltpu.PrefetchScalarGridSpec(
            num_scalar_prefetch=1,
            grid=(2,),
            in_specs=[full_spec(member) for member in members],
            out_specs=pl.BlockSpec(block, lambda i, _: (i, 0, 0, 0)),
        ),
        out_shape=jax.ShapeDtypeStruct((2, *block[1:]), LOWTYPE),
        cost_estimate=takes(15),
        compiler_params=pltpu.CompilerParams(
            dimension_semantics=("arbitrary",), vmem_limit_bytes=48 * MEBI
        ),
        name="chunk_given",
    )(place, *members)


def chunk_kept(place, weights, members, received):
    block = (1, PIECES, chunk_rows(weights), COLUMNS)
    out = jax.ShapeDtypeStruct(block[1:], LOWTYPE)
    return pl.pallas_call(
        functools.partial(kept_kernel, weights),
        grid_spec=pltpu.PrefetchScalarGridSpec(
            num_scalar_prefetch=1,
            grid=(2,),
            in_specs=[full_spec(member) for member in members]
            + [pl.BlockSpec(block, lambda i, _: (1 - i, 0, 0, 0))],
            out_specs=[full_spec(out), full_spec(out)],
        ),
        out_shape=[out, out],
        cost_estimate=takes(20),
        compiler_params=pltpu.CompilerParams(
            dimension_semantics=("arbitrary",), vmem_limit_bytes=48 * MEBI
        ),
        name="chunk_kept",
    )(place, *members, received)


def assemble_kernel(weights, place, own, other, *outs):
    for source, core in ((own, place[3]), (other, 1 - place[3])):
        for piece in range(PIECES):
            at = 0
            for weight, out in zip(weights, outs):
                for block, row, size, offset in weight.segments(piece):
                    columns = aligned(
                        core * (weight.columns // 2) + block * COLUMNS, COLUMNS, LANES
                    )
                    rows = slice(at + offset, at + offset + size)
                    out[row : row + size, columns] = wide(source[piece ^ place[4], rows, :])
                at += weight.run


def assemble(place, weights, own, other):
    outs = [jax.ShapeDtypeStruct((weight.rows, weight.columns), WIDE) for weight in weights]
    return pl.pallas_call(
        functools.partial(assemble_kernel, weights),
        grid_spec=pltpu.PrefetchScalarGridSpec(
            num_scalar_prefetch=1,
            grid=(1,),
            in_specs=[full_spec(own), full_spec(other)],
            out_specs=[full_spec(member) for member in outs],
        ),
        out_shape=outs,
        cost_estimate=takes(2),
        compiler_params=pltpu.CompilerParams(
            dimension_semantics=("arbitrary",), vmem_limit_bytes=48 * MEBI
        ),
        name="assemble",
    )(place, own, other)


def products(*shapes):
    weights = [Weight(*shape) for shape in shapes]
    for weight in weights:
        weight.direct = False
    return weights


def vector_sum(member):
    section = lax.axis_index("section")
    kept = lax.dynamic_index_in_dim(member, section, 0, keepdims=False)
    total = kept + swap_section(lax.dynamic_index_in_dim(member, 1 - section, 0, keepdims=False))
    for bit in range((lax.axis_size("dp") - 1).bit_length()):
        total = total + swap_bit(total, bit)
    return total


def half_block(shape, count=2):
    axis = len(shape) - 2
    if shape[axis] % (16 * count):
        axis -= 1
    block = list(shape)
    block[axis] //= count
    return pl.BlockSpec(tuple(block), lambda i: tuple(i if a == axis else 0 for a in range(len(shape))))


def exchange_kernel(entries, *refs):
    refs = list(refs)
    members = [[refs.pop(0) for _ in range(1 + count)] for _, count in entries]
    for (axis, _), (kept, *got) in zip(entries, members):
        if axis == "join":
            out = refs.pop(0)
            rows = kept.shape[0]
            for index, member in enumerate([kept, *got]):
                out[index * rows : (index + 1) * rows] = member[...]
        elif axis == "far":
            rows = got[0].shape[0]
            refs.pop(0)[...] = low(
                wide(kept[:rows]) + wide(got[0][...]) + wide(got[1][...]) + wide(got[2][...])
            )
        elif axis is None:
            refs.pop(0)[...] = low(wide(kept[...]) + wide(got[0][...]))
        else:
            for side in range(2):
                at = (slice(None),) * axis + (side,)
                refs.pop(0)[...] = low(wide(kept[at]) + wide(got[0][at]))


def exchange(*entries):
    shapes, inputs, kinds = [], [], []
    for axis, kept, got in entries:
        got = list(got) if isinstance(got, (list, tuple)) else [got]
        inputs += [kept, *got]
        kinds.append((axis, len(got)))
        if axis == "join":
            shapes.append(((1 + len(got)) * kept.shape[0], *kept.shape[1:]))
        elif axis == "far":
            shapes.append(got[0].shape)
        elif axis is None:
            shapes.append(kept.shape)
        else:
            shapes += [kept.shape[:axis] + kept.shape[axis + 1 :]] * 2
    return pl.pallas_call(
        functools.partial(exchange_kernel, kinds),
        grid=(2,),
        in_specs=[half_block(member.shape) for member in inputs],
        out_specs=[half_block(shape) for shape in shapes],
        out_shape=[jax.ShapeDtypeStruct(shape, LOWTYPE) for shape in shapes],
        cost_estimate=takes(0.5),
        compiler_params=pltpu.CompilerParams(
            dimension_semantics=("arbitrary",), vmem_limit_bytes=48 * MEBI
        ),
        name="exchange",
    )(*inputs)


def swap_plane(member, distance):
    size = lax.axis_size("dp")
    return lax.ppermute(member, "dp", [(i, i ^ (distance << 2)) for i in range(size)])


def far_parts(member):
    run = member.shape[0] // FAR
    return [
        swap_plane(member[index * run : (index + 1) * run], distance)
        for index, distance in ((1, 2), (2, 1), (3, 3))
    ]


def far_copies(member):
    return [swap_plane(member, distance) for distance in (2, 1, 3)]


def paired(member):
    return member.reshape(2, member.shape[0] // 2, *member.shape[1:])


def vector_back_kernel(d_projected, cond_weight, unit, d_queries, offset, gain, query, d_normed):
    step = pl.program_id(0)
    offset[...] = column_sum(wide(d_projected[...]))
    part = product_right(d_projected[...], cond_weight[...])

    @pl.when(step == 0)
    def _():
        d_normed[...] = part
        query[...] = column_sum(wide(d_queries[...]))

    @pl.when(step > 0)
    def _():
        d_normed[...] += part

    @pl.when(step == pl.num_programs(0) - 1)
    def _():
        gain[...] = column_sum(d_normed[...] * unit[...])


def vector_back(d_projected, cond_weight, unit, d_projections):
    length, columns = d_projected.shape
    width = columns // 6
    depth = unit.shape[1]
    return pl.pallas_call(
        vector_back_kernel,
        grid=(6,),
        in_specs=[
            pl.BlockSpec((length, width), lambda i: (0, i)),
            pl.BlockSpec((depth, width), lambda i: (0, i)),
            full_spec(unit),
            pl.BlockSpec((length, width), lambda i: (0, 0)),
        ],
        out_specs=[
            pl.BlockSpec((1, width), lambda i: (0, i)),
            pl.BlockSpec((1, depth), lambda i: (0, 0)),
            pl.BlockSpec((1, width), lambda i: (0, 0)),
        ],
        out_shape=[
            jax.ShapeDtypeStruct((1, columns), WIDE),
            jax.ShapeDtypeStruct((1, depth), WIDE),
            jax.ShapeDtypeStruct((1, width), WIDE),
        ],
        scratch_shapes=[pltpu.VMEM((length, depth), WIDE)],
        cost_estimate=takes(15),
        compiler_params=pltpu.CompilerParams(
            dimension_semantics=("arbitrary",), vmem_limit_bytes=32 * MEBI
        ),
        name="vector_back",
    )(d_projected, cond_weight, unit, d_projections)


TOKEN_ROWS = 256


def rows_spec(columns, at=0):
    return pl.BlockSpec((TOKEN_ROWS, columns), lambda i: (i, at))


def transition_back_kernel(d_result, gate_two, down_out, gate_up, down_weight, d_down, d_last, d_gate_up):
    half = gate_up.shape[1] // 2
    result = wide(d_result[...])
    gate = sigmoid(gate_two[...])
    given = low(result * gate)
    d_down[...] = given
    d_last[...] = low(result * down_out[...] * gate * (1.0 - gate))
    d_hidden = wide(low(product_right(given, down_weight[...])))
    gate_half = gate_up[:, :half]
    logistic = sigmoid(gate_half)
    d_gate_up[:, :half] = low(
        d_hidden * gate_up[:, half:] * logistic * (1.0 + gate_half * (1.0 - logistic))
    )
    d_gate_up[:, half:] = low(d_hidden * gate_half * logistic)


def transition_back(d_result, projected, down_out, gate_up, down_weight):
    length, width = d_result.shape
    outs = [
        jax.ShapeDtypeStruct((length, width), LOWTYPE),
        jax.ShapeDtypeStruct((length, width), LOWTYPE),
        jax.ShapeDtypeStruct(gate_up.shape, LOWTYPE),
    ]
    return pl.pallas_call(
        transition_back_kernel,
        grid=(length // TOKEN_ROWS,),
        in_specs=[
            rows_spec(width),
            rows_spec(width, 5),
            rows_spec(width),
            rows_spec(gate_up.shape[1]),
            full_spec(down_weight),
        ],
        out_specs=[rows_spec(member.shape[1]) for member in outs],
        out_shape=outs,
        cost_estimate=takes(5),
        compiler_params=pltpu.CompilerParams(
            dimension_semantics=("arbitrary",), vmem_limit_bytes=48 * MEBI
        ),
        name="transition_back",
    )(d_result, projected, down_out, gate_up, down_weight)


def middle_back_kernel(
    d_result,
    gate_one,
    scale_two,
    d_gate_up,
    unit_two,
    spread_two,
    attn_out,
    gu_weight,
    out_weight,
    d_middle,
    d_attn_out,
    d_gated,
    d_pieces,
):
    width = d_result.shape[1]
    d_normed = product_right(d_gate_up[...], gu_weight[...])
    scale = sigmoid(scale_two[...])
    unit = unit_two[...]
    d_pieces[:, width : 2 * width] = low(d_normed * unit * scale * (1.0 - scale))
    d_pieces[:, 2 * width :] = low(d_normed)
    middle = wide(d_result[...]) + normalise_back(d_normed * scale, unit, spread_two[...])
    d_middle[...] = middle
    gate = sigmoid(gate_one[...])
    given = low(middle * gate)
    d_attn_out[...] = given
    d_pieces[:, :width] = low(middle * attn_out[...] * gate * (1.0 - gate))
    d_gated[...] = low(product_right(given, out_weight[...]))


def middle_back(
    d_result, projected, d_gate_up, unit_two, spread_two, attn_out, gu_weight, out_weight
):
    length, width = d_result.shape
    outs = [
        jax.ShapeDtypeStruct((length, width), WIDE),
        jax.ShapeDtypeStruct((length, width), LOWTYPE),
        jax.ShapeDtypeStruct((length, width), LOWTYPE),
        jax.ShapeDtypeStruct((length, 3 * width), LOWTYPE),
    ]
    return pl.pallas_call(
        middle_back_kernel,
        grid=(length // TOKEN_ROWS,),
        in_specs=[
            rows_spec(width),
            rows_spec(width, 2),
            rows_spec(width, 3),
            rows_spec(d_gate_up.shape[1]),
            rows_spec(width),
            rows_spec(1),
            rows_spec(width),
            full_spec(gu_weight),
            full_spec(out_weight),
        ],
        out_specs=[rows_spec(member.shape[1]) for member in outs],
        out_shape=outs,
        cost_estimate=takes(8),
        compiler_params=pltpu.CompilerParams(
            dimension_semantics=("arbitrary",), vmem_limit_bytes=48 * MEBI
        ),
        name="middle_back",
    )(
        d_result,
        projected,
        projected,
        d_gate_up,
        unit_two,
        spread_two,
        attn_out,
        gu_weight,
        out_weight,
    )


def input_back_kernel(
    d_projections,
    scale_one,
    unit_one,
    spread_one,
    d_middle,
    d_pieces,
    d_last,
    proj_weight,
    d_projected,
    d_tokens,
):
    width = unit_one.shape[1]
    d_normed = product_right(d_projections[...], proj_weight[...])
    scale = sigmoid(scale_one[...])
    unit = unit_one[...]
    d_projected[:, :width] = low(d_normed * unit * scale * (1.0 - scale))
    d_projected[:, width : 2 * width] = low(d_normed)
    d_projected[:, 2 * width : 5 * width] = d_pieces[...]
    d_projected[:, 5 * width :] = d_last[...]
    d_tokens[...] = low(d_middle[...] + normalise_back(d_normed * scale, unit, spread_one[...]))


def input_back(
    d_projections, projected, unit_one, spread_one, d_middle, d_pieces, d_last, proj_weight
):
    length, width = unit_one.shape
    outs = [
        jax.ShapeDtypeStruct((length, 6 * width), LOWTYPE),
        jax.ShapeDtypeStruct((length, width), LOWTYPE),
    ]
    return pl.pallas_call(
        input_back_kernel,
        grid=(length // TOKEN_ROWS,),
        in_specs=[
            rows_spec(4 * width),
            rows_spec(width),
            rows_spec(width),
            rows_spec(1),
            rows_spec(width),
            rows_spec(3 * width),
            rows_spec(width),
            full_spec(proj_weight),
        ],
        out_specs=[rows_spec(member.shape[1]) for member in outs],
        out_shape=outs,
        cost_estimate=takes(15),
        compiler_params=pltpu.CompilerParams(
            dimension_semantics=("arbitrary",), vmem_limit_bytes=48 * MEBI
        ),
        name="input_back",
    )(d_projections, projected, unit_one, spread_one, d_middle, d_pieces, d_last, proj_weight)


def together(*members):
    return lax.optimization_barrier(members)


def token_units(pair_rows):
    unit, _ = normalise(wide(pair_rows).reshape(-1, pair_rows.shape[-1]))
    return low(unit)


def atom_units(pair_rows):
    values = wide(pair_rows)
    centre = values - jnp.mean(values, axis=1, keepdims=True)
    return centre * lax.rsqrt(jnp.mean(centre * centre, axis=1, keepdims=True) + EPS)


def in_turn(member):
    member = jnp.stack([member, swap_bit(member, 3)])
    return jnp.concatenate([member, swap_bit(member, 2)], axis=0)


def gather_token_bias(part):
    groups = part.shape[0] // GROUP_HEADS
    gathered = []
    for group in range(groups):
        runs = in_turn(part[group * GROUP_HEADS : (group + 1) * GROUP_HEADS])
        if group % 2:
            runs = jnp.stack([runs, swap_section(runs)])
            runs = jnp.stack([runs, swap_near(runs)])
        else:
            runs = jnp.stack([runs, swap_near(runs)])
            runs = jnp.stack([runs, swap_section(runs)], axis=1)
        gathered += [runs, swap_core(runs)]
    return gathered


def halves_sum(kept, got):
    half = kept.shape[0] // 2
    return add_low(kept[:half], got[:half]), add_low(kept[half:], got[half:])


def cross_of_all(d_token_bias, d_atom_bias, both, pair_units, heads):
    whole = jnp.stack(d_token_bias).transpose(3, 1, 0, 2, 5, 4, 6)
    whole = whole.reshape(-1, heads, whole.shape[-1])
    slab = lax.psum_scatter(whole, both, scatter_dimension=0, tiled=True).transpose(1, 0, 2)
    token_cross = product(slab.reshape(heads, -1), pair_units)
    whole = jnp.stack(d_atom_bias).transpose(2, 1, 0, 3, 4, 5)
    whole = whole.reshape(-1, *whole.shape[4:])
    return token_cross, lax.psum_scatter(whole, "dp", scatter_dimension=0, tiled=True)


def gather_atom_bias(part):
    runs = in_turn(part)
    runs = jnp.stack([runs, swap_near(runs)])
    return [runs, swap_core(runs)]


def token_block_forward(place, token_in, condition, weights, bias):
    gain, cond_weight, cond_bias, proj_weight, query_bias, out_weight, gu_weight, down_weight = (
        weights
    )
    width = token_in.shape[1]
    unit_cond, _ = normalise(condition)
    normed = low(unit_cond * wide(gain))
    projected = product(normed, cond_weight) + wide(cond_bias)
    pieces = [projected[:, i * width : (i + 1) * width] for i in range(6)]
    unit_one, spread_one = normalise(token_in)
    normed_one = low(unit_one * sigmoid(pieces[0]) + pieces[1])
    offset = jnp.concatenate([wide(query_bias), jnp.zeros((3 * width,), WIDE)])
    projections = low(product(normed_one, proj_weight) + offset)
    probability, attended, gated = token_forward(place, projections, bias)
    attn_out = product(gated, out_weight)
    middle = token_in + sigmoid(pieces[2]) * attn_out
    unit_two, spread_two = normalise(middle)
    normed_two = low(unit_two * sigmoid(pieces[3]) + pieces[4])
    gate_up = product(normed_two, gu_weight)
    half = gate_up.shape[1] // 2
    gate_half, up_half = gate_up[:, :half], gate_up[:, half:]
    hidden = low(gate_half * sigmoid(gate_half) * up_half)
    down_out = product(hidden, down_weight)
    output = middle + sigmoid(pieces[5]) * down_out
    stored = (
        unit_cond,
        normed,
        projected,
        unit_one,
        spread_one,
        normed_one,
        projections,
        probability,
        attended,
        gated,
        attn_out,
        unit_two,
        spread_two,
        normed_two,
        gate_up,
        hidden,
        down_out,
    )
    return output, stored


def local(
    atom_features,
    atom_single,
    atom_pairs,
    atom_token,
    window_start,
    pair_repr,
    single_repr,
    noise_table,
    noise_index,
    cotangent,
    *params,
):
    atom_block, atompair_gain, atompair_weight, gather_weight = (
        params[:8],
        params[8],
        params[9],
        params[10],
    )
    token_block, tokpair_gain, tokpair_weight = params[11:19], params[19], params[20]
    section, far, near, core = places()
    here = jnp.stack([section, far, near, core, piece_index()]).astype(jnp.int32)
    length = cotangent.shape[2]
    both = ("dp", "section")

    def mine(member):
        return lax.dynamic_index_in_dim(member, section, 0, keepdims=False)[0]

    rows = pair_repr.shape[0] // 2
    heads = tokpair_weight.shape[1]
    window_units = atom_units(atom_pairs)
    atom_gained = wide(atompair_gain)[:, None] * wide(atompair_weight)
    atom_part = low(
        jnp.sum(window_units[:, :, None] * atom_gained[None, :, :, None, None], axis=1)
    )
    windows, atom_heads, span, keys = atom_part.shape
    pair_units = token_units(lax.dynamic_slice_in_dim(pair_repr, section * rows, rows, 0))
    gained = low(wide(tokpair_gain)[:, None] * wide(tokpair_weight))
    token_part = low(
        lax.dot_general(
            gained, pair_units, (((0,), (1,)), ((), ())), preferred_element_type=WIDE
        )
    ).reshape(heads, rows, length)
    run = length // (8 * FAR)
    direct = lax.axis_size("dp") == 4 * FAR and rows == run
    if direct:
        place = here
        atom_bias = gather_atom_bias(atom_part)
        token_bias = gather_token_bias(token_part)
    else:
        place = jnp.zeros((5,), jnp.int32)
        whole = lax.all_gather(atom_part, "dp", axis=0, tiled=True)
        whole = whole.reshape(FAR, 2, 2, -1, atom_heads, span, keys).transpose(2, 1, 0, 3, 4, 5, 6)
        atom_bias = [whole[0], whole[1]]
        whole = lax.all_gather(token_part, both, axis=0).transpose(0, 2, 1, 3)
        whole = whole.reshape(FAR, 2, 2, 2, run, -1, GROUP_HEADS, length)
        whole = whole.transpose(5, 2, 1, 3, 0, 6, 4, 7)
        token_bias = [whole[g, c] for g in range(whole.shape[0]) for c in range(2)]

    features = mine(atom_features)
    condition = wide(single_repr) + noise_table[mine(noise_index)]
    pooled, counts, *atom_stored = atom_forward(
        window_start,
        place,
        features,
        atom_single,
        atom_token,
        atom_bias,
        atom_block,
        gather_weight,
        length,
    )
    output, token_stored = token_block_forward(
        place, wide(pooled), condition, token_block, token_bias
    )

    (
        unit_cond,
        normed,
        projected,
        unit_one,
        spread_one,
        normed_one,
        projections,
        probability,
        attended,
        gated,
        attn_out,
        unit_two,
        spread_two,
        normed_two,
        gate_up,
        hidden,
        down_out,
    ) = token_stored
    _, cond_weight, _, proj_weight, _, out_weight, gu_weight, down_weight = token_block
    width = output.shape[1]
    chunk_a = products(gu_weight.shape, down_weight.shape)
    chunk_b = products(proj_weight.shape, out_weight.shape, cond_weight.shape)
    d_result = mine(cotangent)
    output_halves = exchange_halves(low(output))
    normed_here = from_here(normed)
    d_result, output_halves, normed_here = together(d_result, output_halves, normed_here)
    d_down, d_last, d_gate_up = transition_back(
        d_result, projected, down_out, gate_up, down_weight
    )
    members_a = [normed_two, d_gate_up, hidden, d_down]
    given_a = chunk_given(here, chunk_a, members_a)
    given_a_there = swap_core(given_a)
    d_gate_up, given_a_there = together(d_gate_up, given_a_there)
    send_a, keep_a = chunk_kept(here, chunk_a, members_a, given_a_there)
    d_gate_up, send_a = together(d_gate_up, send_a)
    got_a = swap_section(send_a)
    d_middle, d_attn_out, d_gated, d_pieces = middle_back(
        d_result, projected, d_gate_up, unit_two, spread_two, attn_out, gu_weight, out_weight
    )
    *d_token_bias, d_projections = token_backward(
        place, projections, probability, attended, d_gated, run
    )
    if direct:
        got_bias = swap_core(d_token_bias[1])

    d_projections, got_a = together(d_projections, got_a)
    keep_a, send_a = exchange((0, paired(keep_a), paired(got_a)))
    d_projections, send_a = together(d_projections, send_a)
    got_a = swap_near(send_a)
    d_projected, d_tokens = input_back(
        d_projections, projected, unit_one, spread_one, d_middle, d_pieces, d_last, proj_weight
    )
    members_b = [normed_one, d_projections, gated, d_attn_out, normed_here, d_projected]
    given_b = chunk_given(here, chunk_b, members_b)
    d_projected, given_b = together(d_projected, given_b)
    given_b_there = swap_core(given_b)
    grad_offset, grad_gain, grad_query = vector_back(
        d_projected, cond_weight, unit_cond, d_projections
    )
    given_b_there, grad_query = together(given_b_there, grad_query)
    send_b, keep_b = chunk_kept(here, chunk_b, members_b, given_b_there)
    d_tokens, send_b, got_a = together(d_tokens, send_b, got_a)
    got_b = swap_section(send_b)

    entries = [(0, paired(keep_a), paired(got_a))]
    if direct:
        entries.append((0, d_token_bias[0], got_bias))
    keep_a, send_a, *bias = exchange(*entries)
    d_tokens, send_a, *bias = together(d_tokens, send_a, *bias)
    got_a = swap_plane(send_a, 1)
    if direct:
        bias, send_bias = bias
        got_bias = swap_near(send_bias)
    d_attended, d_gates, d_middles, d_atom_pieces, packed_a = atom_tokens_back(
        features, atom_single, atom_token, d_tokens, counts, atom_stored, atom_block, gather_weight
    )
    d_attended, got_a = together(d_attended, got_a)
    keep_a, send_a = exchange((0, paired(keep_a), paired(got_a)))
    d_attended, send_a = together(d_attended, send_a)
    got_a = swap_plane(send_a, 2)
    d_atom_projections, *d_atom_bias = atom_attention_back(
        window_start, place, d_attended, atom_stored
    )
    d_atom_projections, got_b, got_a = together(d_atom_projections, got_b, got_a)
    entries = [(0, paired(keep_b), paired(got_b)), (None, keep_a, got_a)]
    keep_b, send_b, total_a = exchange(*entries)
    total_a = rest_sum(total_a)
    d_middles, send_b, total_a = together(d_middles, send_b, total_a)
    got_b, got_a = swap_near(send_b), swap_plane(total_a, 2)
    if direct:
        d_middles, got_bias = together(d_middles, got_bias)
        bias, send_bias = exchange((0, bias, got_bias))
        d_middles, send_bias = together(d_middles, send_bias)
        got_bias = swap_section(send_bias)
        got_atom = swap_core(d_atom_bias[1])
    d_features, packed_b, gain, offset, query = atom_features_back(
        features, atom_single, d_atom_projections, d_gates, d_middles, d_atom_pieces, atom_block
    )
    packed = jnp.concatenate([packed_b, packed_a], axis=1)
    packed = jnp.pad(packed, ((0, 0), (0, -packed.shape[1] % (2 * COLUMNS))))
    chunk_d = products(packed.shape)
    chunk_d[0].direct = True
    given_d = chunk_given(here, chunk_d, [packed])
    got_d = swap_core(given_d)
    given_d, got_a = together(given_d, got_a)
    entries = [("join", total_a, got_a)]
    if direct:
        entries.append((0, d_atom_bias[0], got_atom))
    total_a, *atom = exchange(*entries)
    got_d, total_a, *atom = together(got_d, total_a, *atom)
    got_a = swap_plane(total_a, 1)
    if direct:
        atom, send_atom = atom
        got_atom = swap_near(send_atom)
    send_d, keep_d = chunk_kept(here, chunk_d, [packed], got_d)
    got_d = swap_section(send_d)
    feature_halves = exchange_halves(low(d_features))
    got_d, feature_halves = together(got_d, feature_halves)

    entries = [
        (0, paired(keep_b), paired(got_b)),
        (0, paired(keep_d), paired(got_d)),
        ("join", total_a, got_a),
    ]
    if direct:
        entries += [(0, paired(atom), paired(got_atom)), (0, paired(bias), paired(got_bias))]
    keep_b, send_b, keep_d, send_d, total_a, *atom = exchange(*entries)
    got_b, got_d, got_a = swap_plane(send_b, 1), swap_near(send_d), swap_near(total_a)
    if direct:
        *atom, bias, send_bias = atom
        got_atom, got_bias = swap_plane(atom[1], 1), swap_plane(send_bias, 1)

    entries = [
        (0, paired(keep_b), paired(got_b)),
        (0, paired(keep_d), paired(got_d)),
        ("join", total_a, got_a),
    ]
    if direct:
        entries += [(0, paired(atom[0]), paired(got_atom)), (0, paired(bias), paired(got_bias))]
    keep_b, send_b, keep_d, send_d, total_a, *atom = exchange(*entries)
    got_b, got_d, core_a = swap_plane(send_b, 2), swap_plane(send_d, 1), swap_core(total_a)
    if direct:
        *atom, bias, send_bias = atom
        got_atom, got_bias = swap_plane(atom[1], 2), swap_plane(send_bias, 2)

    entries = [(None, keep_b, got_b), (0, paired(keep_d), paired(got_d))]
    if direct:
        entries += [(None, atom[0], got_atom), (None, bias, got_bias)]
    total_b, keep_d, send_d, *atom = exchange(*entries)
    total_b = rest_sum(total_b)
    got_b, got_d = swap_plane(total_b, 2), swap_plane(send_d, 2)
    if direct:
        atom_slab, token_slab = atom
        token_cross = product(token_slab.reshape(heads, -1), pair_units)
    else:
        token_cross, atom_slab = cross_of_all(d_token_bias, d_atom_bias, both, pair_units, heads)
    atom_slab = atom_slab.reshape(windows, atom_heads, span, keys)
    atom_cross = jnp.sum(window_units[:, :, None] * wide(atom_slab)[:, None], axis=(0, 3, 4))
    vectors = [gain, offset, query, grad_gain, grad_offset, grad_query]
    vectors += [token_cross.reshape(1, -1), atom_cross.reshape(1, -1)]
    total = jnp.concatenate(vectors, axis=1)
    got_b, got_d, total = together(got_b, got_d, total)
    got = swap_section(total)

    total_b, total_d = exchange(("join", total_b, got_b), (None, keep_d, got_d))
    total_d = rest_sum(total_d)
    got_b, got_d = swap_plane(total_b, 1), swap_plane(total_d, 2)
    grad_gu, grad_down = assemble(here, chunk_a, total_a, core_a)
    got_b, got_d, got, grad_gu = together(got_b, got_d, got, grad_gu)
    total = total + got

    total_b, total_d = exchange(("join", total_b, got_b), ("join", total_d, got_d))
    total_b, total_d, total = together(total_b, total_d, total)
    got_b, got_d, got = swap_near(total_b), swap_plane(total_d, 1), swap_plane(total, 1)
    got_d, got = together(got_d, got)
    total = total + got
    (total_d,) = exchange(("join", total_d, got_d))
    total_d, total = together(total_d, total)
    got_d, got = swap_near(total_d), swap_plane(total, 2)
    got_d, got_b, got = together(got_d, got_b, got)
    total = total + got
    for bit in more_bits():
        total = total + swap_bit(total, bit)
    total_b, total_d = exchange(("join", total_b, got_b), ("join", total_d, got_d))
    core_b, core_d, got = swap_core(total_b), swap_core(total_d), swap_near(total)
    core_d, got = together(core_d, got)
    total = total + got
    got = swap_core(total)
    (packed,) = assemble(here, chunk_d, total_d, core_d)
    core_b, packed, got = together(core_b, packed, got)
    total = (total + got)[0]
    grad_proj, grad_out, grad_cond = assemble(here, chunk_b, total_b, core_b)

    atom_width = features.shape[1]
    sizes = [6 * atom_width, 4 * atom_width, width, atom_block[6].shape[1], atom_width]
    sizes.append(2 * atom_width)
    pieces_of = []
    first = 0
    for size in sizes:
        pieces_of.append(packed[:, first : first + size])
        first += size
    atom_cond, atom_proj, atom_gather, atom_gu, atom_out, quarters = pieces_of
    atom_down = quarters.reshape(-1, 2, atom_width).transpose(1, 0, 2).reshape(-1, atom_width)


    sums = []
    first = 0
    for member in vectors:
        sums.append(total[first : first + member.size])
        first += member.size
    gain, offset, query, token_gain, token_offset, token_query = [
        run_of(member, section, 2) for member in sums[:6]
    ]
    token_cross = run_of(sums[6].reshape(heads, -1).T, section, 2)
    atom_cross = run_of(sums[7].reshape(atom_cross.shape), section, 2)
    token_pair_gain = jnp.sum(token_cross * wide(run_of(tokpair_weight, section, 2)), axis=1)
    token_pair_weight = token_cross * wide(run_of(tokpair_gain, section, 2))[:, None]
    pair_gain = jnp.sum(atom_cross * wide(run_of(atompair_weight, section, 2)), axis=1)
    pair_weight = atom_cross * wide(run_of(atompair_gain, section, 2))[:, None]
    return (
        output_halves,
        wide(feature_halves),
        gain,
        atom_cond,
        offset,
        atom_proj,
        query,
        atom_out,
        atom_gu,
        atom_down,
        pair_gain,
        pair_weight,
        atom_gather,
        token_gain,
        grad_cond,
        token_offset,
        grad_proj,
        token_query,
        grad_out,
        grad_gu,
        grad_down,
        token_pair_gain,
        token_pair_weight,
    )


def exchange_halves(member):
    section = lax.axis_index("section")
    halves = member.reshape(2, -1, member.shape[1])
    given = lax.dynamic_index_in_dim(halves, 1 - section, 0, keepdims=False)
    kept = lax.dynamic_index_in_dim(halves, section, 0, keepdims=False)
    taken = swap_section(given)
    first = section == 0
    return jnp.stack([jnp.where(first, kept, taken), jnp.where(first, taken, kept)])[:, None]


def solution(mesh):
    weights = [P()] * 21
    halves = P(None, "dp", "section", None)
    grads = [1, 2, 1, 2, 1, 2, 2, 2, 1, 2, 2, 1, 2, 1, 2, 1, 2, 2, 2, 1, 2]
    return jax.shard_map(
        local,
        mesh=mesh,
        in_specs=(
            P(None, "dp", None, None),
            P(),
            P("dp", None, None, None),
            P(),
            P(),
            P("dp", None, None),
            P(),
            P(),
            P(None, "dp"),
            P(None, "dp", None, None),
            *weights,
        ),
        out_specs=(halves, halves)
        + tuple(P("section") if rank == 1 else P("section", None) for rank in grads),
        check_vma=False,
    )
```

time: 1260 us -> 625 us (0.50)
  local copies, waits for them, and re-layouts: 305 us -> 40.9 us
  Pallas kernels: 0 us -> 248 us
  waiting for transfers between devices: 431 us -> 193 us
  matrix products: 258 us -> 28 us
  other arithmetic: 219 us -> 43.2 us
  starting transfers between devices: 5.4 us -> 57.6 us
  between operations: 18 us -> 4.65 us
    reduce_scatter x7 -> x0, waiting for transfers between devices: 261 us -> none  [the longest x5 235 us: local(): lax.psum_scatter(grads[i].astype(LOWTYPE), 'section', scatter_dimension=0...]
    pallas_call x0 -> x32, Pallas kernels: none -> 248 us  [the longest x1 40.7 us: atom_forward(): pl.pallas_call(atom_forward_kernel, grid_spec=pltpu.PrefetchScalarGridSpe...]
    dot_general x40 -> x1, matrix products: 208 us -> 0.64 us  [local(): lax.dot_general(gained, pair_units, (((0,), (1,)), ((), ())), preferred_e...]
    ppermute x0 -> x57, waiting for transfers between devices: none -> 193 us  [the longest x30 90 us: swap_bit(): lax.ppermute(member, 'dp', [(i, i ^ 1 << bit) for i in range(lax.axis_siz...]
    psum x1 -> x0, waiting for transfers between devices: 157 us -> none  [local(): flat = lax.psum(flat, 'dp')[0].astype(WIDE)]
    scatter-add x2 -> x0, other arithmetic: 90.6 us -> none  [the longest x1 45.3 us: atom_backward_attend(): d_keys = jnp.zeros((atom_count, col_count), WIDE).at[flat_positions].add(...]
    reshape x30 -> x4, local copies, waits for them, and re-layouts: 73.8 us -> 1.55 us  [the longest x1 1.35 us: atom_tokens_back(): token_cols = atom_token.reshape(atoms, 1)]
    gather x4 -> x0, local copies, waits for them, and re-layouts: 72.2 us -> none  [the longest x2 36.1 us: atom_windows(): value_rows[positions].reshape(windows, span_key, head_count, head_size)]
  transfers between devices with their start and end apart: 12 -> 57, of which waited for: 9 -> 29; matrix products, arithmetic and copies ran while one was open for 43% -> 8% of each run, Pallas kernels for 0% -> 26%
where the time goes in v2:
time: 625 us; the launch traced here: 615 us
  Pallas kernels  248 us (40%)
  waiting for transfers between devices  193 us (31%)
  starting transfers between devices  57.6 us (9%)
  other arithmetic  43.2 us (7%)
  local copies, waits for them, and re-layouts  40.9 us (7%)
  matrix products  28 us (4%)
    ppermute x30, waiting for transfers between devices, swap_bit(): lax.ppermute(member, 'dp', [(i, i ^ 1 << bit) for i in range(lax.axis_siz...  90 us
    ppermute x18, waiting for transfers between devices, swap_plane(): lax.ppermute(member, 'dp', [(i, i ^ distance << 2) for i in range(size)])  86.4 us
    pallas_call x1, Pallas kernels, atom_forward(): pl.pallas_call(atom_forward_kernel, grid_spec=pltpu.PrefetchScalarGridSpe...  40.7 us
    pallas_call x1, Pallas kernels, token_forward(): pl.pallas_call(token_forward_kernel, grid_spec=pltpu.PrefetchScalarGridSp...  32.8 us
    unnamed x262, local copies, waits for them, and re-layouts  30.5 us
    dot_general x6, matrix products, product(): return jnp.dot(left, right, preferred_element_type=WIDE)  27.3 us
    pallas_call x1, Pallas kernels, token_backward(): pl.pallas_call(token_backward_kernel, grid_spec=pltpu.PrefetchScalarGridS...  27.1 us
    ppermute x30, starting transfers between devices, swap_bit(): lax.ppermute(member, 'dp', [(i, i ^ 1 << bit) for i in range(lax.axis_siz...  26 us
  transfers between devices with their start and end apart: 57, of which 29 were waited for; matrix products, arithmetic and copies ran while one was open for 8% of the time, Pallas kernels for 26%

profile of v2, /device:TPU:0, one launch (start us, length us, event | category | flops | bytes accessed | tf_op | source)
XLA Modules:
  0.0 615.4 jit_solution(11684165284416450101)
XLA Ops:
  22.2 5.4 collective-permute-done.9
  63.0 6.9 %collective-permute-done.2 = bf16[4,4,4,32,128]{4,3,2,1,0:T(8,128)(2,1)} collective-permute-done((bf16[4,4,4,32,128]{4,3,2,1,0:T(8,128)(2,1)}, bf16[4,4,4,32,128]{4,3,2,1,0:T(8,128)(2,1)}, u32[]{:S(2)}, u32[]{:S(2)}) %collective-permute-start.2) | collective-permute-done | bytes 524320 | tf_op jit(solution)/shard_map/ppermute | solution.py:854
  71.3 7.1 %convolution_add_fusion.gate_two.gate_one.scale_two.scale_one = f32[512,4608]{1,0:T(8,128)} fusion(bf16[512,384]{1,0:T(8,128)(2,1)S(1)} %get-tuple-element.431, bf16[384,4608]{1,0:T(8,128)(2,1)} %cond_weight.5, f32[4608]{0:T(1024)S(1)} %convert_element_type.121), kind=kOutput, calls=%fused_computation.1 | convolution fusion | flops 1814298624 | bytes 13387776 | tf_op jit(solution)/shard_map/dot_general | solution.py:24
  78.4 13.0 %collective-permute-done.12 = bf16[2,4,8,16,512]{4,3,2,1,0:T(8,128)(2,1)} collective-permute-done((bf16[2,4,8,16,512]{4,3,2,1,0:T(8,128)(2,1)}, bf16[2,4,8,16,512]{4,3,2,1,0:T(8,128)(2,1)}, u32[]{:S(2)}, u32[]{:S(2)}) %collective-permute-start.12) | collective-permute-done | bytes 1048608 | tf_op jit(solution)/shard_map/ppermute | solution.py:854
  96.6 40.7 %atom_forward.1 = (bf16[512,768]{1,0:T(8,128)(2,1)S(1)}, f32[512,1]{1,0:T(8,128)S(1)}, bf16[2048,512]{1,0:T(8,128)(2,1)}, f32[2048,128]{1,0:T(8,128)S(1)}, bf16[64,128,128]{2,1,0:T(8,128)(2,1)}) custom-call(s32[64]{0:T(128)S(1)} %copy-done.71, s32[5]{0:T(128)S(1)} %stack.111.place, bf16[2048,128]{1,0:T(8,128)(2,1)S(1)} %dynamic-slice_bitcast_fusion.1.features, ...), custom_call_target="tpu_custom_call" | custom-call | bytes 147600000 | tf_op jit(solution)/shard_map/atom_forward/pallas_call | solution.py:230
  141.6 6.8 %add_convert_fusion.queries.keys.values.gates = bf16[512,3072]{1,0:T(8,128)(2,1)} fusion(bf16[512,768]{1,0:T(8,128)(2,1)S(1)} %get-tuple-element.417.refs_0_, bf16[768,3072]{1,0:T(8,128)(2,1)} %proj_weight.4, f32[3072]{0:T(1024)S(1)} %pad_convert_fusion), kind=kOutput, calls=%fused_computation.2 | convolution fusion | flops 2419064832 | bytes 8663040 | tf_op jit(solution)/shard_map/dot_general | solution.py:24
  148.5 32.8 %token_forward.1 = (bf16[16,512,512]{2,1,0:T(8,128)(2,1)}, f32[512,768]{1,0:T(8,128)S(1)}, bf16[512,768]{1,0:T(8,128)(2,1)S(1)}) custom-call(s32[5]{0:T(128)S(1)} %stack.111.place, bf16[512,3072]{1,0:T(8,128)(2,1)} %add_convert_fusion.queries.keys.values.gates, bf16[512,3072]{1,0:T(8,128)(2,1)} %add_convert_fusion.queries.keys.values.gates, ...), custom_call_target="tpu_custom_call" | custom-call | bytes 114390000 | tf_op jit(solution)/shard_map/token_forward/pallas_call | solution.py:692
  204.7 7.3 %collective-permute-done.14 = bf16[256,768]{1,0:T(8,128)(2,1)} collective-permute-done((bf16[256,768]{1,0:T(8,128)(2,1)}, bf16[256,768]{1,0:T(8,128)(2,1)}, u32[]{:S(2)}, u32[]{:S(2)}) %collective-permute-start.14) | collective-permute-done | bytes 393248 | tf_op jit(solution)/shard_map/ppermute | solution.py:850
  214.0 6.5 %transition_back.1 = (bf16[512,768]{1,0:T(8,128)(2,1)S(1)}, bf16[512,768]{1,0:T(8,128)(2,1)S(1)}, bf16[512,3072]{1,0:T(8,128)(2,1)}) custom-call(bf16[512,768]{1,0:T(8,128)(2,1)S(1)} %dynamic-slice_bitcast_fusion.d_result, f32[512,4608]{1,0:T(8,128)} %convolution_add_fusion.gate_two.gate_one.scale_two.scale_one, f32[512,768]{1,0:T(8,128)S(1)} %copy-done.31, ...), custom_call_target="tpu_custom_call" | custom-call | bytes 18450000 | tf_op jit(solution)/shard_map/transition_back/pallas_call | solution.py:1253
  220.5 7.0 %chunk_given.3 = bf16[2,8,288,384]{3,2,1,0:T(8,128)(2,1)} custom-call(s32[5]{0:T(128)S(1)} %stack.111.place, bf16[512,768]{1,0:T(8,128)(2,1)S(1)} %copy-done.6, bf16[512,3072]{1,0:T(8,128)(2,1)} %get-tuple-element.194.refs_1_.d_gate_up, bf16[512,1536]{1,0:T(8,128)(2,1)S(1)} %fusion.2.refs_2_, bf16[512,768]{1,0:T(8,128)(2,1)S(1)} %get-tuple-element.190.refs_3_), custom_call_target="tpu_custom_call" | custom-call | bytes 55350000 | tf_op jit(solution)/shard_map/chunk_given/pallas_call | solution.py:1005
  227.6 6.4 %collective-permute-done.15.refs_4_ = bf16[2,8,288,384]{3,2,1,0:T(8,128)(2,1)S(1)} collective-permute-done((bf16[2,8,288,384]{3,2,1,0:T(8,128)(2,1)}, bf16[2,8,288,384]{3,2,1,0:T(8,128)(2,1)S(1)}, u32[]{:S(2)}, u32[]{:S(2)}) %collective-permute-start.15) | collective-permute-done | bytes 3538976 | tf_op jit(solution)/shard_map/ppermute | solution.py:854
  235.8 7.8 %chunk_kept.3 = (bf16[8,288,384]{2,1,0:T(8,128)(2,1)}, bf16[8,288,384]{2,1,0:T(8,128)(2,1)}) custom-call(s32[5]{0:T(128)S(1)} %stack.111.place, bf16[512,768]{1,0:T(8,128)(2,1)S(1)} %copy-done.6, bf16[512,3072]{1,0:T(8,128)(2,1)} %get-tuple-element.194.refs_1_.d_gate_up, bf16[512,1536]{1,0:T(8,128)(2,1)S(1)} %fusion.2.refs_2_, ...), custom_call_target="tpu_custom_call" | custom-call | bytes 73800000 | tf_op jit(solution)/shard_map/chunk_kept/pallas_call | solution.py:1025
  246.7 10.5 %middle_back.1 = (f32[512,768]{1,0:T(8,128)S(1)}, bf16[512,768]{1,0:T(8,128)(2,1)S(1)}, bf16[512,768]{1,0:T(8,128)(2,1)S(1)}, bf16[512,2304]{1,0:T(8,128)(2,1)}) custom-call(bf16[512,768]{1,0:T(8,128)(2,1)S(1)} %copy-done.12, f32[512,4608]{1,0:T(8,128)} %convolution_add_fusion.gate_two.gate_one.scale_two.scale_one, ...), custom_call_target="tpu_custom_call" | custom-call | bytes 29520000 | tf_op jit(solution)/shard_map/middle_back/pallas_call | solution.py:1313
  257.2 27.1 %token_backward.1 = (bf16[2,2,4,16,16,512]{5,4,3,2,1,0:T(8,128)(2,1)}, bf16[2,2,4,16,16,512]{5,4,3,2,1,0:T(8,128)(2,1)}, bf16[512,3072]{1,0:T(8,128)(2,1)S(1)}) custom-call(s32[5]{0:T(128)S(1)} %stack.111.place, bf16[512,3072]{1,0:T(8,128)(2,1)} %add_convert_fusion.queries.keys.values.gates, bf16[512,3072]{1,0:T(8,128)(2,1)} %add_convert_fusion.queries.keys.values.gates, ...), custom_call_target="tpu_custom_call" | custom-call | bytes 29520000 | tf_op jit(solution)/shard_map/token_backward/pallas_call | solution.py:813
  290.0 9.1 %input_back.1 = (bf16[512,4608]{1,0:T(8,128)(2,1)}, bf16[512,768]{1,0:T(8,128)(2,1)S(1)}) custom-call(bf16[512,3072]{1,0:T(8,128)(2,1)} %copy-done.2, f32[512,4608]{1,0:T(8,128)} %convolution_add_fusion.gate_two.gate_one.scale_two.scale_one, f32[512,768]{1,0:T(8,128)S(1)} %copy-done.13, f32[512,1]{1,0:T(8,128)S(1)} %copy.70.spread_one, ...), custom_call_target="tpu_custom_call" | custom-call | bytes 55350000 | tf_op jit(solution)/shard_map/input_back/pallas_call | solution.py:1378
  300.0 8.6 %chunk_given.4 = bf16[2,8,384,384]{3,2,1,0:T(8,128)(2,1)} custom-call(s32[5]{0:T(128)S(1)} %stack.111.place, bf16[512,768]{1,0:T(8,128)(2,1)S(1)} %copy-done.10, bf16[512,3072]{1,0:T(8,128)(2,1)S(1)} %copy-done.3, bf16[512,768]{1,0:T(8,128)(2,1)S(1)} %copy-done.19, bf16[512,768]{1,0:T(8,128)(2,1)S(1)} %get-tuple-element.207.refs_3_, ...), custom_call_target="tpu_custom_call" | custom-call | bytes 55350000 | tf_op jit(solution)/shard_map/chunk_given/pallas_call | solution.py:1005
  312.7 5.2 vector_back.1
  325.0 10.9 %chunk_kept.4 = (bf16[8,384,384]{2,1,0:T(8,128)(2,1)}, bf16[8,384,384]{2,1,0:T(8,128)(2,1)}) custom-call(s32[5]{0:T(128)S(1)} %stack.111.place, bf16[512,768]{1,0:T(8,128)(2,1)S(1)} %copy-done.10, bf16[512,3072]{1,0:T(8,128)(2,1)} %copy-done.2, bf16[512,768]{1,0:T(8,128)(2,1)S(1)} %copy-done.19, bf16[512,768]{1,0:T(8,128)(2,1)S(1)} %get-tuple-element.207.refs_3_, ...), custom_call_target="tpu_custom_call" | custom-call | bytes 73800000 | tf_op jit(solution)/shard_map/chunk_kept/pallas_call | solution.py:1025
  336.6 5.3 exchange.14
  350.8 22.6 %atom_tokens_back.1 = (bf16[2048,128]{1,0:T(8,128)(2,1)S(1)}, bf16[2048,128]{1,0:T(8,128)(2,1)S(1)}, f32[2048,128]{1,0:T(8,128)S(1)}, bf16[2048,512]{1,0:T(8,128)(2,1)}, bf16[128,1664]{1,0:T(8,128)(2,1)S(1)}) custom-call(bf16[2048,128]{1,0:T(8,128)(2,1)S(1)} %copy-done.8, bf16[2048,128]{1,0:T(8,128)(2,1)S(1)} %copy-done.15, s32[2048,1]{1,0:T(8,128)} %copy.71.token_cols, ...), custom_call_target="tpu_custom_call" | custom-call | bytes 11070000 | tf_op jit(solution)/shard_map/atom_tokens_back/pallas_call | solution.py:510
  375.7 18.7 %atom_attention_back.1 = (bf16[2048,384]{1,0:T(8,128)(2,1)S(1)}, bf16[2,4,4,128,128]{4,3,2,1,0:T(8,128)(2,1)S(1)}, bf16[2,4,4,128,128]{4,3,2,1,0:T(8,128)(2,1)}) custom-call(s32[64]{0:T(128)S(1)} %copy-done.72, s32[5]{0:T(128)S(1)} %stack.111.place, bf16[2048,512]{1,0:T(8,128)(2,1)} %get-tuple-element.183.gates.projections, f32[2048,128]{1,0:T(8,128)S(1)} %copy-done.17, ...), custom_call_target="tpu_custom_call" | custom-call | bytes 7380000 | tf_op jit(solution)/shard_map/atom_attention_back/pallas_call | solution.py:554
  398.5 10.8 %collective-permute-done.22.refs_3_ = bf16[1,288,384]{2,1,0:T(8,128)(2,1)S(1)} collective-permute-done((bf16[1,288,384]{2,1,0:T(8,128)(2,1)S(1)}, bf16[1,288,384]{2,1,0:T(8,128)(2,1)S(1)}, u32[]{:S(2)}, u32[]{:S(2)}) %collective-permute-start.22) | collective-permute-done | bytes 221216 | tf_op jit(solution)/shard_map/ppermute | solution.py:1153
  417.8 7.4 %atom_features_back.1 = (f32[2048,128]{1,0:T(8,128)S(1)}, bf16[128,1280]{1,0:T(8,128)(2,1)S(1)}, f32[1,128]{1,0:T(1,128)S(1)}, f32[1,768]{1,0:T(1,128)S(1)}, f32[1,128]{1,0:T(1,128)S(1)}) custom-call(bf16[2048,128]{1,0:T(8,128)(2,1)S(1)} %copy-done.8, bf16[2048,128]{1,0:T(8,128)(2,1)S(1)} %copy-done.15, ...), custom_call_target="tpu_custom_call" | custom-call | bytes 1845000 | tf_op jit(solution)/shard_map/atom_features_back/pallas_call | solution.py:590
  426.2 12.8 %collective-permute-done.25.refs_1_ = bf16[1,288,384]{2,1,0:T(8,128)(2,1)S(1)} collective-permute-done((bf16[1,288,384]{2,1,0:T(8,128)(2,1)S(1)}, bf16[1,288,384]{2,1,0:T(8,128)(2,1)S(1)}, u32[]{:S(2)}, u32[]{:S(2)}) %collective-permute-start.25) | collective-permute-done | bytes 221216 | tf_op jit(solution)/shard_map/ppermute | solution.py:1153
  468.1 15.0 %collective-permute-done.34 = bf16[4,32,384]{2,1,0:T(8,128)(2,1)S(1)} collective-permute-done((bf16[4,32,384]{2,1,0:T(8,128)(2,1)S(1)}, bf16[4,32,384]{2,1,0:T(8,128)(2,1)S(1)}, u32[]{:S(2)}, u32[]{:S(2)}) %collective-permute-start.34) | collective-permute-done | bytes 98336 | tf_op jit(solution)/shard_map/ppermute | solution.py:854
  483.1 8.6 %collective-permute-done.36 = bf16[2,4,128,128]{3,2,1,0:T(8,128)(2,1)S(1)} collective-permute-done((bf16[2,4,128,128]{3,2,1,0:T(8,128)(2,1)S(1)}, bf16[2,4,128,128]{3,2,1,0:T(8,128)(2,1)S(1)}, u32[]{:S(2)}, u32[]{:S(2)}) %collective-permute-start.36) | collective-permute-done | bytes 262176 | tf_op jit(solution)/shard_map/ppermute | solution.py:1153
  498.6 11.9 %collective-permute-done.39 = bf16[2,32,384]{2,1,0:T(8,128)(2,1)S(1)} collective-permute-done((bf16[2,32,384]{2,1,0:T(8,128)(2,1)S(1)}, bf16[2,32,384]{2,1,0:T(8,128)(2,1)S(1)}, u32[]{:S(2)}, u32[]{:S(2)}) %collective-permute-start.39) | collective-permute-done | bytes 49184 | tf_op jit(solution)/shard_map/ppermute | solution.py:1153
  510.5 16.5 %collective-permute-done.40.refs_5_ = bf16[1,4,128,128]{3,2,1,0:T(8,128)(2,1)S(1)} collective-permute-done((bf16[1,4,128,128]{3,2,1,0:T(8,128)(2,1)S(1)}, bf16[1,4,128,128]{3,2,1,0:T(8,128)(2,1)S(1)}, u32[]{:S(2)}, u32[]{:S(2)}) %collective-permute-start.40) | collective-permute-done | bytes 131104 | tf_op jit(solution)/shard_map/ppermute | solution.py:1153
  533.9 11.3 %collective-permute-done.43.refs_3_ = bf16[1,32,384]{2,1,0:T(8,128)(2,1)S(1)} collective-permute-done((bf16[1,32,384]{2,1,0:T(8,128)(2,1)}, bf16[1,32,384]{2,1,0:T(8,128)(2,1)S(1)}, u32[]{:S(2)}, u32[]{:S(2)}) %collective-permute-start.43) | collective-permute-done | bytes 24608 | tf_op jit(solution)/shard_map/ppermute | solution.py:1153
  553.2 5.8 collective-permute-done.45.refs_3_
  574.6 16.5 %collective-permute-done.50.refs_3_ = bf16[4,32,384]{2,1,0:T(8,128)(2,1)S(1)} collective-permute-done((bf16[4,32,384]{2,1,0:T(8,128)(2,1)S(1)}, bf16[4,32,384]{2,1,0:T(8,128)(2,1)S(1)}, u32[]{:S(2)}, u32[]{:S(2)}) %collective-permute-start.50) | collective-permute-done | bytes 98336 | tf_op jit(solution)/shard_map/ppermute | solution.py:854
  602.8 6.5 %assemble.5 = (f32[384,3072]{1,0:T(8,128)}, f32[384,768]{1,0:T(8,128)}, f32[192,4608]{1,0:T(8,128)}) custom-call(s32[5]{0:T(128)S(1)} %stack.111.place, bf16[8,384,384]{2,1,0:T(8,128)(2,1)S(1)} %copy-done.22, bf16[8,384,384]{2,1,0:T(8,128)(2,1)} %collective-permute-done.55.other), custom_call_target="tpu_custom_call" | custom-call | bytes 7380000 | tf_op jit(solution)/shard_map/assemble/pallas_call | solution.py:1059
  (482 shorter events, 222.1 us)
Async XLA Ops:
  10.6 17.0 %collective-permute-start.9 = (bf16[8,16,512]{2,1,0:T(8,128)(2,1)S(1)}, bf16[8,16,512]{2,1,0:T(8,128)(2,1)}, u32[]{:S(2)}, u32[]{:S(2)}) collective-permute-start(bf16[8,16,512]{2,1,0:T(8,128)(2,1)S(1)} %bitcast.195), channel_id=1, source_target_pairs={{0,8},{1,9},{2,10},{3,11},{4,12},{5,13},{6,14},{7,15},{8,0},{9,1},... | collective-permute-start | bytes 393224 | tf_op jit(solution)/shard_map/ppermute | solution.py:854
  15.9 16.6 %collective-permute-start = (bf16[4,4,32,128]{3,2,1,0:T(8,128)(2,1)S(1)}, bf16[4,4,32,128]{3,2,1,0:T(8,128)(2,1)}, u32[]{:S(2)}, u32[]{:S(2)}) collective-permute-start(bf16[4,4,32,128]{3,2,1,0:T(8,128)(2,1)S(1)} %multiply_reduce_fusion.2), channel_id=1, source_target_pairs={{0,8},{1,9},{2,10},{3,11},{4,12},{5,13},{6,14},{7,15},{8,0},{9,1},... | collective-permute-start | bytes 393224 | tf_op jit(solution)/shard_map/ppermute | solution.py:854
  51.1 18.8 %collective-permute-start.2 = (bf16[4,4,4,32,128]{4,3,2,1,0:T(8,128)(2,1)}, bf16[4,4,4,32,128]{4,3,2,1,0:T(8,128)(2,1)}, u32[]{:S(2)}, u32[]{:S(2)}) collective-permute-start(bf16[4,4,4,32,128]{4,3,2,1,0:T(8,128)(2,1)} %get-tuple-element.429), channel_id=1, source_target_pairs={{0,2},{1,3},{2,0},{3,1},{4,6},{5,7},{6,4},{7,5},{8,10},{9,11},{10,... | collective-permute-start | bytes 1572872 | tf_op jit(solution)/shard_map/ppermute | solution.py:854
  53.9 37.4 %collective-permute-start.12 = (bf16[2,4,8,16,512]{4,3,2,1,0:T(8,128)(2,1)}, bf16[2,4,8,16,512]{4,3,2,1,0:T(8,128)(2,1)}, u32[]{:S(2)}, u32[]{:S(2)}) collective-permute-start(bf16[2,4,8,16,512]{4,3,2,1,0:T(8,128)(2,1)} %get-tuple-element.413), channel_id=1, source_target_pairs={{0,2},{1,3},{2,0},{3,1},{4,6},{5,7},{6,4},{7,5},{8,10},{9,11},{10,... | collective-permute-start | bytes 3145736 | tf_op jit(solution)/shard_map/ppermute | solution.py:854
  60.0 34.1 %collective-permute-start.7 = (bf16[2,4,8,16,512]{4,3,2,1,0:T(8,128)(2,1)}, bf16[2,4,8,16,512]{4,3,2,1,0:T(8,128)(2,1)}, u32[]{:S(2)}, u32[]{:S(2)}) collective-permute-start(bf16[2,4,8,16,512]{4,3,2,1,0:T(8,128)(2,1)} %get-tuple-element.415), channel_id=1, source_target_pairs={{0,16},{16,0},{1,17},{17,1},{2,18},{18,2},{3,19},{19,3},{4,20},{20... | collective-permute-start | bytes 3145736 | tf_op jit(solution)/shard_map/ppermute | solution.py:850
  71.2 25.3 %collective-permute-start.3 = (bf16[2,4,4,4,32,128]{5,4,3,2,1,0:T(8,128)(2,1)S(1)}, bf16[2,4,4,4,32,128]{5,4,3,2,1,0:T(8,128)(2,1)S(1)}, u32[]{:S(2)}, u32[]{:S(2)}) collective-permute-start(bf16[2,4,4,4,32,128]{5,4,3,2,1,0:T(8,128)(2,1)S(1)} %pad_maximum_fusion.2.bias_own), channel_id=1, source_target_pairs={{0,1},{1,0},{2,3},{3,2},{4,5},{5,4},{6,7},{7,6},{8,9},{9,8},{10,11... | collective-permute-start | bytes 3145736 | tf_op jit(solution)/shard_map/ppermute | solution.py:854
  94.2 54.3 %collective-permute-start.13 = (bf16[2,2,4,8,16,512]{5,4,3,2,1,0:T(8,128)(2,1)}, bf16[2,2,4,8,16,512]{5,4,3,2,1,0:T(8,128)(2,1)}, u32[]{:S(2)}, u32[]{:S(2)}) collective-permute-start(bf16[2,2,4,8,16,512]{5,4,3,2,1,0:T(8,128)(2,1)} %pad_maximum_fusion.1.own_b), channel_id=1, source_target_pairs={{0,1},{1,0},{2,3},{3,2},{4,5},{5,4},{6,7},{7,6},{8,9},{9,8},{10,11... | collective-permute-start | bytes 6291464 | tf_op jit(solution)/shard_map/ppermute | solution.py:854
  95.9 52.6 %collective-permute-start.8 = (bf16[2,2,4,8,16,512]{5,4,3,2,1,0:T(8,128)(2,1)S(1)}, bf16[2,2,4,8,16,512]{5,4,3,2,1,0:T(8,128)(2,1)}, u32[]{:S(2)}, u32[]{:S(2)}) collective-permute-start(bf16[2,2,4,8,16,512]{5,4,3,2,1,0:T(8,128)(2,1)S(1)} %pad_maximum_fusion.own_a), channel_id=1, source_target_pairs={{0,1},{1,0},{2,3},{3,2},{4,5},{5,4},{6,7},{7,6},{8,9},{9,8},{10,11... | collective-permute-start | bytes 6291464 | tf_op jit(solution)/shard_map/ppermute | solution.py:854
  243.6 42.4 %collective-permute-start.16 = (bf16[8,288,384]{2,1,0:T(8,128)(2,1)}, bf16[8,288,384]{2,1,0:T(8,128)(2,1)}, u32[]{:S(2)}, u32[]{:S(2)}) collective-permute-start(bf16[8,288,384]{2,1,0:T(8,128)(2,1)} %get-tuple-element.197), channel_id=1, source_target_pairs={{0,16},{16,0},{1,17},{17,1},{2,18},{18,2},{3,19},{19,3},{4,20},{20... | collective-permute-start | bytes 5308424 | tf_op jit(solution)/shard_map/ppermute | solution.py:850
  308.7 27.9 %collective-permute-start.19 = (bf16[2,2,4,16,16,512]{5,4,3,2,1,0:T(8,128)(2,1)}, bf16[2,2,4,16,16,512]{5,4,3,2,1,0:T(8,128)(2,1)}, u32[]{:S(2)}, u32[]{:S(2)}) collective-permute-start(bf16[2,2,4,16,16,512]{5,4,3,2,1,0:T(8,128)(2,1)} %get-tuple-element.220), channel_id=1, source_target_pairs={{0,1},{1,0},{2,3},{3,2},{4,5},{5,4},{6,7},{7,6},{8,9},{9,8},{10,11... | collective-permute-start | bytes 12582920 | tf_op jit(solution)/shard_map/ppermute | solution.py:854
  309.2 26.7 %collective-permute-start.18 = (bf16[4,288,384]{2,1,0:T(8,128)(2,1)S(1)}, bf16[4,288,384]{2,1,0:T(8,128)(2,1)S(1)}, u32[]{:S(2)}, u32[]{:S(2)}) collective-permute-start(bf16[4,288,384]{2,1,0:T(8,128)(2,1)S(1)} %copy-done.78), channel_id=1, source_target_pairs={{0,2},{1,3},{2,0},{3,1},{4,6},{5,7},{6,4},{7,5},{8,10},{9,11},{10,... | collective-permute-start | bytes 2654216 | tf_op jit(solution)/shard_map/ppermute | solution.py:854
  335.9 73.4 %collective-permute-start.21 = (bf16[8,384,384]{2,1,0:T(8,128)(2,1)}, bf16[8,384,384]{2,1,0:T(8,128)(2,1)}, u32[]{:S(2)}, u32[]{:S(2)}) collective-permute-start(bf16[8,384,384]{2,1,0:T(8,128)(2,1)} %get-tuple-element.234), channel_id=1, source_target_pairs={{0,16},{16,0},{1,17},{17,1},{2,18},{18,2},{3,19},{19,3},{4,20},{20... | collective-permute-start | bytes 7077896 | tf_op jit(solution)/shard_map/ppermute | solution.py:850
  342.7 70.9 %collective-permute-start.23 = (bf16[2,4,16,16,512]{4,3,2,1,0:T(8,128)(2,1)}, bf16[2,4,16,16,512]{4,3,2,1,0:T(8,128)(2,1)}, u32[]{:S(2)}, u32[]{:S(2)}) collective-permute-start(bf16[2,4,16,16,512]{4,3,2,1,0:T(8,128)(2,1)} %get-tuple-element.246), channel_id=1, source_target_pairs={{0,2},{1,3},{2,0},{3,1},{4,6},{5,7},{6,4},{7,5},{8,10},{9,11},{10,... | collective-permute-start | bytes 6291464 | tf_op jit(solution)/shard_map/ppermute | solution.py:854
  344.2 30.2 %collective-permute-start.20 = (bf16[2,288,384]{2,1,0:T(8,128)(2,1)}, bf16[2,288,384]{2,1,0:T(8,128)(2,1)}, u32[]{:S(2)}, u32[]{:S(2)}) collective-permute-start(bf16[2,288,384]{2,1,0:T(8,128)(2,1)} %get-tuple-element.227), channel_id=1, source_target_pairs={{0,4},{1,5},{2,6},{3,7},{4,0},{5,1},{6,2},{7,3},{8,12},{9,13},{10,... | collective-permute-start | bytes 1327112 | tf_op jit(solution)/shard_map/ppermute | solution.py:1153
  394.4 45.1 %collective-permute-start.26 = (bf16[2,4,4,128,128]{4,3,2,1,0:T(8,128)(2,1)}, bf16[2,4,4,128,128]{4,3,2,1,0:T(8,128)(2,1)S(1)}, u32[]{:S(2)}, u32[]{:S(2)}) collective-permute-start(bf16[2,4,4,128,128]{4,3,2,1,0:T(8,128)(2,1)} %get-tuple-element.258), channel_id=1, source_target_pairs={{0,1},{1,0},{2,3},{3,2},{4,5},{5,4},{6,7},{7,6},{8,9},{9,8},{10,11... | collective-permute-start | bytes 3145736 | tf_op jit(solution)/shard_map/ppermute | solution.py:854
  415.7 40.7 %collective-permute-start.32 = (bf16[4,16,16,512]{3,2,1,0:T(8,128)(2,1)S(1)}, bf16[4,16,16,512]{3,2,1,0:T(8,128)(2,1)S(1)}, u32[]{:S(2)}, u32[]{:S(2)}) collective-permute-start(bf16[4,16,16,512]{3,2,1,0:T(8,128)(2,1)S(1)} %get-tuple-element.274), channel_id=1, source_target_pairs={{0,16},{16,0},{1,17},{17,1},{2,18},{18,2},{3,19},{19,3},{4,20},{20... | collective-permute-start | bytes 3145736 | tf_op jit(solution)/shard_map/ppermute | solution.py:850
  417.3 39.1 %collective-permute-start.29 = (bf16[4,384,384]{2,1,0:T(8,128)(2,1)}, bf16[4,384,384]{2,1,0:T(8,128)(2,1)}, u32[]{:S(2)}, u32[]{:S(2)}) collective-permute-start(bf16[4,384,384]{2,1,0:T(8,128)(2,1)} %copy-done.76), channel_id=1, source_target_pairs={{0,2},{1,3},{2,0},{3,1},{4,6},{5,7},{6,4},{7,5},{8,10},{9,11},{10,... | collective-permute-start | bytes 3538952 | tf_op jit(solution)/shard_map/ppermute | solution.py:854
  440.1 16.4 %collective-permute-start.31 = (bf16[4,4,128,128]{3,2,1,0:T(8,128)(2,1)S(1)}, bf16[4,4,128,128]{3,2,1,0:T(8,128)(2,1)S(1)}, u32[]{:S(2)}, u32[]{:S(2)}) collective-permute-start(bf16[4,4,128,128]{3,2,1,0:T(8,128)(2,1)S(1)} %get-tuple-element.272), channel_id=1, source_target_pairs={{0,2},{1,3},{2,0},{3,1},{4,6},{5,7},{6,4},{7,5},{8,10},{9,11},{10,... | collective-permute-start | bytes 1572872 | tf_op jit(solution)/shard_map/ppermute | solution.py:854
  460.4 31.3 %collective-permute-start.35 = (bf16[4,288,384]{2,1,0:T(8,128)(2,1)S(1)}, bf16[4,288,384]{2,1,0:T(8,128)(2,1)S(1)}, u32[]{:S(2)}, u32[]{:S(2)}) collective-permute-start(bf16[4,288,384]{2,1,0:T(8,128)(2,1)S(1)} %get-tuple-element.279.refs_4_), channel_id=1, source_target_pairs={{0,2},{1,3},{2,0},{3,1},{4,6},{5,7},{6,4},{7,5},{8,10},{9,11},{10,... | collective-permute-start | bytes 2654216 | tf_op jit(solution)/shard_map/ppermute | solution.py:854
  461.0 30.7 %collective-permute-start.33 = (bf16[2,384,384]{2,1,0:T(8,128)(2,1)S(1)}, bf16[2,384,384]{2,1,0:T(8,128)(2,1)S(1)}, u32[]{:S(2)}, u32[]{:S(2)}) collective-permute-start(bf16[2,384,384]{2,1,0:T(8,128)(2,1)S(1)} %get-tuple-element.276), channel_id=1, source_target_pairs={{0,4},{1,5},{2,6},{3,7},{4,0},{5,1},{6,2},{7,3},{8,12},{9,13},{10,... | collective-permute-start | bytes 1769480 | tf_op jit(solution)/shard_map/ppermute | solution.py:1153
  461.0 30.7 %collective-permute-start.37 = (bf16[2,16,16,512]{3,2,1,0:T(8,128)(2,1)S(1)}, bf16[2,16,16,512]{3,2,1,0:T(8,128)(2,1)S(1)}, u32[]{:S(2)}, u32[]{:S(2)}) collective-permute-start(bf16[2,16,16,512]{3,2,1,0:T(8,128)(2,1)S(1)} %get-tuple-element.283), channel_id=1, source_target_pairs={{0,4},{1,5},{2,6},{3,7},{4,0},{5,1},{6,2},{7,3},{8,12},{9,13},{10,... | collective-permute-start | bytes 1572872 | tf_op jit(solution)/shard_map/ppermute | solution.py:1153
  466.5 25.2 %collective-permute-start.36 = (bf16[2,4,128,128]{3,2,1,0:T(8,128)(2,1)S(1)}, bf16[2,4,128,128]{3,2,1,0:T(8,128)(2,1)S(1)}, u32[]{:S(2)}, u32[]{:S(2)}) collective-permute-start(bf16[2,4,128,128]{3,2,1,0:T(8,128)(2,1)S(1)} %get-tuple-element.281), channel_id=1, source_target_pairs={{0,4},{1,5},{2,6},{3,7},{4,0},{5,1},{6,2},{7,3},{8,12},{9,13},{10,... | collective-permute-start | bytes 786440 | tf_op jit(solution)/shard_map/ppermute | solution.py:1153
  466.5 16.6 %collective-permute-start.34 = (bf16[4,32,384]{2,1,0:T(8,128)(2,1)S(1)}, bf16[4,32,384]{2,1,0:T(8,128)(2,1)S(1)}, u32[]{:S(2)}, u32[]{:S(2)}) collective-permute-start(bf16[4,32,384]{2,1,0:T(8,128)(2,1)S(1)} %get-tuple-element.278), channel_id=1, source_target_pairs={{0,2},{1,3},{2,0},{3,1},{4,6},{5,7},{6,4},{7,5},{8,10},{9,11},{10,... | collective-permute-start | bytes 294920 | tf_op jit(solution)/shard_map/ppermute | solution.py:854
  493.7 55.5 %collective-permute-start.47 = (bf16[8,288,384]{2,1,0:T(8,128)(2,1)}, bf16[8,288,384]{2,1,0:T(8,128)(2,1)S(1)}, u32[]{:S(2)}, u32[]{:S(2)}) collective-permute-start(bf16[8,288,384]{2,1,0:T(8,128)(2,1)} %get-tuple-element.308.own), channel_id=1, source_target_pairs={{0,1},{1,0},{2,3},{3,2},{4,5},{5,4},{6,7},{7,6},{8,9},{9,8},{10,11... | collective-permute-start | bytes 5308424 | tf_op jit(solution)/shard_map/ppermute | solution.py:854
  493.7 33.2 %collective-permute-start.38 = (bf16[1,384,384]{2,1,0:T(8,128)(2,1)S(1)}, bf16[1,384,384]{2,1,0:T(8,128)(2,1)S(1)}, u32[]{:S(2)}, u32[]{:S(2)}) collective-permute-start(bf16[1,384,384]{2,1,0:T(8,128)(2,1)S(1)} %get-tuple-element.285), channel_id=1, source_target_pairs={{0,8},{1,9},{2,10},{3,11},{4,12},{5,13},{6,14},{7,15},{8,0},{9,1},... | collective-permute-start | bytes 884744 | tf_op jit(solution)/shard_map/ppermute | solution.py:1153
  493.9 33.1 %collective-permute-start.41 = (bf16[1,16,16,512]{3,2,1,0:T(8,128)(2,1)S(1)}, bf16[1,16,16,512]{3,2,1,0:T(8,128)(2,1)S(1)}, u32[]{:S(2)}, u32[]{:S(2)}) collective-permute-start(bf16[1,16,16,512]{3,2,1,0:T(8,128)(2,1)S(1)} %get-tuple-element.291), channel_id=1, source_target_pairs={{0,8},{1,9},{2,10},{3,11},{4,12},{5,13},{6,14},{7,15},{8,0},{9,1},... | collective-permute-start | bytes 786440 | tf_op jit(solution)/shard_map/ppermute | solution.py:1153
  496.7 30.3 %collective-permute-start.40 = (bf16[1,4,128,128]{3,2,1,0:T(8,128)(2,1)S(1)}, bf16[1,4,128,128]{3,2,1,0:T(8,128)(2,1)S(1)}, u32[]{:S(2)}, u32[]{:S(2)}) collective-permute-start(bf16[1,4,128,128]{3,2,1,0:T(8,128)(2,1)S(1)} %get-tuple-element.289), channel_id=1, source_target_pairs={{0,8},{1,9},{2,10},{3,11},{4,12},{5,13},{6,14},{7,15},{8,0},{9,1},... | collective-permute-start | bytes 393224 | tf_op jit(solution)/shard_map/ppermute | solution.py:1153
  528.8 16.4 %collective-permute-start.42 = (bf16[1,384,384]{2,1,0:T(8,128)(2,1)}, bf16[1,384,384]{2,1,0:T(8,128)(2,1)S(1)}, u32[]{:S(2)}, u32[]{:S(2)}) collective-permute-start(bf16[1,384,384]{2,1,0:T(8,128)(2,1)} %copy-done.54), channel_id=1, source_target_pairs={{0,8},{1,9},{2,10},{3,11},{4,12},{5,13},{6,14},{7,15},{8,0},{9,1},... | collective-permute-start | bytes 884744 | tf_op jit(solution)/shard_map/ppermute | solution.py:1153
  528.8 16.3 %collective-permute-start.43 = (bf16[1,32,384]{2,1,0:T(8,128)(2,1)}, bf16[1,32,384]{2,1,0:T(8,128)(2,1)S(1)}, u32[]{:S(2)}, u32[]{:S(2)}) collective-permute-start(bf16[1,32,384]{2,1,0:T(8,128)(2,1)} %copy-done.79), channel_id=1, source_target_pairs={{0,8},{1,9},{2,10},{3,11},{4,12},{5,13},{6,14},{7,15},{8,0},{9,1},... | collective-permute-start | bytes 73736 | tf_op jit(solution)/shard_map/ppermute | solution.py:1153
  545.3 15.9 %collective-permute-start.44 = (bf16[2,384,384]{2,1,0:T(8,128)(2,1)S(1)}, bf16[2,384,384]{2,1,0:T(8,128)(2,1)S(1)}, u32[]{:S(2)}, u32[]{:S(2)}) collective-permute-start(bf16[2,384,384]{2,1,0:T(8,128)(2,1)S(1)} %get-tuple-element.305.refs_0_), channel_id=1, source_target_pairs={{0,4},{1,5},{2,6},{3,7},{4,0},{5,1},{6,2},{7,3},{8,12},{9,13},{10,... | collective-permute-start | bytes 1769480 | tf_op jit(solution)/shard_map/ppermute | solution.py:1153
  561.9 29.2 %collective-permute-start.51 = (bf16[4,384,384]{2,1,0:T(8,128)(2,1)S(1)}, bf16[4,384,384]{2,1,0:T(8,128)(2,1)S(1)}, u32[]{:S(2)}, u32[]{:S(2)}) collective-permute-start(bf16[4,384,384]{2,1,0:T(8,128)(2,1)S(1)} %get-tuple-element.321.refs_0_), channel_id=1, source_target_pairs={{0,2},{1,3},{2,0},{3,1},{4,6},{5,7},{6,4},{7,5},{8,10},{9,11},{10,... | collective-permute-start | bytes 3538952 | tf_op jit(solution)/shard_map/ppermute | solution.py:854
  568.8 22.3 %collective-permute-start.50 = (bf16[4,32,384]{2,1,0:T(8,128)(2,1)S(1)}, bf16[4,32,384]{2,1,0:T(8,128)(2,1)S(1)}, u32[]{:S(2)}, u32[]{:S(2)}) collective-permute-start(bf16[4,32,384]{2,1,0:T(8,128)(2,1)S(1)} %exchange.24.refs_2_), channel_id=1, source_target_pairs={{0,2},{1,3},{2,0},{3,1},{4,6},{5,7},{6,4},{7,5},{8,10},{9,11},{10,... | collective-permute-start | bytes 294920 | tf_op jit(solution)/shard_map/ppermute | solution.py:854
  (149 other events, 1717.9 us)

commit v3 on v2

--- a/solution.py
+++ b/solution.py
@@ -33,7 +33,7 @@
 
 
 def sigmoid(values):
-    return jax.nn.sigmoid(values)
+    return 0.5 * jnp.tanh(0.5 * values) + 0.5
 
 
 def normalise(values):
@@ -75,35 +75,72 @@
     return pl.BlockSpec(member.shape, lambda *_: (0,) * rank)
 
 
-def atom_forward_kernel(
+def conditioning(single, cond_gain, cond_weight, cond_bias, first, last):
+    unit, _ = normalise(wide(single[...]))
+    normed = low(unit * wide(cond_gain[...]))
+    return product(normed, cond_weight[:, first:last]) + wide(cond_bias[:, first:last])
+
+
+def atom_project_kernel(
+    features, single, cond_gain, cond_weight, cond_bias, proj_weight, query_bias, projections
+):
+    width = features.shape[1]
+    pieces = conditioning(single, cond_gain, cond_weight, cond_bias, 0, 2 * width)
+    unit, _ = normalise(wide(features[...]))
+    normed_one = low(unit * sigmoid(pieces[:, :width]) + pieces[:, width:])
+    raw = product(normed_one, proj_weight[...])
+    projections[:, :width] = low(raw[:, :width] + wide(query_bias[...]))
+    projections[:, width:] = low(raw[:, width:])
+
+
+def atom_project(features, single, weights):
+    atoms, width = features.shape
+    gain, cond, offset, proj, query = weights[:5]
+    flat = [gain[None], cond, offset[None], proj, query[None]]
+    rows = 2 * ATOM_ROWS
+    return pl.pallas_call(
+        atom_project_kernel,
+        grid=(atoms // rows,),
+        in_specs=[pl.BlockSpec((rows, width), lambda i: (i, 0))] * 2
+        + [full_spec(member) for member in flat],
+        out_specs=pl.BlockSpec((rows, 4 * width), lambda i: (i, 0)),
+        out_shape=jax.ShapeDtypeStruct((atoms, 4 * width), LOWTYPE),
+        cost_estimate=takes(2),
+        compiler_params=pltpu.CompilerParams(
+            dimension_semantics=("arbitrary",), vmem_limit_bytes=32 * MEBI
+        ),
+        name="atom_project",
+    )(features, single, *flat)
+
+
+def atom_attend_kernel(
+    last_part,
     starts,
     place,
+    firsts,
     features,
     single,
     token_rows,
+    projections,
     bias_own,
     bias_other,
     cond_gain,
     cond_weight,
     cond_bias,
-    proj_weight,
-    query_bias,
     out_weight,
     gu_weight,
     down_weight,
     gather_weight,
-    pooled,
-    counts,
-    projections,
-    attended,
-    probability,
-    key_wide,
-    value_wide,
-    pool_sum,
-    count_sum,
+    *rest,
 ):
+    if last_part:
+        pool_before, count_before, _, _, pooled, counts, attended, probability = rest[:8]
+    else:
+        pooled, counts, attended, probability = rest[:4]
+    key_wide, value_wide, pool_sum, count_sum = rest[-4:]
     step = pl.program_id(0)
-    blocks = pl.num_programs(0) // 2
+    blocks = pl.num_programs(0)
+    block = step + (blocks if last_part else 0)
     width = features.shape[1]
     _, _, half_group, head_count, span, keys = bias_own.shape
     group = 2 * half_group
@@ -111,87 +148,76 @@
     factor = head_size**-0.5
     half = gu_weight.shape[1] // 2
 
-    def conditioned(rows, first, last):
-        unit, _ = normalise(wide(single[rows, :]))
-        normed = low(unit * wide(cond_gain[...]))
-        return product(normed, cond_weight[:, first:last]) + wide(cond_bias[:, first:last])
-
-    @pl.when(step < blocks)
+    @pl.when(step == 0)
     def _():
-        rows = pl.ds(pl.multiple_of(step * ATOM_ROWS, ATOM_ROWS), ATOM_ROWS)
-        pieces = conditioned(rows, 0, 2 * width)
-        unit, _ = normalise(wide(features[rows, :]))
-        normed_one = low(unit * sigmoid(pieces[:, :width]) + pieces[:, width:])
-        raw = product(normed_one, proj_weight[...])
-        queries = low(raw[:, :width] + wide(query_bias[...]))
-        rest = low(raw[:, width:])
-        projections[rows, :width] = queries
-        projections[rows, width:] = rest
-        key_wide[rows, :] = wide(rest[:, :width])
-        value_wide[rows, :] = wide(rest[:, width : 2 * width])
-
-    @pl.when(step >= blocks)
+        key_wide[...] = wide(projections[:, width : 2 * width])
+        value_wide[...] = wide(projections[:, 2 * width : 3 * width])
+
+    rows = pl.ds(pl.multiple_of(block * ATOM_ROWS, ATOM_ROWS), ATOM_ROWS)
+    masks = head_masks(head_count, head_size, width, LOWTYPE)
+    wide_masks = head_masks(head_count, head_size, width, WIDE)
+    query_rows = projections[rows, :width]
+    value_wins, all_scores, chances, parts = [], [], [], []
+    for u in range(group):
+        start = starts[block * group + u]
+        key_win = low(key_wide[pl.ds(start, keys), :])
+        value_wins.append(low(value_wide[pl.ds(start, keys), :]))
+        query_win = query_rows[u * span : (u + 1) * span]
+        stacked = jnp.concatenate([query_win * mask for mask in masks], axis=0)
+        all_scores.append(product_right(stacked, key_win))
+    for u in range(group):
+        own, other = bias_own[0, 0, u % half_group], bias_other[0, 0, u % half_group]
+        bias = jnp.where(place[3] == u // half_group, own, other)
+        scores = all_scores[u] * factor + wide(bias.reshape(head_count * span, keys))
+        exponent = jnp.exp(scores - jnp.max(scores, axis=-1, keepdims=True))
+        chance = low(exponent * (1.0 / jnp.sum(exponent, axis=-1, keepdims=True)))
+        probability[u] = chance
+        chances.append(chance)
+    for u in range(group):
+        mixed = product(chances[u], value_wins[u])
+        parts.append(
+            sum(mixed[h * span : (h + 1) * span] * wide_masks[h] for h in range(head_count))
+        )
+    mixed = jnp.concatenate(parts, axis=0)
+    attended[...] = mixed
+    gated = low(mixed * sigmoid(wide(projections[rows, 3 * width :])))
+    pieces = conditioning(
+        single, cond_gain, cond_weight, cond_bias, 2 * width, 6 * width
+    )
+    middle = wide(features[...]) + sigmoid(pieces[:, :width]) * product(
+        gated, out_weight[...]
+    )
+    unit, _ = normalise(middle)
+    normed_two = low(
+        unit * sigmoid(pieces[:, width : 2 * width]) + pieces[:, 2 * width : 3 * width]
+    )
+    gate_up = product(normed_two, gu_weight[...])
+    gate_half = gate_up[:, :half]
+    hidden = low(gate_half * sigmoid(gate_half) * gate_up[:, half:])
+    result = low(middle + sigmoid(pieces[:, 3 * width :]) * product(hidden, down_weight[...]))
+    pre_act = product(result, gather_weight[...])
+    pooled_atoms = low(pre_act * sigmoid(pre_act))
+    reach = ATOM_ROWS + 8
+    first = jnp.minimum(firsts[block] // 8 * 8, pooled.shape[0] - reach)
+    token_ids = token_rows[block]
+    tokens = lax.broadcasted_iota(jnp.int32, (reach, ATOM_ROWS), 0) + first
+    onehot = jnp.where(tokens == token_ids, 1.0, 0.0)
+    part = product(low(onehot), pooled_atoms)
+    part_count = jnp.sum(onehot, axis=1, keepdims=True)
+
+    @pl.when(step == 0)
     def _():
-        block = step - blocks
-        rows = pl.ds(pl.multiple_of(block * ATOM_ROWS, ATOM_ROWS), ATOM_ROWS)
-        masks = head_masks(head_count, head_size, width, LOWTYPE)
-        wide_masks = head_masks(head_count, head_size, width, WIDE)
-        query_rows = projections[rows, :width]
-        parts = []
-        for u in range(group):
-            start = starts[block * group + u]
-            key_win = low(key_wide[pl.ds(start, keys), :])
-            value_win = low(value_wide[pl.ds(start, keys), :])
-            query_win = query_rows[u * span : (u + 1) * span]
-            stacked = jnp.concatenate([query_win * mask for mask in masks], axis=0)
-            scores = product_right(stacked, key_win) * factor
-            own, other = bias_own[0, 0, u % half_group], bias_other[0, 0, u % half_group]
-            bias = jnp.where(place[3] == u // half_group, own, other)
-            scores = scores + wide(bias.reshape(head_count * span, keys))
-            exponent = jnp.exp(scores - jnp.max(scores, axis=-1, keepdims=True))
-            chance = low(exponent / jnp.sum(exponent, axis=-1, keepdims=True))
-            probability[u] = chance
-            mixed = product(chance, value_win)
-            parts.append(
-                sum(mixed[h * span : (h + 1) * span] * wide_masks[h] for h in range(head_count))
-            )
-        mixed = jnp.concatenate(parts, axis=0)
-        attended[rows, :] = mixed
-        gated = low(mixed * sigmoid(wide(projections[rows, 3 * width :])))
-        pieces = conditioned(rows, 2 * width, 6 * width)
-        middle = wide(features[rows, :]) + sigmoid(pieces[:, :width]) * product(
-            gated, out_weight[...]
-        )
-        unit, _ = normalise(middle)
-        normed_two = low(
-            unit * sigmoid(pieces[:, width : 2 * width]) + pieces[:, 2 * width : 3 * width]
-        )
-        gate_up = product(normed_two, gu_weight[...])
-        gate_half = gate_up[:, :half]
-        hidden = low(gate_half * sigmoid(gate_half) * gate_up[:, half:])
-        result = low(middle + sigmoid(pieces[:, 3 * width :]) * product(hidden, down_weight[...]))
-        pre_act = product(result, gather_weight[...])
-        pooled_atoms = low(pre_act * sigmoid(pre_act))
-        token_ids = token_rows[block]
-        tokens = lax.broadcasted_iota(jnp.int32, (pooled.shape[0], ATOM_ROWS), 0)
-        onehot = jnp.where(tokens == token_ids, 1.0, 0.0)
-        part = product(low(onehot), pooled_atoms)
-        part_count = jnp.sum(onehot, axis=1, keepdims=True)
-
-        @pl.when(block == 0)
-        def _():
-            pool_sum[...] = part
-            count_sum[...] = part_count
-
-        @pl.when(block > 0)
-        def _():
-            pool_sum[...] += part
-            count_sum[...] += part_count
-
-        @pl.when(block == blocks - 1)
-        def _():
-            counts[...] = count_sum[...]
-            pooled[...] = low(pool_sum[...] / count_sum[...])
+        pool_sum[...] = pool_before[...] if last_part else jnp.zeros_like(pool_sum)
+        count_sum[...] = count_before[...] if last_part else jnp.zeros_like(count_sum)
+
+    reached = pl.ds(pl.multiple_of(first, 8), reach)
+    pool_sum[reached, :] += part
+    count_sum[reached, :] += part_count
+
+    @pl.when(step == blocks - 1)
+    def _():
+        counts[...] = count_sum[...]
+        pooled[...] = low(pool_sum[...] / count_sum[...]) if last_part else pool_sum[...]
 
 
 def far_at(run, place):
@@ -203,40 +229,50 @@
     return step % 2 ^ place[2], far_at(step // 2, place)
 
 
-def atom_forward(
-    starts, place, features, single, atom_token, bias, weights, gather_weight, length
+def atom_attend(
+    starts, place, features, single, atom_token, projections, bias, weights, gather_weight, length, before
 ):
     atoms, width = features.shape
     blocks = atoms // ATOM_ROWS
+    steps = blocks // 2
     _, _, half_group, head_count, span, keys = bias[0].shape
-    windows = 2 * half_group * blocks
+    group = 2 * half_group
+    windows = group * blocks
     model_width = gather_weight.shape[1]
     token_rows = atom_token.reshape(blocks, 1, ATOM_ROWS)
-    flat = [member[None] if member.ndim == 1 else member for member in weights]
-    whole = [features, single, token_rows]
-
-    def bias_block(i, starts, place):
-        near, far = block_of(jnp.maximum(i - blocks, 0), place)
+    gain, cond, offset, _, _, out, gu, down = weights
+    flat = [gain[None], cond, offset[None], out, gu, down, gather_weight]
+    first = steps if before else 0
+
+    def bias_block(i, starts, place, firsts):
+        near, far = block_of(i + first, place)
         return near, far, 0, 0, 0, 0
 
-    later3 = lambda i, *_: (jnp.maximum(i - blocks, 0), 0, 0)
+    rows = pl.BlockSpec((ATOM_ROWS, width), lambda i, *_: (i + first, 0))
     outs = [
-        jax.ShapeDtypeStruct((length, model_width), LOWTYPE),
+        jax.ShapeDtypeStruct((length, model_width), LOWTYPE if before else WIDE),
         jax.ShapeDtypeStruct((length, 1), WIDE),
-        jax.ShapeDtypeStruct((atoms, 4 * width), LOWTYPE),
         jax.ShapeDtypeStruct((atoms, width), WIDE),
         jax.ShapeDtypeStruct((windows, head_count * span, keys), LOWTYPE),
     ]
+    members = [features, single, token_rows, projections, *bias, *flat]
+    specs = [rows, rows, full_spec(token_rows), full_spec(projections)]
+    specs += [pl.BlockSpec((1, 1, half_group, head_count, span, keys), bias_block)] * 2
+    specs += [full_spec(member) for member in flat]
+    aliases = {}
+    if before:
+        members += before
+        specs += [full_spec(member) for member in before[:2]]
+        specs += [pl.BlockSpec(memory_space=pl.ANY)] * 2
+        aliases = {len(members) + 1 : 2, len(members) + 2 : 3}
     return pl.pallas_call(
-        atom_forward_kernel,
+        functools.partial(atom_attend_kernel, bool(before)),
         grid_spec=pltpu.PrefetchScalarGridSpec(
-            num_scalar_prefetch=2,
-            grid=(2 * blocks,),
-            in_specs=[full_spec(member) for member in whole]
-            + [pl.BlockSpec((1, 1, half_group, head_count, span, keys), bias_block)] * 2
-            + [full_spec(member) for member in flat + [gather_weight]],
-            out_specs=[full_spec(member) for member in outs[:4]]
-            + [pl.BlockSpec((2 * half_group, head_count * span, keys), later3)],
+            num_scalar_prefetch=3,
+            grid=(steps,),
+            in_specs=specs,
+            out_specs=[full_spec(member) for member in outs[:2]]
+            + [rows, pl.BlockSpec((group, head_count * span, keys), lambda i, *_: (i + first, 0, 0))],
             scratch_shapes=[
                 pltpu.VMEM((atoms, width), WIDE),
                 pltpu.VMEM((atoms, width), WIDE),
@@ -245,15 +281,17 @@
             ],
         ),
         out_shape=outs,
-        cost_estimate=takes(40),
+        input_output_aliases=aliases,
+        cost_estimate=takes(2),
         compiler_params=pltpu.CompilerParams(
-            dimension_semantics=("arbitrary",), vmem_limit_bytes=48 * MEBI
-        ),
-        name="atom_forward",
-    )(starts, place, *whole, *bias, *flat, gather_weight)
+            dimension_semantics=("arbitrary",), vmem_limit_bytes=56 * MEBI
+        ),
+        name="atom_attend",
+    )(starts, place, atom_token[::ATOM_ROWS], *members)
 
 
 def atom_tokens_back_kernel(
+    firsts,
     features,
     single,
     token_cols,
@@ -277,6 +315,7 @@
     grad_gu,
     grad_down,
     grad_gather,
+    d_scaled,
 ):
     step = pl.program_id(0)
     blocks = pl.num_programs(0)
@@ -285,6 +324,7 @@
 
     @pl.when(step == 0)
     def _():
+        d_scaled[...] = low(wide(d_tokens[...]) * (1.0 / counts[...]))
         for member in (grad_out, grad_gu, grad_down, grad_gather):
             member[...] = jnp.zeros_like(member)
 
@@ -310,10 +350,11 @@
     result = low(middle + gate_two * down_out)
     pre_act = product(result, gather_weight[...])
 
-    d_scaled = low(wide(d_tokens[...]) / counts[...])
-    tokens = lax.broadcasted_iota(jnp.int32, (ATOM_ROWS, d_tokens.shape[0]), 1)
+    reach = ATOM_ROWS + 16
+    first = jnp.minimum(firsts[step] // 16 * 16, d_tokens.shape[0] - reach)
+    tokens = lax.broadcasted_iota(jnp.int32, (ATOM_ROWS, reach), 1) + first
     onehot = low(jnp.where(tokens == token_cols[...], 1.0, 0.0))
-    d_rows = product(onehot, d_scaled)
+    d_rows = product(onehot, d_scaled[pl.ds(pl.multiple_of(first, 16), reach), :])
     pre_logistic = sigmoid(pre_act)
     d_pre = low(d_rows * (pre_logistic * (1.0 + pre_act * (1.0 - pre_logistic))))
     grad_gather[...] += product_left(result, d_pre)
@@ -397,7 +438,7 @@
     masks = head_masks(head_count, head_size, width, LOWTYPE)
     wide_masks = head_masks(head_count, head_size, width, WIDE)
     query_rows = projections[rows, :width]
-    score_grads, query_grads = [], []
+    held = []
     for u in range(group):
         start = starts[step * group + u]
         cut = slice(u * span, (u + 1) * span)
@@ -407,16 +448,24 @@
         stacked_grad = jnp.concatenate([row_grad[cut] * mask for mask in masks], axis=0)
         stacked_part = jnp.concatenate([row_part[cut] * mask for mask in wide_masks], axis=0)
         row_sum = jnp.sum(stacked_part, axis=-1, keepdims=True)
-        chance = probability[u]
         d_chance = product_right(stacked_grad, value_win)
-        d_scores = low(wide(chance) * (d_chance - row_sum))
-        score_grads.append(d_scores)
-        d_stacked = product(d_scores, key_win) * factor
+        held.append((start, key_win, stacked_query, stacked_grad, row_sum, d_chance))
+    score_grads = [
+        low(wide(probability[u]) * (held[u][5] - held[u][4])) for u in range(group)
+    ]
+    query_grads, key_grads, value_grads = [], [], []
+    for u in range(group):
+        _, key_win, stacked_query, stacked_grad, _, _ = held[u]
+        d_stacked = product(score_grads[u], key_win) * factor
         query_grads.append(
             sum(d_stacked[h * span : (h + 1) * span] * wide_masks[h] for h in range(head_count))
         )
-        d_keys[pl.ds(start, keys), :] += product_left(d_scores, stacked_query) * factor
-        d_values[pl.ds(start, keys), :] += product_left(chance, stacked_grad)
+        key_grads.append(product_left(score_grads[u], stacked_query) * factor)
+        value_grads.append(product_left(probability[u], stacked_grad))
+    for u in range(group):
+        window = pl.ds(held[u][0], keys)
+        d_keys[window, :] += key_grads[u]
+        d_values[window, :] += value_grads[u]
     d_projections[rows, :width] = low(jnp.concatenate(query_grads, axis=0))
     for u in range(half_group):
         first = place[3] == 0
@@ -505,32 +554,36 @@
     ]
 
     def rows_of(member):
-        return pl.BlockSpec((ATOM_ROWS, member.shape[1]), lambda i: (i, 0))
+        return pl.BlockSpec((ATOM_ROWS, member.shape[1]), lambda i, *_: (i, 0))
 
     return pl.pallas_call(
         atom_tokens_back_kernel,
-        grid=(atoms // ATOM_ROWS,),
-        in_specs=[
+        grid_spec=pltpu.PrefetchScalarGridSpec(
+            num_scalar_prefetch=1,
+            grid=(atoms // ATOM_ROWS,),
+            in_specs=[
             rows_of(features),
             rows_of(single),
             rows_of(token_cols),
-            pl.BlockSpec((ATOM_ROWS, width), lambda i: (i, 3)),
+            pl.BlockSpec((ATOM_ROWS, width), lambda i, *_: (i, 3)),
             rows_of(attended),
             full_spec(d_tokens),
             full_spec(counts),
         ]
         + [full_spec(member) for member in flat],
         out_specs=[rows_of(member) for member in outs[:4]] + [full_spec(outs[4])],
+            scratch_shapes=[
+                pltpu.VMEM(member.shape, WIDE) for member in (out, gu, down, gather_weight)
+            ]
+            + [pltpu.VMEM(d_tokens.shape, LOWTYPE)],
+        ),
         out_shape=outs,
-        scratch_shapes=[
-            pltpu.VMEM(member.shape, WIDE) for member in (out, gu, down, gather_weight)
-        ],
         cost_estimate=takes(3),
         compiler_params=pltpu.CompilerParams(
-            dimension_semantics=("arbitrary",), vmem_limit_bytes=48 * MEBI
+            dimension_semantics=("arbitrary",), vmem_limit_bytes=56 * MEBI
         ),
         name="atom_tokens_back",
-    )(features, single, token_cols, projections, attended, d_tokens, counts, *flat)
+    )(atom_token[::ATOM_ROWS], features, single, token_cols, projections, attended, d_tokens, counts, *flat)
 
 
 def atom_attention_back(starts, place, d_attended, stored):
@@ -569,7 +622,7 @@
         out_shape=outs,
         cost_estimate=takes(2),
         compiler_params=pltpu.CompilerParams(
-            dimension_semantics=("arbitrary",), vmem_limit_bytes=48 * MEBI
+            dimension_semantics=("arbitrary",), vmem_limit_bytes=56 * MEBI
         ),
         name="atom_attention_back",
     )(starts, place, projections, attended, probability, d_attended)
@@ -608,6 +661,9 @@
 
 LANES = 128
 GROUP_HEADS = 8
+STAGE = 1
+FORWARD_PARTS = 1
+BACKWARD_PARTS = 1
 
 
 def head_window(head, head_size, total):
@@ -620,15 +676,15 @@
     return jnp.where((lanes >= offset) & (lanes < offset + head_size), 1.0, 0.0).astype(kind)
 
 
-def chosen_rows(place, own, other, head):
+def chosen_rows(place, own, other, head, runs, section_first):
     parts = []
-    for near in range(2):
-        for core in range(2):
-            for section in range(2):
-                at = (near ^ place[2], section ^ place[0])
-                parts.append(
-                    jnp.where(place[3] == core, own[(*at, 0, head)], other[(*at, 0, head)])
-                )
+    for far in runs:
+        for near in range(2):
+            for core in range(2):
+                for section in range(2):
+                    at = [near ^ place[2], section ^ place[0]]
+                    at = (*(at[::-1] if section_first else at), far_at(far, place), head)
+                    parts.append(jnp.where(place[3] == core, own[at], other[at]))
     return jnp.concatenate(parts, axis=0)
 
 
@@ -640,50 +696,53 @@
     head_size = total // heads
     factor = head_size**-0.5
 
-    def attend(own, other):
+    run_count = FAR // FORWARD_PARTS
+    runs = [pl.program_id(1) * run_count + index for index in range(run_count)]
+
+    def score(h):
+        first, offset = head_window(h, head_size, total)
+        cut = slice(first, first + 2 * LANES)
+        return product_right(queries[:, cut] * head_lanes(offset, head_size, LOWTYPE), keys[:, cut])
+
+    def attend(own, other, section_first):
         tiles = [None] * (total // LANES)
-        for h in range(heads):
-            first, offset = head_window(h, head_size, total)
-            cut = slice(first, first + 2 * LANES)
-            mask = head_lanes(offset, head_size, LOWTYPE)
-            scores = product_right(queries[:, cut] * mask, keys[:, cut]) * factor
-            scores = scores + wide(chosen_rows(place, own, other, h))
-            exponent = jnp.exp(scores - jnp.max(scores, axis=-1, keepdims=True))
-            chance = low(exponent * (1.0 / jnp.sum(exponent, axis=-1, keepdims=True)))
-            probability[h] = chance
-            mixed = product(chance, values[:, cut]) * wide(mask)
-            for t in range(2):
-                at = first // LANES + t
-                part = mixed[:, t * LANES : (t + 1) * LANES]
-                tiles[at] = part if tiles[at] is None else tiles[at] + part
+        for start in range(0, heads, STAGE):
+            run = range(start, start + STAGE)
+            raw_scores = [score(h) for h in run]
+            chances = []
+            for h in run:
+                scores = raw_scores[h - start] * factor + wide(
+                    chosen_rows(place, own, other, h, runs, section_first)
+                )
+                exponent = jnp.exp(scores - jnp.max(scores, axis=-1, keepdims=True))
+                chance = low(exponent * (1.0 / jnp.sum(exponent, axis=-1, keepdims=True)))
+                probability[h] = chance
+                chances.append(chance)
+            for h in run:
+                first, offset = head_window(h, head_size, total)
+                mixed = product(chances[h - start], values[:, first : first + 2 * LANES])
+                mixed = mixed * head_lanes(offset, head_size, WIDE)
+                for t in range(2):
+                    at = first // LANES + t
+                    part = mixed[:, t * LANES : (t + 1) * LANES]
+                    tiles[at] = part if tiles[at] is None else tiles[at] + part
         whole = jnp.concatenate(tiles, axis=1)
         attended[...] = whole
         gated[...] = low(whole * sigmoid(wide(gates[...])))
 
     @pl.when(pl.program_id(0) == 0)
     def _():
-        attend(own_a, other_a)
+        attend(own_a, other_a, True)
 
     @pl.when(pl.program_id(0) == 1)
     def _():
-        attend(own_b, other_b)
-
-
-def bias_spec(member, group):
-    shape = member.shape
-    resting = 0 if group else FAR - 1
-
-    def index(g, i, place):
-        run = jnp.where(g == group, i, resting)
-        return 0, 0, far_at(run, place), 0, 0, 0
-
-    return pl.BlockSpec((*shape[:2], 1, *shape[3:]), index)
+        attend(own_b, other_b, False)
 
 
 def token_forward(place, projections, bias):
     length, columns = projections.shape
     width = columns // 4
-    rows = length // FAR
+    rows = length // FORWARD_PARTS
     group_heads = bias[0].shape[3]
     groups = len(bias) // 2
     heads = group_heads * groups
@@ -693,14 +752,14 @@
         token_forward_kernel,
         grid_spec=pltpu.PrefetchScalarGridSpec(
             num_scalar_prefetch=1,
-            grid=(groups, FAR),
+            grid=(groups, FORWARD_PARTS),
             in_specs=[
                 block,
                 pl.BlockSpec((length, total), lambda g, i, _: (0, groups + g)),
                 pl.BlockSpec((length, total), lambda g, i, _: (0, 2 * groups + g)),
                 pl.BlockSpec((rows, total), lambda g, i, _: (i, 3 * groups + g)),
             ]
-            + [bias_spec(member, index // 2) for index, member in enumerate(bias)],
+            + [full_spec(member) for member in bias],
             out_specs=[
                 pl.BlockSpec((group_heads, rows, length), lambda g, i, _: (g, i, 0)),
                 block,
@@ -712,9 +771,9 @@
             jax.ShapeDtypeStruct((length, width), WIDE),
             jax.ShapeDtypeStruct((length, width), LOWTYPE),
         ],
-        cost_estimate=takes(31),
+        cost_estimate=takes(2),
         compiler_params=pltpu.CompilerParams(
-            dimension_semantics=("arbitrary", "arbitrary"), vmem_limit_bytes=48 * MEBI
+            dimension_semantics=("arbitrary", "arbitrary"), vmem_limit_bytes=56 * MEBI
         ),
         name="token_forward",
     )(place, projections, projections, projections, projections, *bias)
@@ -754,31 +813,49 @@
     d_attended = low(grad * gate)
     d_gates = low(grad * mixed * gate * (1.0 - gate))
     row_part = wide(d_attended) * mixed
-    tiles = [None] * (total // LANES)
-    for h in range(heads):
+
+    def chance_grad(h):
         first, offset = head_window(h, head_size, total)
         cut = slice(first, first + 2 * LANES)
         mask = head_lanes(offset, head_size, LOWTYPE)
-        row_sum = jnp.sum(row_part[:, cut] * wide(mask), axis=-1, keepdims=True)
-        head_grad = d_attended[:, cut] * mask
-        chance = probability[h]
-        d_scores = low(wide(chance) * (product_right(head_grad, values[:, cut]) - row_sum))
-        for near in range(2):
-            for section in range(2):
-                at = (near ^ place[2], section ^ place[0], 0, h)
-                pair = []
-                for core in range(2):
-                    start = (4 * near + 2 * core + section) * run
-                    pair.append(d_scores[start : start + run])
-                own[at] = jnp.where(place[3] == 0, pair[0], pair[1])
-                other[at] = jnp.where(place[3] == 0, pair[1], pair[0])
-        part = product(d_scores, keys[:, cut]) * (wide(mask) * factor)
-        for t in range(2):
-            at = first // LANES + t
-            piece = part[:, t * LANES : (t + 1) * LANES]
-            tiles[at] = piece if tiles[at] is None else tiles[at] + piece
-        d_keys[:, cut] += product_left(d_scores, queries[:, cut] * mask)
-        d_values[:, cut] += product_left(chance, head_grad)
+        return product_right(d_attended[:, cut] * mask, values[:, cut])
+
+    tiles = [None] * (total // LANES)
+    for begin in range(0, heads, STAGE):
+        run_heads = range(begin, begin + STAGE)
+        d_chances = [chance_grad(h) for h in run_heads]
+        score_grads = []
+        for h in run_heads:
+            first, offset = head_window(h, head_size, total)
+            cut = slice(first, first + 2 * LANES)
+            row_sum = jnp.sum(
+                row_part[:, cut] * head_lanes(offset, head_size, WIDE), axis=-1, keepdims=True
+            )
+            d_scores = low(wide(probability[h]) * (d_chances[h - begin] - row_sum))
+            score_grads.append(d_scores)
+            for index in range(FAR // BACKWARD_PARTS):
+                far = far_at(step * (FAR // BACKWARD_PARTS) + index, place)
+                for near in range(2):
+                    for section in range(2):
+                        at = (near ^ place[2], section ^ place[0], far, h)
+                        pair = []
+                        for core in range(2):
+                            start = (8 * index + 4 * near + 2 * core + section) * run
+                            pair.append(d_scores[start : start + run])
+                        own[at] = jnp.where(place[3] == 0, pair[0], pair[1])
+                        other[at] = jnp.where(place[3] == 0, pair[1], pair[0])
+        for h in run_heads:
+            first, offset = head_window(h, head_size, total)
+            cut = slice(first, first + 2 * LANES)
+            mask = head_lanes(offset, head_size, LOWTYPE)
+            d_scores = score_grads[h - begin]
+            part = product(d_scores, keys[:, cut]) * (wide(mask) * factor)
+            for t in range(2):
+                at = first // LANES + t
+                piece = part[:, t * LANES : (t + 1) * LANES]
+                tiles[at] = piece if tiles[at] is None else tiles[at] + piece
+            d_keys[:, cut] += product_left(d_scores, queries[:, cut] * mask)
+            d_values[:, cut] += product_left(probability[h], d_attended[:, cut] * mask)
     rows_at = pl.ds(pl.multiple_of(step * rows, rows), rows)
     first = group * total
     d_projections[rows_at, pl.ds(pl.multiple_of(first, LANES), total)] = low(
@@ -801,20 +878,20 @@
 def token_backward(place, projections, probability, attended, d_gated, run):
     length, columns = projections.shape
     width = columns // 4
-    rows = length // FAR
+    rows = length // BACKWARD_PARTS
     heads = probability.shape[0]
     groups = heads // GROUP_HEADS
     total = width // groups
     block = pl.BlockSpec((rows, total), lambda g, i, _: (i, g))
     grad = jax.ShapeDtypeStruct((2, 2, FAR, heads, run, length), LOWTYPE)
     grad_spec = pl.BlockSpec(
-        (2, 2, 1, GROUP_HEADS, run, length), lambda g, i, place: (0, 0, far_at(i, place), g, 0, 0)
+        (2, 2, FAR, GROUP_HEADS, run, length), lambda g, i, place: (0, 0, 0, g, 0, 0)
     )
     return pl.pallas_call(
         token_backward_kernel,
         grid_spec=pltpu.PrefetchScalarGridSpec(
             num_scalar_prefetch=1,
-            grid=(groups, FAR),
+            grid=(groups, BACKWARD_PARTS),
             in_specs=[
                 block,
                 pl.BlockSpec((length, total), lambda g, i, _: (0, groups + g)),
@@ -829,9 +906,9 @@
             scratch_shapes=[pltpu.VMEM((length, total), WIDE)] * 2,
         ),
         out_shape=[grad] * 2 + [jax.ShapeDtypeStruct((length, columns), LOWTYPE)],
-        cost_estimate=takes(8),
+        cost_estimate=takes(3),
         compiler_params=pltpu.CompilerParams(
-            dimension_semantics=("arbitrary", "arbitrary"), vmem_limit_bytes=48 * MEBI
+            dimension_semantics=("arbitrary", "arbitrary"), vmem_limit_bytes=56 * MEBI
         ),
         name="token_backward",
     )(place, projections, projections, projections, projections, probability, attended, d_gated)
@@ -1011,7 +1088,7 @@
             out_specs=pl.BlockSpec(block, lambda i, _: (i, 0, 0, 0)),
         ),
         out_shape=jax.ShapeDtypeStruct((2, *block[1:]), LOWTYPE),
-        cost_estimate=takes(15),
+        cost_estimate=takes(0.5 if weights[0].direct else 3),
         compiler_params=pltpu.CompilerParams(
             dimension_semantics=("arbitrary",), vmem_limit_bytes=48 * MEBI
         ),
@@ -1032,7 +1109,7 @@
             out_specs=[full_spec(out), full_spec(out)],
         ),
         out_shape=[out, out],
-        cost_estimate=takes(20),
+        cost_estimate=takes(0.5 if weights[0].direct else 6),
         compiler_params=pltpu.CompilerParams(
             dimension_semantics=("arbitrary",), vmem_limit_bytes=48 * MEBI
         ),
@@ -1107,6 +1184,12 @@
             rows = kept.shape[0]
             for index, member in enumerate([kept, *got]):
                 out[index * rows : (index + 1) * rows] = member[...]
+        elif axis == "group":
+            rows = kept.shape[0]
+            for side in range(2):
+                out = refs.pop(0)
+                out[:rows] = kept[:, side]
+                out[rows:] = got[0][:, side]
         elif axis == "far":
             rows = got[0].shape[0]
             refs.pop(0)[...] = low(
@@ -1128,6 +1211,8 @@
         kinds.append((axis, len(got)))
         if axis == "join":
             shapes.append(((1 + len(got)) * kept.shape[0], *kept.shape[1:]))
+        elif axis == "group":
+            shapes += [(2 * kept.shape[0], *kept.shape[2:])] * 2
         elif axis == "far":
             shapes.append(got[0].shape)
         elif axis is None:
@@ -1151,18 +1236,6 @@
 def swap_plane(member, distance):
     size = lax.axis_size("dp")
     return lax.ppermute(member, "dp", [(i, i ^ (distance << 2)) for i in range(size)])
-
-
-def far_parts(member):
-    run = member.shape[0] // FAR
-    return [
-        swap_plane(member[index * run : (index + 1) * run], distance)
-        for index, distance in ((1, 2), (2, 1), (3, 3))
-    ]
-
-
-def far_copies(member):
-    return [swap_plane(member, distance) for distance in (2, 1, 3)]
 
 
 def paired(member):
@@ -1212,12 +1285,20 @@
             jax.ShapeDtypeStruct((1, width), WIDE),
         ],
         scratch_shapes=[pltpu.VMEM((length, depth), WIDE)],
-        cost_estimate=takes(15),
+        cost_estimate=takes(3),
         compiler_params=pltpu.CompilerParams(
             dimension_semantics=("arbitrary",), vmem_limit_bytes=32 * MEBI
         ),
         name="vector_back",
     )(d_projected, cond_weight, unit, d_projections)
+
+
+def far_paired(member):
+    return member.reshape(member.shape[0], 2, 2, *member.shape[2:])
+
+
+def by_group(member):
+    return member.reshape(member.shape[0], -1, GROUP_HEADS, *member.shape[2:])
 
 
 TOKEN_ROWS = 256
@@ -1326,7 +1407,7 @@
         ],
         out_specs=[rows_spec(member.shape[1]) for member in outs],
         out_shape=outs,
-        cost_estimate=takes(8),
+        cost_estimate=takes(3),
         compiler_params=pltpu.CompilerParams(
             dimension_semantics=("arbitrary",), vmem_limit_bytes=48 * MEBI
         ),
@@ -1390,7 +1471,7 @@
         ],
         out_specs=[rows_spec(member.shape[1]) for member in outs],
         out_shape=outs,
-        cost_estimate=takes(15),
+        cost_estimate=takes(2),
         compiler_params=pltpu.CompilerParams(
             dimension_semantics=("arbitrary",), vmem_limit_bytes=48 * MEBI
         ),
@@ -1416,21 +1497,6 @@
 def in_turn(member):
     member = jnp.stack([member, swap_bit(member, 3)])
     return jnp.concatenate([member, swap_bit(member, 2)], axis=0)
-
-
-def gather_token_bias(part):
-    groups = part.shape[0] // GROUP_HEADS
-    gathered = []
-    for group in range(groups):
-        runs = in_turn(part[group * GROUP_HEADS : (group + 1) * GROUP_HEADS])
-        if group % 2:
-            runs = jnp.stack([runs, swap_section(runs)])
-            runs = jnp.stack([runs, swap_near(runs)])
-        else:
-            runs = jnp.stack([runs, swap_near(runs)])
-            runs = jnp.stack([runs, swap_section(runs)], axis=1)
-        gathered += [runs, swap_core(runs)]
-    return gathered
 
 
 def halves_sum(kept, got):
@@ -1448,20 +1514,17 @@
     return token_cross, lax.psum_scatter(whole, "dp", scatter_dimension=0, tiled=True)
 
 
-def gather_atom_bias(part):
-    runs = in_turn(part)
-    runs = jnp.stack([runs, swap_near(runs)])
-    return [runs, swap_core(runs)]
-
-
-def token_block_forward(place, token_in, condition, weights, bias):
-    gain, cond_weight, cond_bias, proj_weight, query_bias, out_weight, gu_weight, down_weight = (
-        weights
-    )
-    width = token_in.shape[1]
+def token_conditioning(condition, weights):
+    gain, cond_weight, cond_bias = weights[:3]
     unit_cond, _ = normalise(condition)
     normed = low(unit_cond * wide(gain))
-    projected = product(normed, cond_weight) + wide(cond_bias)
+    return unit_cond, normed, product(normed, cond_weight) + wide(cond_bias)
+
+
+def token_block_forward(place, token_in, conditioned, weights, bias):
+    proj_weight, query_bias, out_weight, gu_weight, down_weight = weights[3:]
+    unit_cond, normed, projected = conditioned
+    width = token_in.shape[1]
     pieces = [projected[:, i * width : (i + 1) * width] for i in range(6)]
     unit_one, spread_one = normalise(token_in)
     normed_one = low(unit_one * sigmoid(pieces[0]) + pieces[1])
@@ -1530,50 +1593,75 @@
 
     rows = pair_repr.shape[0] // 2
     heads = tokpair_weight.shape[1]
+    features = mine(atom_features)
     window_units = atom_units(atom_pairs)
     atom_gained = wide(atompair_gain)[:, None] * wide(atompair_weight)
     atom_part = low(
         jnp.sum(window_units[:, :, None] * atom_gained[None, :, :, None, None], axis=1)
     )
     windows, atom_heads, span, keys = atom_part.shape
-    pair_units = token_units(lax.dynamic_slice_in_dim(pair_repr, section * rows, rows, 0))
+    pair_rows = lax.dynamic_slice_in_dim(pair_repr, section * rows, rows, 0)
+    atom_part, pair_rows = together(atom_part, pair_rows)
+    pair_units = token_units(pair_rows)
     gained = low(wide(tokpair_gain)[:, None] * wide(tokpair_weight))
     token_part = low(
         lax.dot_general(
             gained, pair_units, (((0,), (1,)), ((), ())), preferred_element_type=WIDE
         )
     ).reshape(heads, rows, length)
+    condition = wide(single_repr) + noise_table[mine(noise_index)]
+    unit_cond, normed, projected = token_conditioning(condition, token_block)
     run = length // (8 * FAR)
     direct = lax.axis_size("dp") == 4 * FAR and rows == run
     if direct:
-        place = here
-        atom_bias = gather_atom_bias(atom_part)
-        token_bias = gather_token_bias(token_part)
+        place = jnp.stack([section, far, near, core]).astype(jnp.int32)
+        got_atom = swap_plane(atom_part, 2)
+        token_part, got_atom = together(token_part, got_atom)
+        got_token = swap_plane(token_part, 2)
+        runs = jnp.stack([atom_part, got_atom])
+        runs = jnp.concatenate([runs, swap_plane(runs, 1)])
+        runs, got_token = together(runs, got_token)
+        got_atom = swap_near(runs)
+        token_runs = jnp.stack([token_part, got_token])
+        got_token = swap_plane(token_runs, 1)
+        projections = atom_project(features, atom_single, atom_block)
+        got_atom, got_token, projections, projected = together(
+            got_atom, got_token, projections, projected
+        )
+        runs = jnp.stack([runs, got_atom])
+        atom_bias = [runs, swap_core(runs)]
+        runs_a, runs_b = exchange(("group", by_group(token_runs), by_group(got_token)))
+        runs_a, runs_b, atom_bias[1] = together(runs_a, runs_b, atom_bias[1])
+        got_a, got_b = swap_near(runs_a), swap_section(runs_b)
     else:
-        place = jnp.zeros((5,), jnp.int32)
+        place = jnp.zeros((4,), jnp.int32)
+        projections = atom_project(features, atom_single, atom_block)
         whole = lax.all_gather(atom_part, "dp", axis=0, tiled=True)
         whole = whole.reshape(FAR, 2, 2, -1, atom_heads, span, keys).transpose(2, 1, 0, 3, 4, 5, 6)
         atom_bias = [whole[0], whole[1]]
         whole = lax.all_gather(token_part, both, axis=0).transpose(0, 2, 1, 3)
         whole = whole.reshape(FAR, 2, 2, 2, run, -1, GROUP_HEADS, length)
         whole = whole.transpose(5, 2, 1, 3, 0, 6, 4, 7)
-        token_bias = [whole[g, c] for g in range(whole.shape[0]) for c in range(2)]
-
-    features = mine(atom_features)
-    condition = wide(single_repr) + noise_table[mine(noise_index)]
-    pooled, counts, *atom_stored = atom_forward(
-        window_start,
-        place,
-        features,
-        atom_single,
-        atom_token,
-        atom_bias,
-        atom_block,
-        gather_weight,
-        length,
-    )
+        token_bias = [whole[0, 0].swapaxes(0, 1), whole[0, 1].swapaxes(0, 1), whole[1, 0], whole[1, 1]]
+
+    atom_args = (window_start, place, features, atom_single, atom_token, projections, atom_bias)
+    atom_args += (atom_block, gather_weight, length)
+    before = list(atom_attend(*atom_args, None))
+    if direct:
+        before[0], got_a, got_b = together(before[0], got_a, got_b)
+        runs_a, runs_b = exchange(("join", runs_a, got_a), ("join", runs_b, got_b))
+        before[0], runs_a, runs_b = together(before[0], runs_a, runs_b)
+        got_a, got_b = swap_section(runs_a), swap_near(runs_b)
+    pooled, counts, attended, probability = atom_attend(*atom_args, before)
+    atom_stored = [projections, attended, probability]
+    if direct:
+        pooled, got_a, got_b = together(pooled, got_a, got_b)
+        runs_a, runs_b = exchange(("join", runs_a, got_a), ("join", runs_b, got_b))
+        runs_a = runs_a.reshape(2, 2, FAR, *runs_a.shape[1:])
+        runs_b = runs_b.reshape(2, 2, FAR, *runs_b.shape[1:])
+        token_bias = [runs_a, swap_core(runs_a), runs_b, swap_core(runs_b)]
     output, token_stored = token_block_forward(
-        place, wide(pooled), condition, token_block, token_bias
+        place, wide(pooled), (unit_cond, normed, projected), token_block, token_bias
     )
 
     (
@@ -1600,9 +1688,8 @@
     chunk_a = products(gu_weight.shape, down_weight.shape)
     chunk_b = products(proj_weight.shape, out_weight.shape, cond_weight.shape)
     d_result = mine(cotangent)
-    output_halves = exchange_halves(low(output))
     normed_here = from_here(normed)
-    d_result, output_halves, normed_here = together(d_result, output_halves, normed_here)
+    d_result, normed_here, output_low = together(d_result, normed_here, low(output))
     d_down, d_last, d_gate_up = transition_back(
         d_result, projected, down_out, gate_up, down_weight
     )
@@ -1619,16 +1706,16 @@
     *d_token_bias, d_projections = token_backward(
         place, projections, probability, attended, d_gated, run
     )
+
+    d_projected, d_tokens = input_back(
+        d_projections, projected, unit_one, spread_one, d_middle, d_pieces, d_last, proj_weight
+    )
+    d_projected, got_a = together(d_projected, got_a)
+    keep_a, send_a = exchange((0, paired(keep_a), paired(got_a)))
+    d_projected, send_a, d_token_bias[1] = together(d_projected, send_a, d_token_bias[1])
+    got_a = swap_near(send_a)
     if direct:
         got_bias = swap_core(d_token_bias[1])
-
-    d_projections, got_a = together(d_projections, got_a)
-    keep_a, send_a = exchange((0, paired(keep_a), paired(got_a)))
-    d_projections, send_a = together(d_projections, send_a)
-    got_a = swap_near(send_a)
-    d_projected, d_tokens = input_back(
-        d_projections, projected, unit_one, spread_one, d_middle, d_pieces, d_last, proj_weight
-    )
     members_b = [normed_one, d_projections, gated, d_attn_out, normed_here, d_projected]
     given_b = chunk_given(here, chunk_b, members_b)
     d_projected, given_b = together(d_projected, given_b)
@@ -1636,20 +1723,18 @@
     grad_offset, grad_gain, grad_query = vector_back(
         d_projected, cond_weight, unit_cond, d_projections
     )
+    if direct:
+        grad_query, got_bias = together(grad_query, got_bias)
+        bias, send_bias = exchange((0, d_token_bias[0], got_bias))
+        grad_query, send_bias = together(grad_query, send_bias)
+        got_bias = swap_near(send_bias)
     given_b_there, grad_query = together(given_b_there, grad_query)
     send_b, keep_b = chunk_kept(here, chunk_b, members_b, given_b_there)
     d_tokens, send_b, got_a = together(d_tokens, send_b, got_a)
     got_b = swap_section(send_b)
-
-    entries = [(0, paired(keep_a), paired(got_a))]
-    if direct:
-        entries.append((0, d_token_bias[0], got_bias))
-    keep_a, send_a, *bias = exchange(*entries)
-    d_tokens, send_a, *bias = together(d_tokens, send_a, *bias)
+    keep_a, send_a = exchange((0, paired(keep_a), paired(got_a)))
+    d_tokens, send_a = together(d_tokens, send_a)
     got_a = swap_plane(send_a, 1)
-    if direct:
-        bias, send_bias = bias
-        got_bias = swap_near(send_bias)
     d_attended, d_gates, d_middles, d_atom_pieces, packed_a = atom_tokens_back(
         features, atom_single, atom_token, d_tokens, counts, atom_stored, atom_block, gather_weight
     )
@@ -1662,14 +1747,16 @@
     )
     d_atom_projections, got_b, got_a = together(d_atom_projections, got_b, got_a)
     entries = [(0, paired(keep_b), paired(got_b)), (None, keep_a, got_a)]
-    keep_b, send_b, total_a = exchange(*entries)
+    if direct:
+        entries.append((0, bias, got_bias))
+    keep_b, send_b, total_a, *bias = exchange(*entries)
     total_a = rest_sum(total_a)
-    d_middles, send_b, total_a = together(d_middles, send_b, total_a)
+    d_middles, send_b, total_a, d_atom_bias[1], *bias = together(
+        d_middles, send_b, total_a, d_atom_bias[1], *bias
+    )
     got_b, got_a = swap_near(send_b), swap_plane(total_a, 2)
     if direct:
-        d_middles, got_bias = together(d_middles, got_bias)
-        bias, send_bias = exchange((0, bias, got_bias))
-        d_middles, send_bias = together(d_middles, send_bias)
+        bias, send_bias = bias
         got_bias = swap_section(send_bias)
         got_atom = swap_core(d_atom_bias[1])
     d_features, packed_b, gain, offset, query = atom_features_back(
@@ -1680,21 +1767,18 @@
     chunk_d = products(packed.shape)
     chunk_d[0].direct = True
     given_d = chunk_given(here, chunk_d, [packed])
-    got_d = swap_core(given_d)
     given_d, got_a = together(given_d, got_a)
     entries = [("join", total_a, got_a)]
     if direct:
         entries.append((0, d_atom_bias[0], got_atom))
     total_a, *atom = exchange(*entries)
-    got_d, total_a, *atom = together(got_d, total_a, *atom)
+    given_d, total_a, *atom = together(given_d, total_a, *atom)
+    got_d = swap_core(given_d)
     got_a = swap_plane(total_a, 1)
     if direct:
         atom, send_atom = atom
-        got_atom = swap_near(send_atom)
     send_d, keep_d = chunk_kept(here, chunk_d, [packed], got_d)
     got_d = swap_section(send_d)
-    feature_halves = exchange_halves(low(d_features))
-    got_d, feature_halves = together(got_d, feature_halves)
 
     entries = [
         (0, paired(keep_b), paired(got_b)),
@@ -1702,35 +1786,62 @@
         ("join", total_a, got_a),
     ]
     if direct:
-        entries += [(0, paired(atom), paired(got_atom)), (0, paired(bias), paired(got_bias))]
-    keep_b, send_b, keep_d, send_d, total_a, *atom = exchange(*entries)
+        entries.append((0, paired(bias), paired(got_bias)))
+    keep_b, send_b, keep_d, send_d, total_a, *bias = exchange(*entries)
     got_b, got_d, got_a = swap_plane(send_b, 1), swap_near(send_d), swap_near(total_a)
     if direct:
-        *atom, bias, send_bias = atom
-        got_atom, got_bias = swap_plane(atom[1], 1), swap_plane(send_bias, 1)
-
-    entries = [
-        (0, paired(keep_b), paired(got_b)),
-        (0, paired(keep_d), paired(got_d)),
-        ("join", total_a, got_a),
-    ]
+        bias, send_bias = bias
+        got_bias = swap_plane(send_bias, 1)
+
+    entries = [(0, paired(keep_b), paired(got_b)), (0, paired(keep_d), paired(got_d))]
     if direct:
-        entries += [(0, paired(atom[0]), paired(got_atom)), (0, paired(bias), paired(got_bias))]
-    keep_b, send_b, keep_d, send_d, total_a, *atom = exchange(*entries)
-    got_b, got_d, core_a = swap_plane(send_b, 2), swap_plane(send_d, 1), swap_core(total_a)
+        entries.append((0, paired(bias), paired(got_bias)))
+    keep_b, send_b, keep_d, send_d, *bias = exchange(*entries)
+    got_b, got_d = swap_plane(send_b, 2), swap_plane(send_d, 1)
     if direct:
-        *atom, bias, send_bias = atom
-        got_atom, got_bias = swap_plane(atom[1], 2), swap_plane(send_bias, 2)
+        bias, send_bias = bias
+        got_bias = swap_plane(send_bias, 2)
+        send_d, send_atom = together(send_d, send_atom)
+        got_atom = swap_near(send_atom)
 
     entries = [(None, keep_b, got_b), (0, paired(keep_d), paired(got_d))]
     if direct:
-        entries += [(None, atom[0], got_atom), (None, bias, got_bias)]
-    total_b, keep_d, send_d, *atom = exchange(*entries)
+        entries.append((None, bias, got_bias))
+    total_b, keep_d, send_d, *token_slab = exchange(*entries)
     total_b = rest_sum(total_b)
+    total_b, send_d, output_low, features_low = together(
+        total_b, send_d, output_low, low(d_features)
+    )
     got_b, got_d = swap_plane(total_b, 2), swap_plane(send_d, 2)
+    feature_halves = exchange_halves(features_low)
+    output_halves = exchange_halves(output_low)
     if direct:
-        atom_slab, token_slab = atom
-        token_cross = product(token_slab.reshape(heads, -1), pair_units)
+        token_cross = product(token_slab[0].reshape(heads, -1), pair_units)
+        got_b, token_cross = together(got_b, token_cross)
+
+    entries = [("join", total_b, got_b), (None, keep_d, got_d), ("join", total_a, got_a)]
+    if direct:
+        entries.append((0, paired(atom), paired(got_atom)))
+    total_b, total_d, total_a, *atom = exchange(*entries)
+    total_d = rest_sum(total_d)
+    got_b, got_d = swap_plane(total_b, 1), swap_plane(total_d, 2)
+    if direct:
+        got_atom = swap_plane(atom[1], 1)
+
+    entries = [("join", total_b, got_b), ("join", total_d, got_d)]
+    if direct:
+        entries.append((0, paired(atom[0]), paired(got_atom)))
+    total_b, total_d, *atom = exchange(*entries)
+    total_b, total_d, total_a = together(total_b, total_d, total_a)
+    got_b, got_d, core_a = swap_near(total_b), swap_plane(total_d, 1), swap_core(total_a)
+    entries = [("join", total_d, got_d)]
+    if direct:
+        entries.append((None, atom[0], swap_plane(atom[1], 2)))
+    total_d, *atom = exchange(*entries)
+    total_d, core_a, *atom = together(total_d, core_a, *atom)
+    got_d = swap_near(total_d)
+    if direct:
+        (atom_slab,) = atom
     else:
         token_cross, atom_slab = cross_of_all(d_token_bias, d_atom_bias, both, pair_units, heads)
     atom_slab = atom_slab.reshape(windows, atom_heads, span, keys)
@@ -1738,36 +1849,23 @@
     vectors = [gain, offset, query, grad_gain, grad_offset, grad_query]
     vectors += [token_cross.reshape(1, -1), atom_cross.reshape(1, -1)]
     total = jnp.concatenate(vectors, axis=1)
-    got_b, got_d, total = together(got_b, got_d, total)
-    got = swap_section(total)
-
-    total_b, total_d = exchange(("join", total_b, got_b), (None, keep_d, got_d))
-    total_d = rest_sum(total_d)
-    got_b, got_d = swap_plane(total_b, 1), swap_plane(total_d, 2)
+    total = total + swap_section(total)
+    total = total + swap_plane(total, 1)
+    total = total + swap_plane(total, 2)
+    for bit in more_bits():
+        total = total + swap_bit(total, bit)
+    total = total + swap_core(total)
     grad_gu, grad_down = assemble(here, chunk_a, total_a, core_a)
-    got_b, got_d, got, grad_gu = together(got_b, got_d, got, grad_gu)
-    total = total + got
-
+    got_d, got_b, total, feature_halves, output_halves, grad_gu = together(
+        got_d, got_b, total, feature_halves, output_halves, grad_gu
+    )
     total_b, total_d = exchange(("join", total_b, got_b), ("join", total_d, got_d))
     total_b, total_d, total = together(total_b, total_d, total)
-    got_b, got_d, got = swap_near(total_b), swap_plane(total_d, 1), swap_plane(total, 1)
-    got_d, got = together(got_d, got)
-    total = total + got
-    (total_d,) = exchange(("join", total_d, got_d))
-    total_d, total = together(total_d, total)
-    got_d, got = swap_near(total_d), swap_plane(total, 2)
-    got_d, got_b, got = together(got_d, got_b, got)
-    total = total + got
-    for bit in more_bits():
-        total = total + swap_bit(total, bit)
-    total_b, total_d = exchange(("join", total_b, got_b), ("join", total_d, got_d))
     core_b, core_d, got = swap_core(total_b), swap_core(total_d), swap_near(total)
     core_d, got = together(core_d, got)
-    total = total + got
-    got = swap_core(total)
+    total = (total + got)[0]
     (packed,) = assemble(here, chunk_d, total_d, core_d)
-    core_b, packed, got = together(core_b, packed, got)
-    total = (total + got)[0]
+    core_b, packed, total = together(core_b, packed, total)
     grad_proj, grad_out, grad_cond = assemble(here, chunk_b, total_b, core_b)
 
     atom_width = features.shape[1]

time: 625 us -> 531 us (0.85)
  Pallas kernels: 248 us -> 207 us
  waiting for transfers between devices: 193 us -> 155 us
  starting transfers between devices: 57.6 us -> 49.3 us
    ppermute x30 -> x24, waiting for transfers between devices: 90 us -> 20.6 us  [swap_bit(): lax.ppermute(member, 'dp', [(i, i ^ 1 << bit) for i in range(lax.axis_siz...]
    ppermute x9, waiting for transfers between devices: 16.7 us -> 36.2 us  [swap_section(): return lax.ppermute(member, 'section', [(0, 1), (1, 0)])]
    pallas_call x1, Pallas kernels: 32.8 us -> 16.4 us  [token_forward(): pl.pallas_call(token_forward_kernel, grid_spec=pltpu.PrefetchScalarGridSp...]
    ppermute x18 -> x22, waiting for transfers between devices: 86.4 us -> 98.7 us  [swap_plane(): lax.ppermute(member, 'dp', [(i, i ^ distance << 2) for i in range(size)])]
    pallas_call x2 -> x4, Pallas kernels: 63.3 us -> 51.6 us  [the longest x2 24.9 us: atom_attend(): pl.pallas_call(functools.partial(atom_attend_kernel, bool(before)), grid_...]
    ppermute x30 -> x24, starting transfers between devices: 26 us -> 15.2 us  [swap_bit(): lax.ppermute(member, 'dp', [(i, i ^ 1 << bit) for i in range(lax.axis_siz...]
    another operation x11 -> x5, other arithmetic: 13.1 us -> 2.92 us  [the longest x2 2.21 us: local(): token_runs = jnp.stack([token_part, got_token])]
    pallas_call x1, Pallas kernels: 27.1 us -> 17 us  [token_backward(): pl.pallas_call(token_backward_kernel, grid_spec=pltpu.PrefetchScalarGridS...]
  transfers between devices with their start and end apart: 57 -> 55, of which waited for: 29 -> 31; matrix products, arithmetic and copies ran while one was open for 8% -> 10% of each run, Pallas kernels for 26% -> 26%
where the time goes in v3:
time: 531 us; the launch traced here: 520 us
  Pallas kernels  207 us (39%)
  waiting for transfers between devices  155 us (29%)
  starting transfers between devices  49.3 us (9%)
  local copies, waits for them, and re-layouts  41.5 us (8%)
  other arithmetic  39.8 us (7%)
  matrix products  22.6 us (4%)
    ppermute x22, waiting for transfers between devices, swap_plane(): lax.ppermute(member, 'dp', [(i, i ^ distance << 2) for i in range(size)])  98.7 us
    ppermute x9, waiting for transfers between devices, swap_section(): return lax.ppermute(member, 'section', [(0, 1), (1, 0)])  36.2 us
    pallas_call x16, Pallas kernels, exchange(): pl.pallas_call(functools.partial(exchange_kernel, kinds), grid=(2,), in_s...  25.9 us
    pallas_call x2, Pallas kernels, atom_attend(): pl.pallas_call(functools.partial(atom_attend_kernel, bool(before)), grid_...  24.9 us
    ppermute x22, starting transfers between devices, swap_plane(): lax.ppermute(member, 'dp', [(i, i ^ distance << 2) for i in range(size)])  24.2 us
    pallas_call x1, Pallas kernels, atom_tokens_back(): pl.pallas_call(atom_tokens_back_kernel, grid_spec=pltpu.PrefetchScalarGri...  23.6 us
    dot_general x6, matrix products, product(): return jnp.dot(left, right, preferred_element_type=WIDE)  21.9 us
    unnamed x197, local copies, waits for them, and re-layouts  21.3 us
  transfers between devices with their start and end apart: 55, of which 31 were waited for; matrix products, arithmetic and copies ran while one was open for 10% of the time, Pallas kernels for 26%

profile of v3, /device:TPU:0, one launch (start us, length us, event | category | flops | bytes accessed | tf_op | source)
XLA Modules:
  0.0 520.5 jit_solution(9767307631088226800)
XLA Ops:
  33.2 7.8 %collective-permute-done.1 = bf16[2,4,4,32,128]{4,3,2,1,0:T(8,128)(2,1)S(1)} collective-permute-done((bf16[2,4,4,32,128]{4,3,2,1,0:T(8,128)(2,1)S(1)}, bf16[2,4,4,32,128]{4,3,2,1,0:T(8,128)(2,1)S(1)}, u32[]{:S(2)}, u32[]{:S(2)}) %collective-permute-start.1) | collective-permute-done | bytes 262176 | tf_op jit(solution)/shard_map/ppermute | solution.py:1238
  48.7 5.1 convolution_add_fusion.gate_two.gate_one.scale_two.scale_one
  53.7 5.5 %collective-permute-done.4 = bf16[2,16,16,512]{3,2,1,0:T(8,128)(2,1)S(1)} collective-permute-done((bf16[2,16,16,512]{3,2,1,0:T(8,128)(2,1)S(1)}, bf16[2,16,16,512]{3,2,1,0:T(8,128)(2,1)S(1)}, u32[]{:S(2)}, u32[]{:S(2)}) %collective-permute-start.4) | collective-permute-done | bytes 524320 | tf_op jit(solution)/shard_map/ppermute | solution.py:1238
  67.2 12.2 %atom_attend.2 = (f32[512,768]{1,0:T(8,128)}, f32[512,1]{1,0:T(8,128)}, f32[2048,128]{1,0:T(8,128)}, bf16[64,128,128]{2,1,0:T(8,128)(2,1)}) custom-call(s32[64]{0:T(128)} %starts.5, s32[4]{0:T(128)} %pad_add_fusion.place, s32[8]{0:T(128)} %slice.85.firsts, bf16[2048,128]{1,0:T(8,128)(2,1)} %copy-done.4, bf16[2048,128]{1,0:T(8,128)(2,1)} %single.9, ...), custom_call_target="tpu_custom_call" | custom-call | bytes 7380000 | tf_op jit(solution)/shard_map/atom_attend/pallas_call | solution.py:268
  82.5 12.7 %atom_attend.3 = (bf16[512,768]{1,0:T(8,128)(2,1)}, f32[512,1]{1,0:T(8,128)}, f32[2048,128]{1,0:T(8,128)}, bf16[64,128,128]{2,1,0:T(8,128)(2,1)}) custom-call(s32[64]{0:T(128)} %starts.5, s32[4]{0:T(128)} %pad_add_fusion.place, s32[8]{0:T(128)} %slice.85.firsts, bf16[2048,128]{1,0:T(8,128)(2,1)} %copy-done.4, ...), custom_call_target="tpu_custom_call", output_to_operand_aliasing={{2}: (18, {}), {3}: (19, {})} | custom-call | bytes 7380000 | tf_op jit(solution)/shard_map/atom_attend/pallas_call | solution.py:268
  95.2 10.2 %collective-permute-done.8.refs_1_ = bf16[8,8,16,512]{3,2,1,0:T(8,128)(2,1)S(1)} collective-permute-done((bf16[8,8,16,512]{3,2,1,0:T(8,128)(2,1)S(1)}, bf16[8,8,16,512]{3,2,1,0:T(8,128)(2,1)S(1)}, u32[]{:S(2)}, u32[]{:S(2)}) %collective-permute-start.8) | collective-permute-done | bytes 1048608 | tf_op jit(solution)/shard_map/ppermute | solution.py:927
  114.1 6.3 %add_convert_fusion.queries.keys.values.gates = bf16[512,3072]{1,0:T(8,128)(2,1)} fusion(bf16[512,768]{1,0:T(8,128)(2,1)S(1)} %get-tuple-element.489.refs_0_, bf16[768,3072]{1,0:T(8,128)(2,1)} %proj_weight.4, f32[3072]{0:T(1024)S(1)} %pad_convert_fusion), kind=kOutput, calls=%fused_computation.2 | convolution fusion | flops 2419064832 | bytes 8663040 | tf_op jit(solution)/shard_map/dot_general | solution.py:24
  120.5 16.4 %token_forward.1 = (bf16[16,512,512]{2,1,0:T(8,128)(2,1)}, f32[512,768]{1,0:T(8,128)}, bf16[512,768]{1,0:T(8,128)(2,1)}) custom-call(s32[4]{0:T(128)} %pad_add_fusion.place, bf16[512,3072]{1,0:T(8,128)(2,1)} %add_convert_fusion.queries.keys.values.gates, bf16[512,3072]{1,0:T(8,128)(2,1)} %add_convert_fusion.queries.keys.values.gates, ...), custom_call_target="tpu_custom_call" | custom-call | bytes 7380000 | tf_op jit(solution)/shard_map/token_forward/pallas_call | solution.py:751
  154.3 6.6 %transition_back.1 = (bf16[512,768]{1,0:T(8,128)(2,1)S(1)}, bf16[512,768]{1,0:T(8,128)(2,1)S(1)}, bf16[512,3072]{1,0:T(8,128)(2,1)}) custom-call(bf16[512,768]{1,0:T(8,128)(2,1)S(1)} %dynamic-slice_bitcast_fusion.d_result, f32[512,4608]{1,0:T(8,128)} %convolution_add_fusion.gate_two.gate_one.scale_two.scale_one, f32[512,768]{1,0:T(8,128)S(1)} %get-tuple-element.514.down_out, ...), custom_call_target="tpu_custom_call" | custom-call | bytes 18450000 | tf_op jit(solution)/shard_map/transition_back/pallas_call | solution.py:1334
  160.8 6.6 %chunk_given.3 = bf16[2,8,288,384]{3,2,1,0:T(8,128)(2,1)} custom-call(s32[5]{0:T(128)S(1)} %stack.81.place, bf16[512,768]{1,0:T(8,128)(2,1)S(1)} %get-tuple-element.482.refs_0_, bf16[512,3072]{1,0:T(8,128)(2,1)} %get-tuple-element.260.refs_1_.d_gate_up, bf16[512,1536]{1,0:T(8,128)(2,1)S(1)} %fusion.2.refs_2_, bf16[512,768]{1,0:T(8,128)(2,1)S(1)} %get-tuple-element.256.refs_3_), custom_call_target="tpu_custom_call" | custom-call | bytes 11070000 | tf_op jit(solution)/shard_map/chunk_given/pallas_call | solution.py:1082
  167.5 6.4 %collective-permute-done.12.refs_4_ = bf16[2,8,288,384]{3,2,1,0:T(8,128)(2,1)S(1)} collective-permute-done((bf16[2,8,288,384]{3,2,1,0:T(8,128)(2,1)}, bf16[2,8,288,384]{3,2,1,0:T(8,128)(2,1)S(1)}, u32[]{:S(2)}, u32[]{:S(2)}) %collective-permute-start.12) | collective-permute-done | bytes 3538976 | tf_op jit(solution)/shard_map/ppermute | solution.py:931
  175.7 8.0 %chunk_kept.3 = (bf16[8,288,384]{2,1,0:T(8,128)(2,1)}, bf16[8,288,384]{2,1,0:T(8,128)(2,1)}) custom-call(s32[5]{0:T(128)S(1)} %stack.81.place, bf16[512,768]{1,0:T(8,128)(2,1)S(1)} %get-tuple-element.482.refs_0_, bf16[512,3072]{1,0:T(8,128)(2,1)} %get-tuple-element.260.refs_1_.d_gate_up, bf16[512,1536]{1,0:T(8,128)(2,1)S(1)} %fusion.2.refs_2_, ...), custom_call_target="tpu_custom_call" | custom-call | bytes 22140000 | tf_op jit(solution)/shard_map/chunk_kept/pallas_call | solution.py:1102
  187.2 10.4 %middle_back.1 = (f32[512,768]{1,0:T(8,128)S(1)}, bf16[512,768]{1,0:T(8,128)(2,1)S(1)}, bf16[512,768]{1,0:T(8,128)(2,1)S(1)}, bf16[512,2304]{1,0:T(8,128)(2,1)}) custom-call(bf16[512,768]{1,0:T(8,128)(2,1)S(1)} %dynamic-slice_bitcast_fusion.d_result, f32[512,4608]{1,0:T(8,128)} %convolution_add_fusion.gate_two.gate_one.scale_two.scale_one, ...), custom_call_target="tpu_custom_call" | custom-call | bytes 11070000 | tf_op jit(solution)/shard_map/middle_back/pallas_call | solution.py:1394
  199.3 17.0 %token_backward.1 = (bf16[2,2,4,16,16,512]{5,4,3,2,1,0:T(8,128)(2,1)}, bf16[2,2,4,16,16,512]{5,4,3,2,1,0:T(8,128)(2,1)}, bf16[512,3072]{1,0:T(8,128)(2,1)}) custom-call(s32[4]{0:T(128)} %pad_add_fusion.place, bf16[512,3072]{1,0:T(8,128)(2,1)} %add_convert_fusion.queries.keys.values.gates, bf16[512,3072]{1,0:T(8,128)(2,1)} %add_convert_fusion.queries.keys.values.gates, ...), custom_call_target="tpu_custom_call" | custom-call | bytes 11070000 | tf_op jit(solution)/shard_map/token_backward/pallas_call | solution.py:890
  217.5 8.8 %input_back.1 = (bf16[512,4608]{1,0:T(8,128)(2,1)}, bf16[512,768]{1,0:T(8,128)(2,1)S(1)}) custom-call(bf16[512,3072]{1,0:T(8,128)(2,1)} %get-tuple-element.262.d_projections.refs_1_.d_queries, f32[512,4608]{1,0:T(8,128)} %convolution_add_fusion.gate_two.gate_one.scale_two.scale_one, f32[512,768]{1,0:T(8,128)S(1)} %copy-done.11, ...), custom_call_target="tpu_custom_call" | custom-call | bytes 7380000 | tf_op jit(solution)/shard_map/input_back/pallas_call | solution.py:1459
  230.0 9.3 %chunk_given.4 = bf16[2,8,384,384]{3,2,1,0:T(8,128)(2,1)} custom-call(s32[5]{0:T(128)S(1)} %stack.81.place, bf16[512,768]{1,0:T(8,128)(2,1)S(1)} %get-tuple-element.489.refs_0_, bf16[512,3072]{1,0:T(8,128)(2,1)S(1)} %copy-done.3, bf16[512,768]{1,0:T(8,128)(2,1)S(1)} %copy-done.10, bf16[512,768]{1,0:T(8,128)(2,1)S(1)} %copy-done.17, ...), custom_call_target="tpu_custom_call" | custom-call | bytes 11070000 | tf_op jit(solution)/shard_map/chunk_given/pallas_call | solution.py:1082
  243.1 5.1 vector_back.1
  248.2 4.8 collective-permute-done.15.refs_1_
  255.2 5.0 exchange.20
  261.5 10.9 %chunk_kept.4 = (bf16[8,384,384]{2,1,0:T(8,128)(2,1)}, bf16[8,384,384]{2,1,0:T(8,128)(2,1)}) custom-call(s32[5]{0:T(128)S(1)} %stack.81.place, bf16[512,768]{1,0:T(8,128)(2,1)S(1)} %get-tuple-element.489.refs_0_, bf16[512,3072]{1,0:T(8,128)(2,1)} %get-tuple-element.262.d_projections.refs_1_.d_queries, bf16[512,768]{1,0:T(8,128)(2,1)S(1)} %copy-done.10, ...), custom_call_target="tpu_custom_call" | custom-call | bytes 22140000 | tf_op jit(solution)/shard_map/chunk_kept/pallas_call | solution.py:1102
  278.6 23.6 %atom_tokens_back.1 = (bf16[2048,128]{1,0:T(8,128)(2,1)}, bf16[2048,128]{1,0:T(8,128)(2,1)}, f32[2048,128]{1,0:T(8,128)}, bf16[2048,512]{1,0:T(8,128)(2,1)}, bf16[128,1664]{1,0:T(8,128)(2,1)}) custom-call(s32[8]{0:T(128)} %slice.85.firsts, bf16[2048,128]{1,0:T(8,128)(2,1)} %copy-done.4, bf16[2048,128]{1,0:T(8,128)(2,1)} %single.9, ...), custom_call_target="tpu_custom_call" | custom-call | bytes 11070000 | tf_op jit(solution)/shard_map/atom_tokens_back/pallas_call | solution.py:559
  302.7 11.1 %atom_attention_back.1 = (bf16[2048,384]{1,0:T(8,128)(2,1)}, bf16[2,4,4,128,128]{4,3,2,1,0:T(8,128)(2,1)}, bf16[2,4,4,128,128]{4,3,2,1,0:T(8,128)(2,1)}) custom-call(s32[64]{0:T(128)} %starts.5, s32[4]{0:T(128)} %pad_add_fusion.place, bf16[2048,512]{1,0:T(8,128)(2,1)} %copy-done.2, f32[2048,128]{1,0:T(8,128)} %get-tuple-element.287.attended, ...), custom_call_target="tpu_custom_call" | custom-call | bytes 7380000 | tf_op jit(solution)/shard_map/atom_attention_back/pallas_call | solution.py:607
  314.9 11.4 %collective-permute-done.18 = bf16[8,384,384]{2,1,0:T(8,128)(2,1)} collective-permute-done((bf16[8,384,384]{2,1,0:T(8,128)(2,1)}, bf16[8,384,384]{2,1,0:T(8,128)(2,1)}, u32[]{:S(2)}, u32[]{:S(2)}) %collective-permute-start.18) | collective-permute-done | bytes 2359328 | tf_op jit(solution)/shard_map/ppermute | solution.py:927
  327.7 4.5 exchange.23
  334.4 7.3 %atom_features_back.1 = (f32[2048,128]{1,0:T(8,128)S(1)}, bf16[128,1280]{1,0:T(8,128)(2,1)S(1)}, f32[1,128]{1,0:T(1,128)S(1)}, f32[1,768]{1,0:T(1,128)S(1)}, f32[1,128]{1,0:T(1,128)S(1)}) custom-call(bf16[2048,128]{1,0:T(8,128)(2,1)S(1)} %copy-done.5, bf16[2048,128]{1,0:T(8,128)(2,1)S(1)} %copy-done.9, bf16[2048,384]{1,0:T(8,128)(2,1)S(1)} %copy-done.25, ...), custom_call_target="tpu_custom_call" | custom-call | bytes 1845000 | tf_op jit(solution)/shard_map/atom_features_back/pallas_call | solution.py:643
  342.5 4.4 collective-permute-done.22.refs_1_
  351.7 8.0 %collective-permute-done.27 = bf16[4,16,16,512]{3,2,1,0:T(8,128)(2,1)} collective-permute-done((bf16[4,16,16,512]{3,2,1,0:T(8,128)(2,1)S(1)}, bf16[4,16,16,512]{3,2,1,0:T(8,128)(2,1)}, u32[]{:S(2)}, u32[]{:S(2)}) %collective-permute-start.27) | collective-permute-done | bytes 1048608 | tf_op jit(solution)/shard_map/ppermute | solution.py:927
  372.2 19.2 %collective-permute-done.30 = bf16[2,16,16,512]{3,2,1,0:T(8,128)(2,1)S(1)} collective-permute-done((bf16[2,16,16,512]{3,2,1,0:T(8,128)(2,1)S(1)}, bf16[2,16,16,512]{3,2,1,0:T(8,128)(2,1)S(1)}, u32[]{:S(2)}, u32[]{:S(2)}) %collective-permute-start.30) | collective-permute-done | bytes 524320 | tf_op jit(solution)/shard_map/ppermute | solution.py:1238
  403.9 13.9 %collective-permute-done.33.refs_5_ = bf16[1,16,16,512]{3,2,1,0:T(8,128)(2,1)S(1)} collective-permute-done((bf16[1,16,16,512]{3,2,1,0:T(8,128)(2,1)S(1)}, bf16[1,16,16,512]{3,2,1,0:T(8,128)(2,1)S(1)}, u32[]{:S(2)}, u32[]{:S(2)}) %collective-permute-start.33) | collective-permute-done | bytes 262176 | tf_op jit(solution)/shard_map/ppermute | solution.py:1238
  424.1 9.3 %collective-permute-done.34.refs_1_ = bf16[1,384,384]{2,1,0:T(8,128)(2,1)S(1)} collective-permute-done((bf16[1,384,384]{2,1,0:T(8,128)(2,1)S(1)}, bf16[1,384,384]{2,1,0:T(8,128)(2,1)S(1)}, u32[]{:S(2)}, u32[]{:S(2)}) %collective-permute-start.34) | collective-permute-done | bytes 294944 | tf_op jit(solution)/shard_map/ppermute | solution.py:1238
  437.6 17.1 %collective-permute-done.39.refs_3_ = bf16[1,32,384]{2,1,0:T(8,128)(2,1)S(1)} collective-permute-done((bf16[1,32,384]{2,1,0:T(8,128)(2,1)S(1)}, bf16[1,32,384]{2,1,0:T(8,128)(2,1)S(1)}, u32[]{:S(2)}, u32[]{:S(2)}) %collective-permute-start.39) | collective-permute-done | bytes 24608 | tf_op jit(solution)/shard_map/ppermute | solution.py:1238
  506.5 6.5 %assemble.5 = (f32[384,3072]{1,0:T(8,128)}, f32[384,768]{1,0:T(8,128)}, f32[192,4608]{1,0:T(8,128)}) custom-call(s32[5]{0:T(128)S(1)} %stack.81.place, bf16[8,384,384]{2,1,0:T(8,128)(2,1)S(1)} %copy-done.20, bf16[8,384,384]{2,1,0:T(8,128)(2,1)} %collective-permute-done.52.other), custom_call_target="tpu_custom_call" | custom-call | bytes 7380000 | tf_op jit(solution)/shard_map/assemble/pallas_call | solution.py:1136
  (416 shorter events, 204.5 us)
Async XLA Ops:
  8.3 21.7 %collective-permute-start = (bf16[4,4,32,128]{3,2,1,0:T(8,128)(2,1)S(1)}, bf16[4,4,32,128]{3,2,1,0:T(8,128)(2,1)S(1)}, u32[]{:S(2)}, u32[]{:S(2)}) collective-permute-start(bf16[4,4,32,128]{3,2,1,0:T(8,128)(2,1)S(1)} %multiply_reduce_fusion.2), channel_id=1, source_target_pairs={{0,8},{1,9},{2,10},{3,11},{4,12},{5,13},{6,14},{7,15},{8,0},{9,1},... | collective-permute-start | bytes 393224 | tf_op jit(solution)/shard_map/ppermute | solution.py:1238
  31.7 14.3 %collective-permute-start.2 = (bf16[16,16,512]{2,1,0:T(8,128)(2,1)}, bf16[16,16,512]{2,1,0:T(8,128)(2,1)S(1)}, u32[]{:S(2)}, u32[]{:S(2)}) collective-permute-start(bf16[16,16,512]{2,1,0:T(8,128)(2,1)} %bitcast.77), channel_id=1, source_target_pairs={{0,8},{1,9},{2,10},{3,11},{4,12},{5,13},{6,14},{7,15},{8,0},{9,1},... | collective-permute-start | bytes 786440 | tf_op jit(solution)/shard_map/ppermute | solution.py:1238
  62.2 17.2 %collective-permute-start.6 = (bf16[4,8,16,512]{3,2,1,0:T(8,128)(2,1)S(1)}, bf16[4,8,16,512]{3,2,1,0:T(8,128)(2,1)S(1)}, u32[]{:S(2)}, u32[]{:S(2)}) collective-permute-start(bf16[4,8,16,512]{3,2,1,0:T(8,128)(2,1)S(1)} %get-tuple-element.231.refs_0_), channel_id=1, source_target_pairs={{0,2},{1,3},{2,0},{3,1},{4,6},{5,7},{6,4},{7,5},{8,10},{9,11},{10,... | collective-permute-start | bytes 1572872 | tf_op jit(solution)/shard_map/ppermute | solution.py:931
  63.8 15.6 %collective-permute-start.7 = (bf16[4,8,16,512]{3,2,1,0:T(8,128)(2,1)S(1)}, bf16[4,8,16,512]{3,2,1,0:T(8,128)(2,1)}, u32[]{:S(2)}, u32[]{:S(2)}) collective-permute-start(bf16[4,8,16,512]{3,2,1,0:T(8,128)(2,1)S(1)} %get-tuple-element.232.refs_2_), channel_id=1, source_target_pairs={{0,16},{16,0},{1,17},{17,1},{2,18},{18,2},{3,19},{19,3},{4,20},{20... | collective-permute-start | bytes 1572872 | tf_op jit(solution)/shard_map/ppermute | solution.py:927
  80.8 24.7 %collective-permute-start.8 = (bf16[8,8,16,512]{3,2,1,0:T(8,128)(2,1)S(1)}, bf16[8,8,16,512]{3,2,1,0:T(8,128)(2,1)S(1)}, u32[]{:S(2)}, u32[]{:S(2)}) collective-permute-start(bf16[8,8,16,512]{3,2,1,0:T(8,128)(2,1)S(1)} %get-tuple-element.243.refs_0_), channel_id=1, source_target_pairs={{0,16},{16,0},{1,17},{17,1},{2,18},{18,2},{3,19},{19,3},{4,20},{20... | collective-permute-start | bytes 3145736 | tf_op jit(solution)/shard_map/ppermute | solution.py:927
  81.4 24.4 %collective-permute-start.9 = (bf16[8,8,16,512]{3,2,1,0:T(8,128)(2,1)S(1)}, bf16[8,8,16,512]{3,2,1,0:T(8,128)(2,1)S(1)}, u32[]{:S(2)}, u32[]{:S(2)}) collective-permute-start(bf16[8,8,16,512]{3,2,1,0:T(8,128)(2,1)S(1)} %get-tuple-element.244.refs_2_), channel_id=1, source_target_pairs={{0,2},{1,3},{2,0},{3,1},{4,6},{5,7},{6,4},{7,5},{8,10},{9,11},{10,... | collective-permute-start | bytes 3145736 | tf_op jit(solution)/shard_map/ppermute | solution.py:931
  183.6 43.6 %collective-permute-start.13 = (bf16[8,288,384]{2,1,0:T(8,128)(2,1)}, bf16[8,288,384]{2,1,0:T(8,128)(2,1)}, u32[]{:S(2)}, u32[]{:S(2)}) collective-permute-start(bf16[8,288,384]{2,1,0:T(8,128)(2,1)} %get-tuple-element.269), channel_id=1, source_target_pairs={{0,16},{16,0},{1,17},{17,1},{2,18},{18,2},{3,19},{19,3},{4,20},{20... | collective-permute-start | bytes 5308424 | tf_op jit(solution)/shard_map/ppermute | solution.py:927
  239.3 22.2 %collective-permute-start.14 = (bf16[2,8,384,384]{3,2,1,0:T(8,128)(2,1)}, bf16[2,8,384,384]{3,2,1,0:T(8,128)(2,1)}, u32[]{:S(2)}, u32[]{:S(2)}) collective-permute-start(bf16[2,8,384,384]{3,2,1,0:T(8,128)(2,1)} %chunk_given.4), channel_id=1, source_target_pairs={{0,1},{1,0},{2,3},{3,2},{4,5},{5,4},{6,7},{7,6},{8,9},{9,8},{10,11... | collective-permute-start | bytes 14155784 | tf_op jit(solution)/shard_map/ppermute | solution.py:931
  239.3 13.7 %collective-permute-start.15 = (bf16[2,2,4,16,16,512]{5,4,3,2,1,0:T(8,128)(2,1)}, bf16[2,2,4,16,16,512]{5,4,3,2,1,0:T(8,128)(2,1)S(1)}, u32[]{:S(2)}, u32[]{:S(2)}) collective-permute-start(bf16[2,2,4,16,16,512]{5,4,3,2,1,0:T(8,128)(2,1)} %get-tuple-element.279), channel_id=1, source_target_pairs={{0,1},{1,0},{2,3},{3,2},{4,5},{5,4},{6,7},{7,6},{8,9},{9,8},{10,11... | collective-permute-start | bytes 12582920 | tf_op jit(solution)/shard_map/ppermute | solution.py:931
  239.8 32.6 %collective-permute-start.16 = (bf16[4,288,384]{2,1,0:T(8,128)(2,1)}, bf16[4,288,384]{2,1,0:T(8,128)(2,1)}, u32[]{:S(2)}, u32[]{:S(2)}) collective-permute-start(bf16[4,288,384]{2,1,0:T(8,128)(2,1)} %get-tuple-element.291), channel_id=1, source_target_pairs={{0,2},{1,3},{2,0},{3,1},{4,6},{5,7},{6,4},{7,5},{8,10},{9,11},{10,... | collective-permute-start | bytes 2654216 | tf_op jit(solution)/shard_map/ppermute | solution.py:931
  272.4 53.9 %collective-permute-start.18 = (bf16[8,384,384]{2,1,0:T(8,128)(2,1)}, bf16[8,384,384]{2,1,0:T(8,128)(2,1)}, u32[]{:S(2)}, u32[]{:S(2)}) collective-permute-start(bf16[8,384,384]{2,1,0:T(8,128)(2,1)} %get-tuple-element.306), channel_id=1, source_target_pairs={{0,16},{16,0},{1,17},{17,1},{2,18},{18,2},{3,19},{19,3},{4,20},{20... | collective-permute-start | bytes 7077896 | tf_op jit(solution)/shard_map/ppermute | solution.py:927
  272.9 53.4 %collective-permute-start.20 = (bf16[2,4,16,16,512]{4,3,2,1,0:T(8,128)(2,1)}, bf16[2,4,16,16,512]{4,3,2,1,0:T(8,128)(2,1)S(1)}, u32[]{:S(2)}, u32[]{:S(2)}) collective-permute-start(bf16[2,4,16,16,512]{4,3,2,1,0:T(8,128)(2,1)} %get-tuple-element.312), channel_id=1, source_target_pairs={{0,2},{1,3},{2,0},{3,1},{4,6},{5,7},{6,4},{7,5},{8,10},{9,11},{10,... | collective-permute-start | bytes 6291464 | tf_op jit(solution)/shard_map/ppermute | solution.py:931
  275.5 26.7 %collective-permute-start.17 = (bf16[2,288,384]{2,1,0:T(8,128)(2,1)S(1)}, bf16[2,288,384]{2,1,0:T(8,128)(2,1)S(1)}, u32[]{:S(2)}, u32[]{:S(2)}) collective-permute-start(bf16[2,288,384]{2,1,0:T(8,128)(2,1)S(1)} %get-tuple-element.299), channel_id=1, source_target_pairs={{0,4},{1,5},{2,6},{3,7},{4,0},{5,1},{6,2},{7,3},{8,12},{9,13},{10,... | collective-permute-start | bytes 1327112 | tf_op jit(solution)/shard_map/ppermute | solution.py:1238
  332.2 14.8 %collective-permute-start.23 = (bf16[2,4,4,128,128]{4,3,2,1,0:T(8,128)(2,1)}, bf16[2,4,4,128,128]{4,3,2,1,0:T(8,128)(2,1)S(1)}, u32[]{:S(2)}, u32[]{:S(2)}) collective-permute-start(bf16[2,4,4,128,128]{4,3,2,1,0:T(8,128)(2,1)} %get-tuple-element.331), channel_id=1, source_target_pairs={{0,1},{1,0},{2,3},{3,2},{4,5},{5,4},{6,7},{7,6},{8,9},{9,8},{10,11... | collective-permute-start | bytes 3145736 | tf_op jit(solution)/shard_map/ppermute | solution.py:931
  332.3 28.5 %collective-permute-start.21 = (bf16[4,384,384]{2,1,0:T(8,128)(2,1)S(1)}, bf16[4,384,384]{2,1,0:T(8,128)(2,1)}, u32[]{:S(2)}, u32[]{:S(2)}) collective-permute-start(bf16[4,384,384]{2,1,0:T(8,128)(2,1)S(1)} %get-tuple-element.320), channel_id=1, source_target_pairs={{0,2},{1,3},{2,0},{3,1},{4,6},{5,7},{6,4},{7,5},{8,10},{9,11},{10,... | collective-permute-start | bytes 3538952 | tf_op jit(solution)/shard_map/ppermute | solution.py:931
  333.6 26.1 %collective-permute-start.27 = (bf16[4,16,16,512]{3,2,1,0:T(8,128)(2,1)S(1)}, bf16[4,16,16,512]{3,2,1,0:T(8,128)(2,1)}, u32[]{:S(2)}, u32[]{:S(2)}) collective-permute-start(bf16[4,16,16,512]{3,2,1,0:T(8,128)(2,1)S(1)} %get-tuple-element.340), channel_id=1, source_target_pairs={{0,16},{16,0},{1,17},{17,1},{2,18},{18,2},{3,19},{19,3},{4,20},{20... | collective-permute-start | bytes 3145736 | tf_op jit(solution)/shard_map/ppermute | solution.py:927
  347.6 13.2 %collective-permute-start.26 = (bf16[2,288,384]{2,1,0:T(8,128)(2,1)S(1)}, bf16[2,288,384]{2,1,0:T(8,128)(2,1)S(1)}, u32[]{:S(2)}, u32[]{:S(2)}) collective-permute-start(bf16[2,288,384]{2,1,0:T(8,128)(2,1)S(1)} %get-tuple-element.338.refs_4_), channel_id=1, source_target_pairs={{0,4},{1,5},{2,6},{3,7},{4,0},{5,1},{6,2},{7,3},{8,12},{9,13},{10,... | collective-permute-start | bytes 1327112 | tf_op jit(solution)/shard_map/ppermute | solution.py:1238
  350.1 12.9 %collective-permute-start.25 = (bf16[8,32,384]{2,1,0:T(8,128)(2,1)S(1)}, bf16[8,32,384]{2,1,0:T(8,128)(2,1)S(1)}, u32[]{:S(2)}, u32[]{:S(2)}) collective-permute-start(bf16[8,32,384]{2,1,0:T(8,128)(2,1)S(1)} %get-tuple-element.337), channel_id=1, source_target_pairs={{0,16},{16,0},{1,17},{17,1},{2,18},{18,2},{3,19},{19,3},{4,20},{20... | collective-permute-start | bytes 589832 | tf_op jit(solution)/shard_map/ppermute | solution.py:927
  365.5 25.9 %collective-permute-start.28 = (bf16[2,384,384]{2,1,0:T(8,128)(2,1)S(1)}, bf16[2,384,384]{2,1,0:T(8,128)(2,1)S(1)}, u32[]{:S(2)}, u32[]{:S(2)}) collective-permute-start(bf16[2,384,384]{2,1,0:T(8,128)(2,1)S(1)} %get-tuple-element.342), channel_id=1, source_target_pairs={{0,4},{1,5},{2,6},{3,7},{4,0},{5,1},{6,2},{7,3},{8,12},{9,13},{10,... | collective-permute-start | bytes 1769480 | tf_op jit(solution)/shard_map/ppermute | solution.py:1238
  367.2 24.1 %collective-permute-start.30 = (bf16[2,16,16,512]{3,2,1,0:T(8,128)(2,1)S(1)}, bf16[2,16,16,512]{3,2,1,0:T(8,128)(2,1)S(1)}, u32[]{:S(2)}, u32[]{:S(2)}) collective-permute-start(bf16[2,16,16,512]{3,2,1,0:T(8,128)(2,1)S(1)} %get-tuple-element.346), channel_id=1, source_target_pairs={{0,4},{1,5},{2,6},{3,7},{4,0},{5,1},{6,2},{7,3},{8,12},{9,13},{10,... | collective-permute-start | bytes 1572872 | tf_op jit(solution)/shard_map/ppermute | solution.py:1238
  392.0 25.9 %collective-permute-start.31 = (bf16[1,384,384]{2,1,0:T(8,128)(2,1)S(1)}, bf16[1,384,384]{2,1,0:T(8,128)(2,1)S(1)}, u32[]{:S(2)}, u32[]{:S(2)}) collective-permute-start(bf16[1,384,384]{2,1,0:T(8,128)(2,1)S(1)} %get-tuple-element.348), channel_id=1, source_target_pairs={{0,8},{1,9},{2,10},{3,11},{4,12},{5,13},{6,14},{7,15},{8,0},{9,1},... | collective-permute-start | bytes 884744 | tf_op jit(solution)/shard_map/ppermute | solution.py:1238
  392.2 41.2 %collective-permute-start.36 = (bf16[4,288,384]{2,1,0:T(8,128)(2,1)S(1)}, bf16[4,288,384]{2,1,0:T(8,128)(2,1)S(1)}, u32[]{:S(2)}, u32[]{:S(2)}) collective-permute-start(bf16[4,288,384]{2,1,0:T(8,128)(2,1)S(1)} %get-tuple-element.362.refs_4_), channel_id=1, source_target_pairs={{0,2},{1,3},{2,0},{3,1},{4,6},{5,7},{6,4},{7,5},{8,10},{9,11},{10,... | collective-permute-start | bytes 2654216 | tf_op jit(solution)/shard_map/ppermute | solution.py:931
  393.0 24.8 %collective-permute-start.33 = (bf16[1,16,16,512]{3,2,1,0:T(8,128)(2,1)S(1)}, bf16[1,16,16,512]{3,2,1,0:T(8,128)(2,1)S(1)}, u32[]{:S(2)}, u32[]{:S(2)}) collective-permute-start(bf16[1,16,16,512]{3,2,1,0:T(8,128)(2,1)S(1)} %get-tuple-element.352), channel_id=1, source_target_pairs={{0,8},{1,9},{2,10},{3,11},{4,12},{5,13},{6,14},{7,15},{8,0},{9,1},... | collective-permute-start | bytes 786440 | tf_op jit(solution)/shard_map/ppermute | solution.py:1238
  398.3 35.6 %collective-permute-start.37 = (bf16[4,4,128,128]{3,2,1,0:T(8,128)(2,1)S(1)}, bf16[4,4,128,128]{3,2,1,0:T(8,128)(2,1)S(1)}, u32[]{:S(2)}, u32[]{:S(2)}) collective-permute-start(bf16[4,4,128,128]{3,2,1,0:T(8,128)(2,1)S(1)} %get-tuple-element.365), channel_id=1, source_target_pairs={{0,2},{1,3},{2,0},{3,1},{4,6},{5,7},{6,4},{7,5},{8,10},{9,11},{10,... | collective-permute-start | bytes 1572872 | tf_op jit(solution)/shard_map/ppermute | solution.py:931
  418.1 15.4 %collective-permute-start.34 = (bf16[1,384,384]{2,1,0:T(8,128)(2,1)S(1)}, bf16[1,384,384]{2,1,0:T(8,128)(2,1)S(1)}, u32[]{:S(2)}, u32[]{:S(2)}) collective-permute-start(bf16[1,384,384]{2,1,0:T(8,128)(2,1)S(1)} %get-tuple-element.357.refs_0_), channel_id=1, source_target_pairs={{0,8},{1,9},{2,10},{3,11},{4,12},{5,13},{6,14},{7,15},{8,0},{9,1},... | collective-permute-start | bytes 884744 | tf_op jit(solution)/shard_map/ppermute | solution.py:1238
  420.8 13.1 %collective-permute-start.35 = (bf16[1,32,384]{2,1,0:T(8,128)(2,1)S(1)}, bf16[1,32,384]{2,1,0:T(8,128)(2,1)S(1)}, u32[]{:S(2)}, u32[]{:S(2)}) collective-permute-start(bf16[1,32,384]{2,1,0:T(8,128)(2,1)S(1)} %get-tuple-element.361), channel_id=1, source_target_pairs={{0,8},{1,9},{2,10},{3,11},{4,12},{5,13},{6,14},{7,15},{8,0},{9,1},... | collective-permute-start | bytes 73736 | tf_op jit(solution)/shard_map/ppermute | solution.py:1238
  435.6 21.4 %collective-permute-start.38 = (bf16[2,384,384]{2,1,0:T(8,128)(2,1)S(1)}, bf16[2,384,384]{2,1,0:T(8,128)(2,1)S(1)}, u32[]{:S(2)}, u32[]{:S(2)}) collective-permute-start(bf16[2,384,384]{2,1,0:T(8,128)(2,1)S(1)} %get-tuple-element.366.refs_0_), channel_id=1, source_target_pairs={{0,4},{1,5},{2,6},{3,7},{4,0},{5,1},{6,2},{7,3},{8,12},{9,13},{10,... | collective-permute-start | bytes 1769480 | tf_op jit(solution)/shard_map/ppermute | solution.py:1238
  435.6 21.4 %collective-permute-start.40 = (bf16[2,4,128,128]{3,2,1,0:T(8,128)(2,1)S(1)}, bf16[2,4,128,128]{3,2,1,0:T(8,128)(2,1)S(1)}, u32[]{:S(2)}, u32[]{:S(2)}) collective-permute-start(bf16[2,4,128,128]{3,2,1,0:T(8,128)(2,1)S(1)} %get-tuple-element.369), channel_id=1, source_target_pairs={{0,4},{1,5},{2,6},{3,7},{4,0},{5,1},{6,2},{7,3},{8,12},{9,13},{10,... | collective-permute-start | bytes 786440 | tf_op jit(solution)/shard_map/ppermute | solution.py:1238
  437.6 17.2 %collective-permute-start.39 = (bf16[1,32,384]{2,1,0:T(8,128)(2,1)S(1)}, bf16[1,32,384]{2,1,0:T(8,128)(2,1)S(1)}, u32[]{:S(2)}, u32[]{:S(2)}) collective-permute-start(bf16[1,32,384]{2,1,0:T(8,128)(2,1)S(1)} %get-tuple-element.367.refs_2_), channel_id=1, source_target_pairs={{0,8},{1,9},{2,10},{3,11},{4,12},{5,13},{6,14},{7,15},{8,0},{9,1},... | collective-permute-start | bytes 73736 | tf_op jit(solution)/shard_map/ppermute | solution.py:1238
  457.5 13.4 %collective-permute-start.43 = (bf16[8,288,384]{2,1,0:T(8,128)(2,1)}, bf16[8,288,384]{2,1,0:T(8,128)(2,1)S(1)}, u32[]{:S(2)}, u32[]{:S(2)}) collective-permute-start(bf16[8,288,384]{2,1,0:T(8,128)(2,1)} %get-tuple-element.377.own), channel_id=1, source_target_pairs={{0,1},{1,0},{2,3},{3,2},{4,5},{5,4},{6,7},{7,6},{8,9},{9,8},{10,11... | collective-permute-start | bytes 5308424 | tf_op jit(solution)/shard_map/ppermute | solution.py:931
  459.5 24.2 %collective-permute-start.51 = (bf16[256,768]{1,0:T(8,128)(2,1)}, bf16[256,768]{1,0:T(8,128)(2,1)}, u32[]{:S(2)}, u32[]{:S(2)}) collective-permute-start(bf16[256,768]{1,0:T(8,128)(2,1)} %dynamic-slice_bitcast_fusion.2), channel_id=1, source_target_pairs={{0,16},{16,0},{1,17},{17,1},{2,18},{18,2},{3,19},{19,3},{4,20},{20... | collective-permute-start | bytes 1179656 | tf_op jit(solution)/shard_map/ppermute | solution.py:927
  463.8 29.8 %collective-permute-start.45 = (bf16[4,384,384]{2,1,0:T(8,128)(2,1)S(1)}, bf16[4,384,384]{2,1,0:T(8,128)(2,1)}, u32[]{:S(2)}, u32[]{:S(2)}) collective-permute-start(bf16[4,384,384]{2,1,0:T(8,128)(2,1)S(1)} %get-tuple-element.380.refs_0_), channel_id=1, source_target_pairs={{0,2},{1,3},{2,0},{3,1},{4,6},{5,7},{6,4},{7,5},{8,10},{9,11},{10,... | collective-permute-start | bytes 3538952 | tf_op jit(solution)/shard_map/ppermute | solution.py:931
  (115 other events, 949.2 us)

commit v4 on v3

--- a/solution.py
+++ b/solution.py
@@ -1117,8 +1117,10 @@
     )(place, *members, received)
 
 
-def assemble_kernel(weights, place, own, other, *outs):
-    for source, core in ((own, place[3]), (other, 1 - place[3])):
+def assemble_kernel(weights, parts, place, *refs):
+    outs = refs[2 * parts :]
+    for index, core in ((0, place[3]), (1, 1 - place[3])):
+        members = refs[index * parts : (index + 1) * parts]
         for piece in range(PIECES):
             at = 0
             for weight, out in zip(weights, outs):
@@ -1127,18 +1129,25 @@
                         core * (weight.columns // 2) + block * COLUMNS, COLUMNS, LANES
                     )
                     rows = slice(at + offset, at + offset + size)
-                    out[row : row + size, columns] = wide(source[piece ^ place[4], rows, :])
+                    place_at = piece ^ place[4]
+                    if parts == 1:
+                        out[row : row + size, columns] = wide(members[0][place_at, rows, :])
+                    else:
+                        first = members[0][place_at % (PIECES // 2), rows, :]
+                        second = members[1][place_at % (PIECES // 2), rows, :]
+                        chosen = jnp.where(place_at < PIECES // 2, first, second)
+                        out[row : row + size, columns] = wide(chosen)
                 at += weight.run
 
 
 def assemble(place, weights, own, other):
     outs = [jax.ShapeDtypeStruct((weight.rows, weight.columns), WIDE) for weight in weights]
     return pl.pallas_call(
-        functools.partial(assemble_kernel, weights),
+        functools.partial(assemble_kernel, weights, len(own)),
         grid_spec=pltpu.PrefetchScalarGridSpec(
             num_scalar_prefetch=1,
             grid=(1,),
-            in_specs=[full_spec(own), full_spec(other)],
+            in_specs=[full_spec(member) for member in [*own, *other]],
             out_specs=[full_spec(member) for member in outs],
         ),
         out_shape=outs,
@@ -1147,7 +1156,7 @@
             dimension_semantics=("arbitrary",), vmem_limit_bytes=48 * MEBI
         ),
         name="assemble",
-    )(place, own, other)
+    )(place, *own, *other)
 
 
 def products(*shapes):
@@ -1157,13 +1166,23 @@
     return weights
 
 
-def vector_sum(member):
-    section = lax.axis_index("section")
-    kept = lax.dynamic_index_in_dim(member, section, 0, keepdims=False)
-    total = kept + swap_section(lax.dynamic_index_in_dim(member, 1 - section, 0, keepdims=False))
-    for bit in range((lax.axis_size("dp") - 1).bit_length()):
-        total = total + swap_bit(total, bit)
-    return total
+def split_vectors(total, vectors, section, atom_shape, pair_params):
+    tok_gain, tok_weight, atom_gain, atom_weight = pair_params
+    sums = []
+    first = 0
+    for member in vectors:
+        sums.append(total[first : first + member.size])
+        first += member.size
+    halves = [run_of(member, section, 2) for member in sums[:6]]
+    token_cross = run_of(sums[6].reshape(tok_weight.shape[1], -1).T, section, 2)
+    atom_cross = run_of(sums[7].reshape(atom_shape), section, 2)
+    for cross, gain, weight in (
+        (token_cross, tok_gain, tok_weight),
+        (atom_cross, atom_gain, atom_weight),
+    ):
+        halves.append(jnp.sum(cross * wide(run_of(weight, section, 2)), axis=1))
+        halves.append(cross * wide(run_of(gain, section, 2))[:, None])
+    return halves
 
 
 def half_block(shape, count=2):
@@ -1723,18 +1742,19 @@
     grad_offset, grad_gain, grad_query = vector_back(
         d_projected, cond_weight, unit_cond, d_projections
     )
-    if direct:
-        grad_query, got_bias = together(grad_query, got_bias)
-        bias, send_bias = exchange((0, d_token_bias[0], got_bias))
-        grad_query, send_bias = together(grad_query, send_bias)
-        got_bias = swap_near(send_bias)
     given_b_there, grad_query = together(given_b_there, grad_query)
     send_b, keep_b = chunk_kept(here, chunk_b, members_b, given_b_there)
     d_tokens, send_b, got_a = together(d_tokens, send_b, got_a)
     got_b = swap_section(send_b)
-    keep_a, send_a = exchange((0, paired(keep_a), paired(got_a)))
-    d_tokens, send_a = together(d_tokens, send_a)
+    entries = [(0, paired(keep_a), paired(got_a))]
+    if direct:
+        entries.append((0, d_token_bias[0], got_bias))
+    keep_a, send_a, *bias = exchange(*entries)
+    d_tokens, send_a, *bias = together(d_tokens, send_a, *bias)
     got_a = swap_plane(send_a, 1)
+    if direct:
+        bias, send_bias = bias
+        got_bias = swap_near(send_bias)
     d_attended, d_gates, d_middles, d_atom_pieces, packed_a = atom_tokens_back(
         features, atom_single, atom_token, d_tokens, counts, atom_stored, atom_block, gather_weight
     )
@@ -1792,6 +1812,9 @@
     if direct:
         bias, send_bias = bias
         got_bias = swap_plane(send_bias, 1)
+    output_low, total_a = together(output_low, total_a)
+    output_halves = exchange_halves(output_low)
+    got_d, output_halves = together(got_d, output_halves)
 
     entries = [(0, paired(keep_b), paired(got_b)), (0, paired(keep_d), paired(got_d))]
     if direct:
@@ -1803,18 +1826,16 @@
         got_bias = swap_plane(send_bias, 2)
         send_d, send_atom = together(send_d, send_atom)
         got_atom = swap_near(send_atom)
+    features_low, send_d = together(low(d_features), send_d)
+    feature_halves = exchange_halves(features_low)
+    got_d, feature_halves = together(got_d, feature_halves)
 
     entries = [(None, keep_b, got_b), (0, paired(keep_d), paired(got_d))]
     if direct:
         entries.append((None, bias, got_bias))
     total_b, keep_d, send_d, *token_slab = exchange(*entries)
     total_b = rest_sum(total_b)
-    total_b, send_d, output_low, features_low = together(
-        total_b, send_d, output_low, low(d_features)
-    )
     got_b, got_d = swap_plane(total_b, 2), swap_plane(send_d, 2)
-    feature_halves = exchange_halves(features_low)
-    output_halves = exchange_halves(output_low)
     if direct:
         token_cross = product(token_slab[0].reshape(heads, -1), pair_units)
         got_b, token_cross = together(got_b, token_cross)
@@ -1855,18 +1876,27 @@
     for bit in more_bits():
         total = total + swap_bit(total, bit)
     total = total + swap_core(total)
-    grad_gu, grad_down = assemble(here, chunk_a, total_a, core_a)
-    got_d, got_b, total, feature_halves, output_halves, grad_gu = together(
-        got_d, got_b, total, feature_halves, output_halves, grad_gu
-    )
-    total_b, total_d = exchange(("join", total_b, got_b), ("join", total_d, got_d))
-    total_b, total_d, total = together(total_b, total_d, total)
-    core_b, core_d, got = swap_core(total_b), swap_core(total_d), swap_near(total)
+    core_b = swap_core(total_b)
+    grad_gu, grad_down = assemble(here, chunk_a, [total_a], [core_a])
+    got_d, got_b, total, grad_gu, core_b = together(got_d, got_b, total, grad_gu, core_b)
+    (total_d,) = exchange(("join", total_d, got_d))
+    total_d, got_b, total = together(total_d, got_b, total)
+    core_got, core_d, got = swap_core(got_b), swap_core(total_d), swap_near(total)
     core_d, got = together(core_d, got)
     total = (total + got)[0]
-    (packed,) = assemble(here, chunk_d, total_d, core_d)
-    core_b, packed, total = together(core_b, packed, total)
-    grad_proj, grad_out, grad_cond = assemble(here, chunk_b, total_b, core_b)
+    vector_grads = split_vectors(
+        total,
+        vectors,
+        section,
+        atom_cross.shape,
+        (tokpair_gain, tokpair_weight, atompair_gain, atompair_weight),
+    )
+    core_d, *vector_grads = together(core_d, *vector_grads)
+    (packed,) = assemble(here, chunk_d, [total_d], [core_d])
+    core_got, packed = together(core_got, packed)
+    grad_proj, grad_out, grad_cond = assemble(
+        here, chunk_b, [total_b, got_b], [core_b, core_got]
+    )
 
     atom_width = features.shape[1]
     sizes = [6 * atom_width, 4 * atom_width, width, atom_block[6].shape[1], atom_width]
@@ -1880,20 +1910,18 @@
     atom_down = quarters.reshape(-1, 2, atom_width).transpose(1, 0, 2).reshape(-1, atom_width)
 
 
-    sums = []
-    first = 0
-    for member in vectors:
-        sums.append(total[first : first + member.size])
-        first += member.size
-    gain, offset, query, token_gain, token_offset, token_query = [
-        run_of(member, section, 2) for member in sums[:6]
-    ]
-    token_cross = run_of(sums[6].reshape(heads, -1).T, section, 2)
-    atom_cross = run_of(sums[7].reshape(atom_cross.shape), section, 2)
-    token_pair_gain = jnp.sum(token_cross * wide(run_of(tokpair_weight, section, 2)), axis=1)
-    token_pair_weight = token_cross * wide(run_of(tokpair_gain, section, 2))[:, None]
-    pair_gain = jnp.sum(atom_cross * wide(run_of(atompair_weight, section, 2)), axis=1)
-    pair_weight = atom_cross * wide(run_of(atompair_gain, section, 2))[:, None]
+    (
+        gain,
+        offset,
+        query,
+        token_gain,
+        token_offset,
+        token_query,
+        token_pair_gain,
+        token_pair_weight,
+        pair_gain,
+        pair_weight,
+    ) = vector_grads
     return (
         output_halves,
         wide(feature_halves),

time: 531 us -> 525 us (0.989)
    ppermute x22, waiting for transfers between devices: 98.7 us -> 86.2 us  [swap_plane(): lax.ppermute(member, 'dp', [(i, i ^ distance << 2) for i in range(size)])]
    ppermute x24 -> x25, waiting for transfers between devices: 20.6 us -> 30.4 us  [swap_bit(): lax.ppermute(member, 'dp', [(i, i ^ 1 << bit) for i in range(lax.axis_siz...]
    unnamed x197 -> x203, local copies, waits for them, and re-layouts: 21.3 us -> 22.7 us
    ppermute x24 -> x25, starting transfers between devices: 15.2 us -> 15.9 us  [swap_bit(): lax.ppermute(member, 'dp', [(i, i ^ 1 << bit) for i in range(lax.axis_siz...]
    pallas_call x16 -> x15, Pallas kernels: 25.9 us -> 25.8 us  [exchange(): pl.pallas_call(functools.partial(exchange_kernel, kinds), grid=(2,), in_s...]
  transfers between devices with their start and end apart: 55 -> 56, of which waited for: 31 -> 32; matrix products, arithmetic and copies ran while one was open for 10% -> 11% of each run, Pallas kernels for 26% -> 27%
where the time goes in v4:
time: 525 us; the launch traced here: 514 us
  Pallas kernels  208 us (40%)
  waiting for transfers between devices  151 us (29%)
  starting transfers between devices  47.5 us (9%)
  other arithmetic  40.5 us (8%)
  local copies, waits for them, and re-layouts  39.3 us (7%)
  matrix products  22.5 us (4%)
    ppermute x22, waiting for transfers between devices, swap_plane(): lax.ppermute(member, 'dp', [(i, i ^ distance << 2) for i in range(size)])  86.2 us
    ppermute x9, waiting for transfers between devices, swap_section(): return lax.ppermute(member, 'section', [(0, 1), (1, 0)])  34.9 us
    ppermute x25, waiting for transfers between devices, swap_bit(): lax.ppermute(member, 'dp', [(i, i ^ 1 << bit) for i in range(lax.axis_siz...  30.4 us
    pallas_call x15, Pallas kernels, exchange(): pl.pallas_call(functools.partial(exchange_kernel, kinds), grid=(2,), in_s...  25.8 us
    pallas_call x2, Pallas kernels, atom_attend(): pl.pallas_call(functools.partial(atom_attend_kernel, bool(before)), grid_...  25 us
    pallas_call x1, Pallas kernels, atom_tokens_back(): pl.pallas_call(atom_tokens_back_kernel, grid_spec=pltpu.PrefetchScalarGri...  23.6 us
    unnamed x203, local copies, waits for them, and re-layouts  22.7 us
    ppermute x22, starting transfers between devices, swap_plane(): lax.ppermute(member, 'dp', [(i, i ^ distance << 2) for i in range(size)])  22.6 us
  transfers between devices with their start and end apart: 56, of which 32 were waited for; matrix products, arithmetic and copies ran while one was open for 11% of the time, Pallas kernels for 27%

profile of v4, /device:TPU:0, one launch (start us, length us, event | category | flops | bytes accessed | tf_op | source)
XLA Modules:
  0.0 514.3 jit_solution(12226624743446189262)
XLA Ops:
  33.2 7.8 %collective-permute-done.1 = bf16[2,4,4,32,128]{4,3,2,1,0:T(8,128)(2,1)S(1)} collective-permute-done((bf16[2,4,4,32,128]{4,3,2,1,0:T(8,128)(2,1)S(1)}, bf16[2,4,4,32,128]{4,3,2,1,0:T(8,128)(2,1)S(1)}, u32[]{:S(2)}, u32[]{:S(2)}) %collective-permute-start.1) | collective-permute-done | bytes 262176 | tf_op jit(solution)/shard_map/ppermute | solution.py:1257
  48.7 5.0 convolution_add_fusion.gate_two.gate_one.scale_two.scale_one
  53.7 5.6 %collective-permute-done.4 = bf16[2,16,16,512]{3,2,1,0:T(8,128)(2,1)S(1)} collective-permute-done((bf16[2,16,16,512]{3,2,1,0:T(8,128)(2,1)S(1)}, bf16[2,16,16,512]{3,2,1,0:T(8,128)(2,1)S(1)}, u32[]{:S(2)}, u32[]{:S(2)}) %collective-permute-start.4) | collective-permute-done | bytes 524320 | tf_op jit(solution)/shard_map/ppermute | solution.py:1257
  67.2 12.3 %atom_attend.2 = (f32[512,768]{1,0:T(8,128)}, f32[512,1]{1,0:T(8,128)}, f32[2048,128]{1,0:T(8,128)}, bf16[64,128,128]{2,1,0:T(8,128)(2,1)}) custom-call(s32[64]{0:T(128)} %starts.5, s32[4]{0:T(128)} %pad_add_fusion.place, s32[8]{0:T(128)} %slice.85.firsts, bf16[2048,128]{1,0:T(8,128)(2,1)} %copy-done.4, bf16[2048,128]{1,0:T(8,128)(2,1)} %single.9, ...), custom_call_target="tpu_custom_call" | custom-call | bytes 7380000 | tf_op jit(solution)/shard_map/atom_attend/pallas_call | solution.py:268
  82.6 12.7 %atom_attend.3 = (bf16[512,768]{1,0:T(8,128)(2,1)}, f32[512,1]{1,0:T(8,128)}, f32[2048,128]{1,0:T(8,128)}, bf16[64,128,128]{2,1,0:T(8,128)(2,1)}) custom-call(s32[64]{0:T(128)} %starts.5, s32[4]{0:T(128)} %pad_add_fusion.place, s32[8]{0:T(128)} %slice.85.firsts, bf16[2048,128]{1,0:T(8,128)(2,1)} %copy-done.4, ...), custom_call_target="tpu_custom_call", output_to_operand_aliasing={{2}: (18, {}), {3}: (19, {})} | custom-call | bytes 7380000 | tf_op jit(solution)/shard_map/atom_attend/pallas_call | solution.py:268
  95.3 10.2 %collective-permute-done.8.refs_1_ = bf16[8,8,16,512]{3,2,1,0:T(8,128)(2,1)S(1)} collective-permute-done((bf16[8,8,16,512]{3,2,1,0:T(8,128)(2,1)S(1)}, bf16[8,8,16,512]{3,2,1,0:T(8,128)(2,1)S(1)}, u32[]{:S(2)}, u32[]{:S(2)}) %collective-permute-start.8) | collective-permute-done | bytes 1048608 | tf_op jit(solution)/shard_map/ppermute | solution.py:927
  114.2 6.3 %add_convert_fusion.queries.keys.values.gates = bf16[512,3072]{1,0:T(8,128)(2,1)} fusion(bf16[512,768]{1,0:T(8,128)(2,1)S(1)} %get-tuple-element.503.refs_0_, bf16[768,3072]{1,0:T(8,128)(2,1)} %proj_weight.4, f32[3072]{0:T(1024)S(1)} %pad_convert_fusion), kind=kOutput, calls=%fused_computation.2 | convolution fusion | flops 2419064832 | bytes 8663040 | tf_op jit(solution)/shard_map/dot_general | solution.py:24
  120.5 16.4 %token_forward.1 = (bf16[16,512,512]{2,1,0:T(8,128)(2,1)}, f32[512,768]{1,0:T(8,128)}, bf16[512,768]{1,0:T(8,128)(2,1)}) custom-call(s32[4]{0:T(128)} %pad_add_fusion.place, bf16[512,3072]{1,0:T(8,128)(2,1)} %add_convert_fusion.queries.keys.values.gates, bf16[512,3072]{1,0:T(8,128)(2,1)} %add_convert_fusion.queries.keys.values.gates, ...), custom_call_target="tpu_custom_call" | custom-call | bytes 7380000 | tf_op jit(solution)/shard_map/token_forward/pallas_call | solution.py:751
  154.4 6.6 %transition_back.1 = (bf16[512,768]{1,0:T(8,128)(2,1)S(1)}, bf16[512,768]{1,0:T(8,128)(2,1)S(1)}, bf16[512,3072]{1,0:T(8,128)(2,1)}) custom-call(bf16[512,768]{1,0:T(8,128)(2,1)S(1)} %dynamic-slice_bitcast_fusion.d_result, f32[512,4608]{1,0:T(8,128)} %convolution_add_fusion.gate_two.gate_one.scale_two.scale_one, f32[512,768]{1,0:T(8,128)S(1)} %get-tuple-element.528.down_out, ...), custom_call_target="tpu_custom_call" | custom-call | bytes 18450000 | tf_op jit(solution)/shard_map/transition_back/pallas_call | solution.py:1353
  161.0 6.6 %chunk_given.3 = bf16[2,8,288,384]{3,2,1,0:T(8,128)(2,1)} custom-call(s32[5]{0:T(128)S(1)} %stack.81.place, bf16[512,768]{1,0:T(8,128)(2,1)S(1)} %get-tuple-element.496.refs_0_, bf16[512,3072]{1,0:T(8,128)(2,1)} %get-tuple-element.267.refs_1_.d_gate_up, bf16[512,1536]{1,0:T(8,128)(2,1)S(1)} %fusion.2.refs_2_, bf16[512,768]{1,0:T(8,128)(2,1)S(1)} %get-tuple-element.263.refs_3_), custom_call_target="tpu_custom_call" | custom-call | bytes 11070000 | tf_op jit(solution)/shard_map/chunk_given/pallas_call | solution.py:1082
  167.7 6.4 %collective-permute-done.12.refs_4_ = bf16[2,8,288,384]{3,2,1,0:T(8,128)(2,1)S(1)} collective-permute-done((bf16[2,8,288,384]{3,2,1,0:T(8,128)(2,1)}, bf16[2,8,288,384]{3,2,1,0:T(8,128)(2,1)S(1)}, u32[]{:S(2)}, u32[]{:S(2)}) %collective-permute-start.12) | collective-permute-done | bytes 3538976 | tf_op jit(solution)/shard_map/ppermute | solution.py:931
  175.8 7.9 %chunk_kept.3 = (bf16[8,288,384]{2,1,0:T(8,128)(2,1)}, bf16[8,288,384]{2,1,0:T(8,128)(2,1)}) custom-call(s32[5]{0:T(128)S(1)} %stack.81.place, bf16[512,768]{1,0:T(8,128)(2,1)S(1)} %get-tuple-element.496.refs_0_, bf16[512,3072]{1,0:T(8,128)(2,1)} %get-tuple-element.267.refs_1_.d_gate_up, bf16[512,1536]{1,0:T(8,128)(2,1)S(1)} %fusion.2.refs_2_, ...), custom_call_target="tpu_custom_call" | custom-call | bytes 22140000 | tf_op jit(solution)/shard_map/chunk_kept/pallas_call | solution.py:1102
  187.3 10.4 %middle_back.1 = (f32[512,768]{1,0:T(8,128)S(1)}, bf16[512,768]{1,0:T(8,128)(2,1)S(1)}, bf16[512,768]{1,0:T(8,128)(2,1)S(1)}, bf16[512,2304]{1,0:T(8,128)(2,1)}) custom-call(bf16[512,768]{1,0:T(8,128)(2,1)S(1)} %dynamic-slice_bitcast_fusion.d_result, f32[512,4608]{1,0:T(8,128)} %convolution_add_fusion.gate_two.gate_one.scale_two.scale_one, ...), custom_call_target="tpu_custom_call" | custom-call | bytes 11070000 | tf_op jit(solution)/shard_map/middle_back/pallas_call | solution.py:1413
  199.5 17.0 %token_backward.1 = (bf16[2,2,4,16,16,512]{5,4,3,2,1,0:T(8,128)(2,1)}, bf16[2,2,4,16,16,512]{5,4,3,2,1,0:T(8,128)(2,1)}, bf16[512,3072]{1,0:T(8,128)(2,1)}) custom-call(s32[4]{0:T(128)} %pad_add_fusion.place, bf16[512,3072]{1,0:T(8,128)(2,1)} %add_convert_fusion.queries.keys.values.gates, bf16[512,3072]{1,0:T(8,128)(2,1)} %add_convert_fusion.queries.keys.values.gates, ...), custom_call_target="tpu_custom_call" | custom-call | bytes 11070000 | tf_op jit(solution)/shard_map/token_backward/pallas_call | solution.py:890
  217.6 8.8 %input_back.1 = (bf16[512,4608]{1,0:T(8,128)(2,1)}, bf16[512,768]{1,0:T(8,128)(2,1)S(1)}) custom-call(bf16[512,3072]{1,0:T(8,128)(2,1)} %get-tuple-element.269.d_projections.refs_1_.d_queries, f32[512,4608]{1,0:T(8,128)} %convolution_add_fusion.gate_two.gate_one.scale_two.scale_one, f32[512,768]{1,0:T(8,128)S(1)} %copy-done.11, ...), custom_call_target="tpu_custom_call" | custom-call | bytes 7380000 | tf_op jit(solution)/shard_map/input_back/pallas_call | solution.py:1478
  230.1 9.3 %chunk_given.4 = bf16[2,8,384,384]{3,2,1,0:T(8,128)(2,1)} custom-call(s32[5]{0:T(128)S(1)} %stack.81.place, bf16[512,768]{1,0:T(8,128)(2,1)S(1)} %get-tuple-element.503.refs_0_, bf16[512,3072]{1,0:T(8,128)(2,1)S(1)} %copy-done.3, bf16[512,768]{1,0:T(8,128)(2,1)S(1)} %copy-done.10, bf16[512,768]{1,0:T(8,128)(2,1)S(1)} %copy-done.17, ...), custom_call_target="tpu_custom_call" | custom-call | bytes 11070000 | tf_op jit(solution)/shard_map/chunk_given/pallas_call | solution.py:1082
  243.2 5.1 vector_back.1
  248.3 5.2 %collective-permute-done.14.refs_6_ = bf16[2,8,384,384]{3,2,1,0:T(8,128)(2,1)S(1)} collective-permute-done((bf16[2,8,384,384]{3,2,1,0:T(8,128)(2,1)}, bf16[2,8,384,384]{3,2,1,0:T(8,128)(2,1)S(1)}, u32[]{:S(2)}, u32[]{:S(2)}) %collective-permute-start.14) | collective-permute-done | bytes 4718624 | tf_op jit(solution)/shard_map/ppermute | solution.py:931
  255.7 10.9 %chunk_kept.4 = (bf16[8,384,384]{2,1,0:T(8,128)(2,1)}, bf16[8,384,384]{2,1,0:T(8,128)(2,1)}) custom-call(s32[5]{0:T(128)S(1)} %stack.81.place, bf16[512,768]{1,0:T(8,128)(2,1)S(1)} %get-tuple-element.503.refs_0_, bf16[512,3072]{1,0:T(8,128)(2,1)} %get-tuple-element.269.d_projections.refs_1_.d_queries, bf16[512,768]{1,0:T(8,128)(2,1)S(1)} %copy-done.10, ...), custom_call_target="tpu_custom_call" | custom-call | bytes 22140000 | tf_op jit(solution)/shard_map/chunk_kept/pallas_call | solution.py:1102
  269.2 5.3 %exchange.19 = (bf16[2,288,384]{2,1,0:T(8,128)(2,1)S(1)}, bf16[2,288,384]{2,1,0:T(8,128)(2,1)S(1)}, bf16[2,4,16,16,512]{4,3,2,1,0:T(8,128)(2,1)S(1)}, bf16[2,4,16,16,512]{4,3,2,1,0:T(8,128)(2,1)}) custom-call(bf16[2,2,288,384]{3,2,1,0:T(8,128)(2,1)S(1)} %bitcast.137, bf16[2,2,288,384]{3,2,1,0:T(8,128)(2,1)S(1)} %bitcast.138, ...), custom_call_target="tpu_custom_call" | custom-call | bytes 1845000 | tf_op jit(solution)/shard_map/exchange/pallas_call | solution.py:1241
  280.0 23.6 %atom_tokens_back.1 = (bf16[2048,128]{1,0:T(8,128)(2,1)}, bf16[2048,128]{1,0:T(8,128)(2,1)}, f32[2048,128]{1,0:T(8,128)}, bf16[2048,512]{1,0:T(8,128)(2,1)}, bf16[128,1664]{1,0:T(8,128)(2,1)}) custom-call(s32[8]{0:T(128)} %slice.85.firsts, bf16[2048,128]{1,0:T(8,128)(2,1)} %copy-done.4, bf16[2048,128]{1,0:T(8,128)(2,1)} %single.9, ...), custom_call_target="tpu_custom_call" | custom-call | bytes 11070000 | tf_op jit(solution)/shard_map/atom_tokens_back/pallas_call | solution.py:559
  304.1 11.1 %atom_attention_back.1 = (bf16[2048,384]{1,0:T(8,128)(2,1)}, bf16[2,4,4,128,128]{4,3,2,1,0:T(8,128)(2,1)}, bf16[2,4,4,128,128]{4,3,2,1,0:T(8,128)(2,1)}) custom-call(s32[64]{0:T(128)} %starts.5, s32[4]{0:T(128)} %pad_add_fusion.place, bf16[2048,512]{1,0:T(8,128)(2,1)} %copy-done.2, f32[2048,128]{1,0:T(8,128)} %get-tuple-element.288.attended, ...), custom_call_target="tpu_custom_call" | custom-call | bytes 7380000 | tf_op jit(solution)/shard_map/atom_attention_back/pallas_call | solution.py:607
  324.8 5.3 %exchange.21 = (bf16[4,384,384]{2,1,0:T(8,128)(2,1)S(1)}, bf16[4,384,384]{2,1,0:T(8,128)(2,1)}, bf16[1,288,384]{2,1,0:T(8,128)(2,1)S(1)}, bf16[4,16,16,512]{3,2,1,0:T(8,128)(2,1)S(1)}, bf16[4,16,16,512]{3,2,1,0:T(8,128)(2,1)}) custom-call(bf16[2,4,384,384]{3,2,1,0:T(8,128)(2,1)} %bitcast.166, bf16[2,4,384,384]{3,2,1,0:T(8,128)(2,1)} %bitcast.33.refs_1_, ...), custom_call_target="tpu_custom_call" | custom-call | bytes 1845000 | tf_op jit(solution)/shard_map/exchange/pallas_call | solution.py:1241
  333.3 7.3 %atom_features_back.1 = (f32[2048,128]{1,0:T(8,128)S(1)}, bf16[128,1280]{1,0:T(8,128)(2,1)S(1)}, f32[1,128]{1,0:T(1,128)S(1)}, f32[1,768]{1,0:T(1,128)S(1)}, f32[1,128]{1,0:T(1,128)S(1)}) custom-call(bf16[2048,128]{1,0:T(8,128)(2,1)S(1)} %copy-done.5, bf16[2048,128]{1,0:T(8,128)(2,1)S(1)} %copy-done.9, bf16[2048,384]{1,0:T(8,128)(2,1)S(1)} %copy-done.23, ...), custom_call_target="tpu_custom_call" | custom-call | bytes 1845000 | tf_op jit(solution)/shard_map/atom_features_back/pallas_call | solution.py:643
  350.9 7.0 %collective-permute-done.27 = bf16[4,16,16,512]{3,2,1,0:T(8,128)(2,1)} collective-permute-done((bf16[4,16,16,512]{3,2,1,0:T(8,128)(2,1)}, bf16[4,16,16,512]{3,2,1,0:T(8,128)(2,1)}, u32[]{:S(2)}, u32[]{:S(2)}) %collective-permute-start.27) | collective-permute-done | bytes 1048608 | tf_op jit(solution)/shard_map/ppermute | solution.py:927
  369.9 7.0 %collective-permute-done.29 = bf16[256,768]{1,0:T(8,128)(2,1)S(1)} collective-permute-done((bf16[256,768]{1,0:T(8,128)(2,1)S(1)}, bf16[256,768]{1,0:T(8,128)(2,1)S(1)}, u32[]{:S(2)}, u32[]{:S(2)}) %collective-permute-start.29) | collective-permute-done | bytes 393248 | tf_op jit(solution)/shard_map/ppermute | solution.py:927
  378.8 12.2 %collective-permute-done.28 = bf16[4,32,384]{2,1,0:T(8,128)(2,1)S(1)} collective-permute-done((bf16[4,32,384]{2,1,0:T(8,128)(2,1)S(1)}, bf16[4,32,384]{2,1,0:T(8,128)(2,1)S(1)}, u32[]{:S(2)}, u32[]{:S(2)}) %collective-permute-start.28) | collective-permute-done | bytes 98336 | tf_op jit(solution)/shard_map/ppermute | solution.py:931
  398.9 5.3 %collective-permute-done.32 = bf16[2,32,384]{2,1,0:T(8,128)(2,1)S(1)} collective-permute-done((bf16[2,32,384]{2,1,0:T(8,128)(2,1)S(1)}, bf16[2,32,384]{2,1,0:T(8,128)(2,1)S(1)}, u32[]{:S(2)}, u32[]{:S(2)}) %collective-permute-start.32) | collective-permute-done | bytes 49184 | tf_op jit(solution)/shard_map/ppermute | solution.py:1257
  404.2 13.9 %collective-permute-done.35.refs_5_ = bf16[1,16,16,512]{3,2,1,0:T(8,128)(2,1)S(1)} collective-permute-done((bf16[1,16,16,512]{3,2,1,0:T(8,128)(2,1)S(1)}, bf16[1,16,16,512]{3,2,1,0:T(8,128)(2,1)S(1)}, u32[]{:S(2)}, u32[]{:S(2)}) %collective-permute-start.35) | collective-permute-done | bytes 262176 | tf_op jit(solution)/shard_map/ppermute | solution.py:1257
  424.4 9.3 %collective-permute-done.36.refs_1_ = bf16[1,384,384]{2,1,0:T(8,128)(2,1)S(1)} collective-permute-done((bf16[1,384,384]{2,1,0:T(8,128)(2,1)S(1)}, bf16[1,384,384]{2,1,0:T(8,128)(2,1)S(1)}, u32[]{:S(2)}, u32[]{:S(2)}) %collective-permute-start.36) | collective-permute-done | bytes 294944 | tf_op jit(solution)/shard_map/ppermute | solution.py:1257
  438.0 17.1 %collective-permute-done.41.refs_3_ = bf16[1,32,384]{2,1,0:T(8,128)(2,1)S(1)} collective-permute-done((bf16[1,32,384]{2,1,0:T(8,128)(2,1)S(1)}, bf16[1,32,384]{2,1,0:T(8,128)(2,1)S(1)}, u32[]{:S(2)}, u32[]{:S(2)}) %collective-permute-start.41) | collective-permute-done | bytes 24608 | tf_op jit(solution)/shard_map/ppermute | solution.py:1257
  506.9 7.0 %assemble.5 = (f32[384,3072]{1,0:T(8,128)}, f32[384,768]{1,0:T(8,128)}, f32[192,4608]{1,0:T(8,128)}) custom-call(s32[5]{0:T(128)S(1)} %stack.81.place, bf16[4,384,384]{2,1,0:T(8,128)(2,1)} %get-tuple-element.389.refs_0_, bf16[4,384,384]{2,1,0:T(8,128)(2,1)} %collective-permute-done.47.refs_1_, bf16[4,384,384]{2,1,0:T(8,128)(2,1)} %collective-permute-done.52.refs_2_, ...), custom_call_target="tpu_custom_call" | custom-call | bytes 7380000 | tf_op jit(solution)/shard_map/assemble/pallas_call | solution.py:1145
  (421 shorter events, 208.0 us)
Async XLA Ops:
  8.3 21.7 %collective-permute-start = (bf16[4,4,32,128]{3,2,1,0:T(8,128)(2,1)S(1)}, bf16[4,4,32,128]{3,2,1,0:T(8,128)(2,1)S(1)}, u32[]{:S(2)}, u32[]{:S(2)}) collective-permute-start(bf16[4,4,32,128]{3,2,1,0:T(8,128)(2,1)S(1)} %multiply_reduce_fusion.2), channel_id=1, source_target_pairs={{0,8},{1,9},{2,10},{3,11},{4,12},{5,13},{6,14},{7,15},{8,0},{9,1},... | collective-permute-start | bytes 393224 | tf_op jit(solution)/shard_map/ppermute | solution.py:1257
  31.7 14.3 %collective-permute-start.2 = (bf16[16,16,512]{2,1,0:T(8,128)(2,1)}, bf16[16,16,512]{2,1,0:T(8,128)(2,1)S(1)}, u32[]{:S(2)}, u32[]{:S(2)}) collective-permute-start(bf16[16,16,512]{2,1,0:T(8,128)(2,1)} %bitcast.80), channel_id=1, source_target_pairs={{0,8},{1,9},{2,10},{3,11},{4,12},{5,13},{6,14},{7,15},{8,0},{9,1},... | collective-permute-start | bytes 786440 | tf_op jit(solution)/shard_map/ppermute | solution.py:1257
  62.2 17.3 %collective-permute-start.6 = (bf16[4,8,16,512]{3,2,1,0:T(8,128)(2,1)S(1)}, bf16[4,8,16,512]{3,2,1,0:T(8,128)(2,1)S(1)}, u32[]{:S(2)}, u32[]{:S(2)}) collective-permute-start(bf16[4,8,16,512]{3,2,1,0:T(8,128)(2,1)S(1)} %get-tuple-element.238.refs_0_), channel_id=1, source_target_pairs={{0,2},{1,3},{2,0},{3,1},{4,6},{5,7},{6,4},{7,5},{8,10},{9,11},{10,... | collective-permute-start | bytes 1572872 | tf_op jit(solution)/shard_map/ppermute | solution.py:931
  63.8 15.7 %collective-permute-start.7 = (bf16[4,8,16,512]{3,2,1,0:T(8,128)(2,1)S(1)}, bf16[4,8,16,512]{3,2,1,0:T(8,128)(2,1)}, u32[]{:S(2)}, u32[]{:S(2)}) collective-permute-start(bf16[4,8,16,512]{3,2,1,0:T(8,128)(2,1)S(1)} %get-tuple-element.239.refs_2_), channel_id=1, source_target_pairs={{0,16},{16,0},{1,17},{17,1},{2,18},{18,2},{3,19},{19,3},{4,20},{20... | collective-permute-start | bytes 1572872 | tf_op jit(solution)/shard_map/ppermute | solution.py:927
  80.9 24.7 %collective-permute-start.8 = (bf16[8,8,16,512]{3,2,1,0:T(8,128)(2,1)S(1)}, bf16[8,8,16,512]{3,2,1,0:T(8,128)(2,1)S(1)}, u32[]{:S(2)}, u32[]{:S(2)}) collective-permute-start(bf16[8,8,16,512]{3,2,1,0:T(8,128)(2,1)S(1)} %get-tuple-element.250.refs_0_), channel_id=1, source_target_pairs={{0,16},{16,0},{1,17},{17,1},{2,18},{18,2},{3,19},{19,3},{4,20},{20... | collective-permute-start | bytes 3145736 | tf_op jit(solution)/shard_map/ppermute | solution.py:927
  81.4 24.4 %collective-permute-start.9 = (bf16[8,8,16,512]{3,2,1,0:T(8,128)(2,1)S(1)}, bf16[8,8,16,512]{3,2,1,0:T(8,128)(2,1)S(1)}, u32[]{:S(2)}, u32[]{:S(2)}) collective-permute-start(bf16[8,8,16,512]{3,2,1,0:T(8,128)(2,1)S(1)} %get-tuple-element.251.refs_2_), channel_id=1, source_target_pairs={{0,2},{1,3},{2,0},{3,1},{4,6},{5,7},{6,4},{7,5},{8,10},{9,11},{10,... | collective-permute-start | bytes 3145736 | tf_op jit(solution)/shard_map/ppermute | solution.py:931
  183.8 43.5 %collective-permute-start.13 = (bf16[8,288,384]{2,1,0:T(8,128)(2,1)}, bf16[8,288,384]{2,1,0:T(8,128)(2,1)}, u32[]{:S(2)}, u32[]{:S(2)}) collective-permute-start(bf16[8,288,384]{2,1,0:T(8,128)(2,1)} %get-tuple-element.276), channel_id=1, source_target_pairs={{0,16},{16,0},{1,17},{17,1},{2,18},{18,2},{3,19},{19,3},{4,20},{20... | collective-permute-start | bytes 5308424 | tf_op jit(solution)/shard_map/ppermute | solution.py:927
  239.4 14.1 %collective-permute-start.14 = (bf16[2,8,384,384]{3,2,1,0:T(8,128)(2,1)}, bf16[2,8,384,384]{3,2,1,0:T(8,128)(2,1)S(1)}, u32[]{:S(2)}, u32[]{:S(2)}) collective-permute-start(bf16[2,8,384,384]{3,2,1,0:T(8,128)(2,1)} %chunk_given.4), channel_id=1, source_target_pairs={{0,1},{1,0},{2,3},{3,2},{4,5},{5,4},{6,7},{7,6},{8,9},{9,8},{10,11... | collective-permute-start | bytes 14155784 | tf_op jit(solution)/shard_map/ppermute | solution.py:931
  239.4 28.7 %collective-permute-start.16 = (bf16[2,2,4,16,16,512]{5,4,3,2,1,0:T(8,128)(2,1)}, bf16[2,2,4,16,16,512]{5,4,3,2,1,0:T(8,128)(2,1)}, u32[]{:S(2)}, u32[]{:S(2)}) collective-permute-start(bf16[2,2,4,16,16,512]{5,4,3,2,1,0:T(8,128)(2,1)} %get-tuple-element.297), channel_id=1, source_target_pairs={{0,1},{1,0},{2,3},{3,2},{4,5},{5,4},{6,7},{7,6},{8,9},{9,8},{10,11... | collective-permute-start | bytes 12582920 | tf_op jit(solution)/shard_map/ppermute | solution.py:931
  239.9 26.7 %collective-permute-start.15 = (bf16[4,288,384]{2,1,0:T(8,128)(2,1)}, bf16[4,288,384]{2,1,0:T(8,128)(2,1)S(1)}, u32[]{:S(2)}, u32[]{:S(2)}) collective-permute-start(bf16[4,288,384]{2,1,0:T(8,128)(2,1)} %get-tuple-element.292), channel_id=1, source_target_pairs={{0,2},{1,3},{2,0},{3,1},{4,6},{5,7},{6,4},{7,5},{8,10},{9,11},{10,... | collective-permute-start | bytes 2654216 | tf_op jit(solution)/shard_map/ppermute | solution.py:931
  267.5 53.6 %collective-permute-start.18 = (bf16[8,384,384]{2,1,0:T(8,128)(2,1)}, bf16[8,384,384]{2,1,0:T(8,128)(2,1)}, u32[]{:S(2)}, u32[]{:S(2)}) collective-permute-start(bf16[8,384,384]{2,1,0:T(8,128)(2,1)} %get-tuple-element.311), channel_id=1, source_target_pairs={{0,16},{16,0},{1,17},{17,1},{2,18},{18,2},{3,19},{19,3},{4,20},{20... | collective-permute-start | bytes 7077896 | tf_op jit(solution)/shard_map/ppermute | solution.py:927
  275.8 47.6 %collective-permute-start.20 = (bf16[2,4,16,16,512]{4,3,2,1,0:T(8,128)(2,1)}, bf16[2,4,16,16,512]{4,3,2,1,0:T(8,128)(2,1)S(1)}, u32[]{:S(2)}, u32[]{:S(2)}) collective-permute-start(bf16[2,4,16,16,512]{4,3,2,1,0:T(8,128)(2,1)} %get-tuple-element.317), channel_id=1, source_target_pairs={{0,2},{1,3},{2,0},{3,1},{4,6},{5,7},{6,4},{7,5},{8,10},{9,11},{10,... | collective-permute-start | bytes 6291464 | tf_op jit(solution)/shard_map/ppermute | solution.py:931
  277.0 26.6 %collective-permute-start.17 = (bf16[2,288,384]{2,1,0:T(8,128)(2,1)S(1)}, bf16[2,288,384]{2,1,0:T(8,128)(2,1)S(1)}, u32[]{:S(2)}, u32[]{:S(2)}) collective-permute-start(bf16[2,288,384]{2,1,0:T(8,128)(2,1)S(1)} %get-tuple-element.304), channel_id=1, source_target_pairs={{0,4},{1,5},{2,6},{3,7},{4,0},{5,1},{6,2},{7,3},{8,12},{9,13},{10,... | collective-permute-start | bytes 1327112 | tf_op jit(solution)/shard_map/ppermute | solution.py:1257
  330.2 15.7 %collective-permute-start.23 = (bf16[2,4,4,128,128]{4,3,2,1,0:T(8,128)(2,1)S(1)}, bf16[2,4,4,128,128]{4,3,2,1,0:T(8,128)(2,1)S(1)}, u32[]{:S(2)}, u32[]{:S(2)}) collective-permute-start(bf16[2,4,4,128,128]{4,3,2,1,0:T(8,128)(2,1)S(1)} %copy-done.86), channel_id=1, source_target_pairs={{0,1},{1,0},{2,3},{3,2},{4,5},{5,4},{6,7},{7,6},{8,9},{9,8},{10,11... | collective-permute-start | bytes 3145736 | tf_op jit(solution)/shard_map/ppermute | solution.py:931
  330.2 28.7 %collective-permute-start.21 = (bf16[4,384,384]{2,1,0:T(8,128)(2,1)}, bf16[4,384,384]{2,1,0:T(8,128)(2,1)}, u32[]{:S(2)}, u32[]{:S(2)}) collective-permute-start(bf16[4,384,384]{2,1,0:T(8,128)(2,1)} %get-tuple-element.325), channel_id=1, source_target_pairs={{0,2},{1,3},{2,0},{3,1},{4,6},{5,7},{6,4},{7,5},{8,10},{9,11},{10,... | collective-permute-start | bytes 3538952 | tf_op jit(solution)/shard_map/ppermute | solution.py:931
  331.5 26.3 %collective-permute-start.27 = (bf16[4,16,16,512]{3,2,1,0:T(8,128)(2,1)}, bf16[4,16,16,512]{3,2,1,0:T(8,128)(2,1)}, u32[]{:S(2)}, u32[]{:S(2)}) collective-permute-start(bf16[4,16,16,512]{3,2,1,0:T(8,128)(2,1)} %get-tuple-element.345), channel_id=1, source_target_pairs={{0,16},{16,0},{1,17},{17,1},{2,18},{18,2},{3,19},{19,3},{4,20},{20... | collective-permute-start | bytes 3145736 | tf_op jit(solution)/shard_map/ppermute | solution.py:927
  333.0 12.9 %collective-permute-start.22 = (bf16[1,288,384]{2,1,0:T(8,128)(2,1)S(1)}, bf16[1,288,384]{2,1,0:T(8,128)(2,1)S(1)}, u32[]{:S(2)}, u32[]{:S(2)}) collective-permute-start(bf16[1,288,384]{2,1,0:T(8,128)(2,1)S(1)} %get-tuple-element.332.refs_0_), channel_id=1, source_target_pairs={{0,8},{1,9},{2,10},{3,11},{4,12},{5,13},{6,14},{7,15},{8,0},{9,1},... | collective-permute-start | bytes 663560 | tf_op jit(solution)/shard_map/ppermute | solution.py:1257
  366.4 25.5 %collective-permute-start.30 = (bf16[2,384,384]{2,1,0:T(8,128)(2,1)S(1)}, bf16[2,384,384]{2,1,0:T(8,128)(2,1)S(1)}, u32[]{:S(2)}, u32[]{:S(2)}) collective-permute-start(bf16[2,384,384]{2,1,0:T(8,128)(2,1)S(1)} %get-tuple-element.352), channel_id=1, source_target_pairs={{0,4},{1,5},{2,6},{3,7},{4,0},{5,1},{6,2},{7,3},{8,12},{9,13},{10,... | collective-permute-start | bytes 1769480 | tf_op jit(solution)/shard_map/ppermute | solution.py:1257
  368.0 23.9 %collective-permute-start.31 = (bf16[2,16,16,512]{3,2,1,0:T(8,128)(2,1)S(1)}, bf16[2,16,16,512]{3,2,1,0:T(8,128)(2,1)S(1)}, u32[]{:S(2)}, u32[]{:S(2)}) collective-permute-start(bf16[2,16,16,512]{3,2,1,0:T(8,128)(2,1)S(1)} %get-tuple-element.356), channel_id=1, source_target_pairs={{0,4},{1,5},{2,6},{3,7},{4,0},{5,1},{6,2},{7,3},{8,12},{9,13},{10,... | collective-permute-start | bytes 1572872 | tf_op jit(solution)/shard_map/ppermute | solution.py:1257
  368.5 27.0 %collective-permute-start.33 = (bf16[1024,128]{1,0:T(8,128)(2,1)S(1)}, bf16[1024,128]{1,0:T(8,128)(2,1)S(1)}, u32[]{:S(2)}, u32[]{:S(2)}) collective-permute-start(bf16[1024,128]{1,0:T(8,128)(2,1)S(1)} %dynamic-slice_bitcast_fusion.3), channel_id=1, source_target_pairs={{0,16},{16,0},{1,17},{17,1},{2,18},{18,2},{3,19},{19,3},{4,20},{20... | collective-permute-start | bytes 786440 | tf_op jit(solution)/shard_map/ppermute | solution.py:927
  369.1 64.6 %collective-permute-start.38 = (bf16[4,288,384]{2,1,0:T(8,128)(2,1)S(1)}, bf16[4,288,384]{2,1,0:T(8,128)(2,1)S(1)}, u32[]{:S(2)}, u32[]{:S(2)}) collective-permute-start(bf16[4,288,384]{2,1,0:T(8,128)(2,1)S(1)} %get-tuple-element.371.refs_4_), channel_id=1, source_target_pairs={{0,2},{1,3},{2,0},{3,1},{4,6},{5,7},{6,4},{7,5},{8,10},{9,11},{10,... | collective-permute-start | bytes 2654216 | tf_op jit(solution)/shard_map/ppermute | solution.py:931
  377.0 14.0 %collective-permute-start.28 = (bf16[4,32,384]{2,1,0:T(8,128)(2,1)S(1)}, bf16[4,32,384]{2,1,0:T(8,128)(2,1)S(1)}, u32[]{:S(2)}, u32[]{:S(2)}) collective-permute-start(bf16[4,32,384]{2,1,0:T(8,128)(2,1)S(1)} %get-tuple-element.346), channel_id=1, source_target_pairs={{0,2},{1,3},{2,0},{3,1},{4,6},{5,7},{6,4},{7,5},{8,10},{9,11},{10,... | collective-permute-start | bytes 294920 | tf_op jit(solution)/shard_map/ppermute | solution.py:931
  392.5 25.6 %collective-permute-start.34 = (bf16[1,384,384]{2,1,0:T(8,128)(2,1)S(1)}, bf16[1,384,384]{2,1,0:T(8,128)(2,1)S(1)}, u32[]{:S(2)}, u32[]{:S(2)}) collective-permute-start(bf16[1,384,384]{2,1,0:T(8,128)(2,1)S(1)} %get-tuple-element.361), channel_id=1, source_target_pairs={{0,8},{1,9},{2,10},{3,11},{4,12},{5,13},{6,14},{7,15},{8,0},{9,1},... | collective-permute-start | bytes 884744 | tf_op jit(solution)/shard_map/ppermute | solution.py:1257
  392.8 25.3 %collective-permute-start.35 = (bf16[1,16,16,512]{3,2,1,0:T(8,128)(2,1)S(1)}, bf16[1,16,16,512]{3,2,1,0:T(8,128)(2,1)S(1)}, u32[]{:S(2)}, u32[]{:S(2)}) collective-permute-start(bf16[1,16,16,512]{3,2,1,0:T(8,128)(2,1)S(1)} %get-tuple-element.365), channel_id=1, source_target_pairs={{0,8},{1,9},{2,10},{3,11},{4,12},{5,13},{6,14},{7,15},{8,0},{9,1},... | collective-permute-start | bytes 786440 | tf_op jit(solution)/shard_map/ppermute | solution.py:1257
  398.1 36.0 %collective-permute-start.39 = (bf16[4,4,128,128]{3,2,1,0:T(8,128)(2,1)S(1)}, bf16[4,4,128,128]{3,2,1,0:T(8,128)(2,1)S(1)}, u32[]{:S(2)}, u32[]{:S(2)}) collective-permute-start(bf16[4,4,128,128]{3,2,1,0:T(8,128)(2,1)S(1)} %copy-done.51), channel_id=1, source_target_pairs={{0,2},{1,3},{2,0},{3,1},{4,6},{5,7},{6,4},{7,5},{8,10},{9,11},{10,... | collective-permute-start | bytes 1572872 | tf_op jit(solution)/shard_map/ppermute | solution.py:931
  418.3 15.4 %collective-permute-start.36 = (bf16[1,384,384]{2,1,0:T(8,128)(2,1)S(1)}, bf16[1,384,384]{2,1,0:T(8,128)(2,1)S(1)}, u32[]{:S(2)}, u32[]{:S(2)}) collective-permute-start(bf16[1,384,384]{2,1,0:T(8,128)(2,1)S(1)} %get-tuple-element.366.refs_0_), channel_id=1, source_target_pairs={{0,8},{1,9},{2,10},{3,11},{4,12},{5,13},{6,14},{7,15},{8,0},{9,1},... | collective-permute-start | bytes 884744 | tf_op jit(solution)/shard_map/ppermute | solution.py:1257
  421.1 13.1 %collective-permute-start.37 = (bf16[1,32,384]{2,1,0:T(8,128)(2,1)S(1)}, bf16[1,32,384]{2,1,0:T(8,128)(2,1)S(1)}, u32[]{:S(2)}, u32[]{:S(2)}) collective-permute-start(bf16[1,32,384]{2,1,0:T(8,128)(2,1)S(1)} %get-tuple-element.370), channel_id=1, source_target_pairs={{0,8},{1,9},{2,10},{3,11},{4,12},{5,13},{6,14},{7,15},{8,0},{9,1},... | collective-permute-start | bytes 73736 | tf_op jit(solution)/shard_map/ppermute | solution.py:1257
  435.9 21.4 %collective-permute-start.40 = (bf16[2,384,384]{2,1,0:T(8,128)(2,1)S(1)}, bf16[2,384,384]{2,1,0:T(8,128)(2,1)S(1)}, u32[]{:S(2)}, u32[]{:S(2)}) collective-permute-start(bf16[2,384,384]{2,1,0:T(8,128)(2,1)S(1)} %get-tuple-element.375.refs_0_), channel_id=1, source_target_pairs={{0,4},{1,5},{2,6},{3,7},{4,0},{5,1},{6,2},{7,3},{8,12},{9,13},{10,... | collective-permute-start | bytes 1769480 | tf_op jit(solution)/shard_map/ppermute | solution.py:1257
  435.9 21.4 %collective-permute-start.42 = (bf16[2,4,128,128]{3,2,1,0:T(8,128)(2,1)S(1)}, bf16[2,4,128,128]{3,2,1,0:T(8,128)(2,1)S(1)}, u32[]{:S(2)}, u32[]{:S(2)}) collective-permute-start(bf16[2,4,128,128]{3,2,1,0:T(8,128)(2,1)S(1)} %get-tuple-element.378), channel_id=1, source_target_pairs={{0,4},{1,5},{2,6},{3,7},{4,0},{5,1},{6,2},{7,3},{8,12},{9,13},{10,... | collective-permute-start | bytes 786440 | tf_op jit(solution)/shard_map/ppermute | solution.py:1257
  437.9 17.2 %collective-permute-start.41 = (bf16[1,32,384]{2,1,0:T(8,128)(2,1)S(1)}, bf16[1,32,384]{2,1,0:T(8,128)(2,1)S(1)}, u32[]{:S(2)}, u32[]{:S(2)}) collective-permute-start(bf16[1,32,384]{2,1,0:T(8,128)(2,1)S(1)} %get-tuple-element.376.refs_2_), channel_id=1, source_target_pairs={{0,8},{1,9},{2,10},{3,11},{4,12},{5,13},{6,14},{7,15},{8,0},{9,1},... | collective-permute-start | bytes 73736 | tf_op jit(solution)/shard_map/ppermute | solution.py:1257
  458.6 33.9 %collective-permute-start.47 = (bf16[4,384,384]{2,1,0:T(8,128)(2,1)}, bf16[4,384,384]{2,1,0:T(8,128)(2,1)}, u32[]{:S(2)}, u32[]{:S(2)}) collective-permute-start(bf16[4,384,384]{2,1,0:T(8,128)(2,1)} %get-tuple-element.389.refs_0_), channel_id=1, source_target_pairs={{0,2},{1,3},{2,0},{3,1},{4,6},{5,7},{6,4},{7,5},{8,10},{9,11},{10,... | collective-permute-start | bytes 3538952 | tf_op jit(solution)/shard_map/ppermute | solution.py:931
  459.4 33.1 %collective-permute-start.52 = (bf16[4,384,384]{2,1,0:T(8,128)(2,1)}, bf16[4,384,384]{2,1,0:T(8,128)(2,1)}, u32[]{:S(2)}, u32[]{:S(2)}) collective-permute-start(bf16[4,384,384]{2,1,0:T(8,128)(2,1)} %get-tuple-element.389.refs_0_), channel_id=1, source_target_pairs={{0,1},{1,0},{2,3},{3,2},{4,5},{5,4},{6,7},{7,6},{8,9},{9,8},{10,11... | collective-permute-start | bytes 3538952 | tf_op jit(solution)/shard_map/ppermute | solution.py:931
  (119 other events, 1029.3 us)
